TPU v7x, 512 devices: a whole 4x8x8 slice. The times are simulated.
512 devices in a mesh: tm: 64 (over y, z), head: 4 (over x), farm: 2 (over core).
Axes of the slice: x: 4, y: 8, z: 8, core: 2. Of those that a mesh axis runs over, the one named last changes fastest.
Arguments:
- head_inputs: bfloat16 [2, 32768, 3072], P('farm', 'tm', 'head'), may hold values from -6 to 6
- b_proj: bfloat16 [2, 32768, 128], P('farm', 'tm'), may hold values from -0.625 to 0.625
- c_proj: bfloat16 [2, 32768, 128], P('farm', 'tm'), may hold values from -0.5 to 0.5
- log_decay: float32 [2, 32768, 48], P('farm', 'tm', 'head'), may hold values from -2 to 0
- skip_gain: float32 [48], P('head'), may hold values from 0.5 to 2
- w_out: bfloat16 [3072, 1536], P('head'), may hold values from -0.109375 to 0.109375
- norm_gain: float32 [1536], replicated, may hold values from 0.1 to 1.9
- owner_ids: int32 [2, 32768, 1], P('farm', ('tm', 'head')), may hold values from 0 to 127; in each aligned block of 128 rows (0 to 127, 128 to 255, ..., all dimensions but the last counted through in order) at most 2 rows name the same one
Outputs:
- regrouped: bfloat16 [128, 4, 128, 2, 1536], P(('tm', 'farm'), 'head')
Inputs may be any that keep to these rules, and one draw needn't show every extreme that they name: `owner_ids`: in each aligned block of 128 rows no owner is named by more than 2 rows, and some block names an owner exactly 2 times.
All inputs are finite; a program needn't handle non-finite values.
Results may differ from a plain program's by a relative error of at most 0.02.
Values may be sent and summed in bfloat16 or wider, within the bound.
No kernel may reach another device: no remote copies, remote signals or barrier semaphores. Data moves between devices by JAX's collectives and lax.ppermute only.
A program may use at most 128 MiB of HBM per device.

v0:
```python
import jax
import jax.numpy as jnp
from jax import lax
from jax.sharding import PartitionSpec as P

SPAN = 256


def prefix(value, axis, combine, identity):
    length, index = (lax.axis_size(axis), lax.axis_index(axis))
    everything = jax.tree.map(
        lambda part, kind: lax.all_gather(part.astype(kind), axis),
        value,
        (jnp.bfloat16, jnp.bfloat16),
    )
    start = jax.tree.map(
        lambda part, zero: jnp.broadcast_to(jnp.asarray(zero, part.dtype), part.shape),
        value,
        identity,
    )

    def lap(k, before):
        reached = k < index
        new = combine(
            before, jax.tree.map(lambda part, own: part[k].astype(own.dtype), everything, value)
        )
        return jax.tree.map(lambda a, b: jnp.where(reached, a, b), new, before)

    return lax.fori_loop(0, length, lap, start)


def span_step(carried, pieces):
    inputs_block, b_block, c_block, decay_block = pieces
    block_length = decay_block.shape[0]
    running_sum = jnp.cumsum(decay_block, axis=0)
    by_head = running_sum.T
    log_gaps = by_head[:, :, None] - by_head[:, None, :]
    causal = (jnp.arange(block_length)[:, None] >= jnp.arange(block_length)[None, :])[None]
    weights = jnp.where(causal, jnp.exp(jnp.where(causal, log_gaps, 0.0)), 0.0)
    scores = jnp.dot(c_block, b_block.T, precision=lax.Precision.HIGHEST)
    mixing = weights * scores[None]
    within = jnp.einsum("hts,shp->thp", mixing, inputs_block, precision=lax.Precision.HIGHEST)
    within = within + jnp.exp(running_sum)[:, :, None] * jnp.einsum(
        "tn,hpn->thp", c_block, carried, precision=lax.Precision.HIGHEST
    )
    to_end = jnp.exp(running_sum[-1][None, :] - running_sum)
    updated = jnp.exp(running_sum[-1])[:, None, None] * carried + jnp.einsum(
        "shp,sn->hpn", to_end[:, :, None] * inputs_block, b_block, precision=lax.Precision.HIGHEST
    )
    return (updated, within)


def combine(earlier, later_part):
    return (
        earlier[0] + later_part[0],
        jnp.exp(later_part[0])[:, None, None] * earlier[1] + later_part[1],
    )


def slot_targets(routes, owners, capacity):
    matches = (routes[..., None] == jnp.arange(owners, dtype=jnp.int32)).astype(jnp.int32)
    earlier = jnp.cumsum(matches, axis=-2) - matches
    slot_index = jnp.sum(earlier * matches, axis=-1)
    return routes * capacity + slot_index


def row_norm(projected, norm_gain):
    scale_rows = lax.rsqrt(jnp.mean(projected * projected, axis=-1, keepdims=True) + 1e-06)
    return (projected * scale_rows * norm_gain).astype(jnp.bfloat16)


def shards(head_inputs, b_proj, c_proj, log_decay, skip_gain, w_out, norm_gain, owner_ids):
    steps_dev = head_inputs.shape[1]
    head_count = log_decay.shape[2]
    head_width = head_inputs.shape[2] // head_count
    state_dim = b_proj.shape[2]
    blocks = steps_dev // SPAN
    features = head_inputs[0].astype(jnp.float32).reshape(steps_dev, head_count, head_width)
    b_rows = b_proj[0].astype(jnp.float32)
    c_rows = c_proj[0].astype(jnp.float32)
    decays = log_decay[0]
    pieces = (
        features.reshape(blocks, SPAN, head_count, head_width),
        b_rows.reshape(blocks, SPAN, state_dim),
        c_rows.reshape(blocks, SPAN, state_dim),
        decays.reshape(blocks, SPAN, head_count),
    )
    start_state = jnp.zeros((head_count, head_width, state_dim), jnp.float32)
    local_state, local_out = lax.scan(span_step, start_state, pieces)
    local_out = local_out.reshape(steps_dev, head_count, head_width)
    total_decay = jnp.sum(decays, axis=0)
    carried_prior = prefix(
        (total_decay, local_state),
        "tm",
        combine,
        (jnp.zeros_like(total_decay), jnp.zeros_like(local_state)),
    )
    running_sum = jnp.cumsum(decays, axis=0)
    carried_in = jnp.exp(running_sum)[:, :, None] * jnp.einsum(
        "tn,hpn->thp", c_rows, carried_prior[1], precision=lax.Precision.HIGHEST
    )
    ssd_out = local_out + carried_in + skip_gain[None, :, None] * features
    mixed_out = ssd_out.reshape(steps_dev, head_count * head_width).astype(jnp.bfloat16)
    piece_count = lax.axis_size("head")
    row_count = steps_dev // piece_count
    tm_count = lax.axis_size("tm")
    farm_count = lax.axis_size("farm")
    owners = tm_count * farm_count
    capacity = max(2, 2 * row_count // owners)
    width_out = w_out.shape[1]
    slot_range = jnp.arange(owners * capacity, dtype=jnp.int32)
    projected = lax.psum_scatter(
        jnp.dot(mixed_out, w_out, preferred_element_type=jnp.float32).astype(jnp.bfloat16),
        "head",
        scatter_dimension=0,
        tiled=True,
    ).astype(jnp.float32)
    normed = row_norm(projected, norm_gain[None, :])
    routes = owner_ids[0, :, 0]
    target = slot_targets(routes, owners, capacity)
    select = (slot_range[:, None] == target[None, :]).astype(jnp.bfloat16)
    outgoing = jnp.dot(select, normed, preferred_element_type=jnp.float32).astype(jnp.bfloat16)
    outgoing = outgoing.reshape(owners, capacity, width_out)
    result = lax.all_to_all(outgoing, ("tm", "farm"), split_axis=0, concat_axis=0, tiled=True)
    return result[None, None]


def solution(mesh):
    placed = (
        P("farm", "tm", "head"),
        P("farm", "tm", None),
        P("farm", "tm", None),
        P("farm", "tm", "head"),
        P("head"),
        P("head", None),
        P(),
        P("farm", ("tm", "head"), None),
    )
    return jax.shard_map(
        shards,
        mesh=mesh,
        in_specs=placed,
        out_specs=P(("tm", "farm"), "head", None, None, None),
        check_vma=False,
    )
```

profile of v0, /device:TPU:1, one launch (start us, length us, event | category | flops | bytes accessed | tf_op | source)
XLA Modules:
  0.0 397.1 jit_solution(476489286207712375)
XLA Ops:
  6.5 2.8 copy.35
  9.3 3.1 reshape.131
  15.3 67.4 %while.27 = (s32[]{:T(128)}, f32[12,64,128]{2,1,0:T(8,128)S(1)}, f32[2,256,12,64]{1,0,3,2:T(2,128)}, f32[2,256,12]{1,0,2:T(2,128)}, f32[2,256,12,64]{1,0,3,2:T(2...) while((s32[]{:T(128)}, f32[12,64,128]{2,1,0:T(8,128)S(1)}, ...), condition=%wide.region_5.6_spmd.clone, body=%wide.region_2.5_spmd.clone.sunk | while | flops 1313213440 | bytes 11324756 | solution.py:89
  17.8 1.3 fusion.76
  19.1 2.2 constant_dynamic-slice_fusion.4
  21.4 4.6 %fusion.77 = f32[256,12,64]{0,2,1:T(8,128)} fusion(f32[256,256]{1,0:T(8,128)S(1)} %fusion.76, f32[12,256]{1,0:T(8,128)S(1)} %bitcast.116, pred[256,256]{1,0:T(8,128)(4,1)S(1)} %iota_compare_fusion.5, f32[1,256,12,64]{1,0,3,2:T(1,128)S(1)} %constant_dynamic-slice_fusion.4), kind=kOutput, calls=%fused_computation.14.clone.1 | convolution fusion | flops 607125504 | bytes 1912832 | tf_op jit(solution)/shard_map/while/body/eval_jaxpr/hts,shp->thp/dot_general | solution.py:42
  26.0 1.9 fusion.78
  28.0 1.7 copy.78
  29.7 16.7 %dynamic_update_slice.6 = f32[2,256,12,64]{1,0,3,2:T(2,128)} dynamic-update-slice(f32[2,256,12,64]{1,0,3,2:T(2,128)} %get-tuple-element.321, f32[1,256,12,64]{1,0,3,2:T(1,128)} %copy.78, s32[]{:T(128)} %get-tuple-element.319, s32[]{:T(128)} %constant.61.clone.1..sunk, s32[]{:T(128)} %constant.61.clone.1..sunk, s32[]{:T(128)} %constant.61.clone.1..sunk) | dynamic-update-slice | bytes 1572868 | tf_op jit(solution)/shard_map/while/body/jit(dynamic_update_index_in_dim)/dynamic_update_slice | solution.py:89
  47.1 1.8 convolution_add_fusion.2
  51.5 1.3 fusion.76
  52.8 2.2 constant_dynamic-slice_fusion.4
  55.1 4.6 %fusion.77 = f32[256,12,64]{0,2,1:T(8,128)} fusion(f32[256,256]{1,0:T(8,128)S(1)} %fusion.76, f32[12,256]{1,0:T(8,128)S(1)} %bitcast.116, pred[256,256]{1,0:T(8,128)(4,1)S(1)} %iota_compare_fusion.5, f32[1,256,12,64]{1,0,3,2:T(1,128)S(1)} %constant_dynamic-slice_fusion.4), kind=kOutput, calls=%fused_computation.14.clone.1 | convolution fusion | flops 607125504 | bytes 1912832 | tf_op jit(solution)/shard_map/while/body/eval_jaxpr/hts,shp->thp/dot_general | solution.py:42
  59.8 2.0 fusion.78
  61.7 1.7 copy.78
  63.4 16.7 %dynamic_update_slice.6 = f32[2,256,12,64]{1,0,3,2:T(2,128)} dynamic-update-slice(f32[2,256,12,64]{1,0,3,2:T(2,128)} %get-tuple-element.321, f32[1,256,12,64]{1,0,3,2:T(1,128)} %copy.78, s32[]{:T(128)} %get-tuple-element.319, s32[]{:T(128)} %constant.61.clone.1..sunk, s32[]{:T(128)} %constant.61.clone.1..sunk, s32[]{:T(128)} %constant.61.clone.1..sunk) | dynamic-update-slice | bytes 1572868 | tf_op jit(solution)/shard_map/while/body/jit(dynamic_update_index_in_dim)/dynamic_update_slice | solution.py:89
  80.8 1.8 convolution_add_fusion.2
  84.2 1.3 dynamic-slice
  86.9 125.1 %all-reduce = bf16[768]{0:T(1024)(128)(2,1)S(1)} all-reduce(bf16[768]{0:T(1024)(128)(2,1)S(1)} %dynamic-update-slice), channel_id=2, replica_groups=mesh['tm'=64,'head'=4,'farm'=2] {'tm'}, use_global_device_ids=true, to_apply=%add | all-reduce | flops 768 | bytes 3072
  212.2 3.3 reshape.126
  215.5 1.2 reduce-window.16
  217.1 70.1 %while.28 = (s32[]{:T(128)}, f32[12,64,128]{2,1,0:T(8,128)S(1)}, s32[]{:T(128)}, bf16[64,12]{1,0:T(8,128)(2,1)S(1)}, bf16[64,12,64,128]{3,2,1,0:T(8,128)(2,1)}, /*index=5*/s32[]{:T(128)}, s32[]{:T(128)}) while((s32[]{:T(128)}, f32[12,64,128]{2,1,0:T(8,128)S(1)}, s32[]{:T(128)}, bf16[64,12]{1,0:T(8,128)(2,1)S(1)}, ...), condition=%wide.region_10.11_spmd.clone, body=%wide.region_9.10_spmd.clone.sunk | while | flops 491536 | bytes 983265 | solution.py:29
  217.1 1.1 fusion.79
  218.2 1.1 fusion.79
  219.3 1.1 fusion.79
  220.4 1.1 fusion.79
  221.5 1.1 fusion.79
  222.6 1.1 fusion.79
  223.7 1.1 fusion.79
  224.8 1.1 fusion.79
  225.9 1.1 fusion.79
  227.0 1.1 fusion.79
  228.1 1.1 fusion.79
  229.2 1.1 fusion.79
  230.3 1.1 fusion.79
  231.4 1.1 fusion.79
  232.5 1.1 fusion.79
  233.6 1.1 fusion.79
  234.7 1.1 fusion.79
  235.8 1.1 fusion.79
  236.9 1.1 fusion.79
  287.2 2.8 fusion.42
  290.0 2.6 convolution_convert_fusion
  293.7 49.8 %reduce-scatter.2.cloned.1.call-done = bf16[128,1536]{1,0:T(8,128)(2,1)} async-done(((bf16[512,1536]{1,0:T(8,128)(2,1)}), bf16[128,1536]{1,0:T(8,128)(2,1)}) %reduce-scatter.2.cloned.1.call-update) | async-done | bytes 393232 | tf_op jit(solution)/shard_map/reduce_scatter | solution.py:112
  343.5 1.2 fusion.43
  344.7 2.3 convolution_convert_fusion.1
  347.0 2.2 reshape.129
  349.1 40.2 %all_to_all.5 = bf16[128,2,1536]{2,1,0:T(2,128)(2,1)S(1)} all-to-all(bf16[128,2,1536]{2,1,0:T(2,128)(2,1)S(1)} %reshape.129), channel_id=1, replica_groups=mesh['tm'=64,'head'=4,'farm'=2] {'tm','farm'}, dimensions={0} | all-to-all | bytes 1572864 | tf_op jit(solution)/shard_map/all_to_all | solution.py:124
  (193 shorter events, 62.1 us)
Async XLA Ops:
  6.5 283.4 %copy-start = (bf16[768,1536]{1,0:T(8,128)(2,1)S(1)}, bf16[768,1536]{1,0:T(8,128)(2,1)}, u32[]{:S(2)}) copy-start(bf16[768,1536]{1,0:T(8,128)(2,1)} %param.17) | copy-start | bytes 7077892
  6.5 210.5 %all-gather.4.cloned.1.call-start = ((), (), s32[]{:S(2)}) async-start(), calls=%async_computation.3 | async-start | bytes 12779520 | tf_op jit(solution)/shard_map/all_gather | solution.py:12
  9.3 3.1 copy-start.4
  9.3 4.5 %copy-start.3 = (bf16[1,512,128]{2,1,0:T(8,128)(2,1)S(1)}, bf16[1,512,128]{2,1,0:T(8,128)(2,1)}, u32[]{:S(2)}) copy-start(bf16[1,512,128]{2,1,0:T(8,128)(2,1)} %param.13) | copy-start | bytes 393220
  9.3 5.2 %copy-start.1 = (bf16[1,512,128]{2,1,0:T(8,128)(2,1)S(1)}, bf16[1,512,128]{2,1,0:T(8,128)(2,1)}, u32[]{:S(2)}) copy-start(bf16[1,512,128]{2,1,0:T(8,128)(2,1)} %param.14) | copy-start | bytes 393220
  17.1 2.0 copy-start.5
  50.9 2.0 copy-start.5
  83.4 260.1 %reduce-scatter.2.cloned.1.call-start = ((), (), s32[]{:S(2)}) async-start(), calls=%async_computation.2 | async-start | bytes 1966080 | tf_op jit(solution)/shard_map/reduce_scatter | solution.py:112
  217.1 70.1 %copy-start.2 = (bf16[1,512,128]{2,1,0:T(8,128)(2,1)S(1)}, bf16[1,512,128]{2,1,0:T(8,128)(2,1)}, u32[]{:S(2)}) copy-start(bf16[1,512,128]{2,1,0:T(8,128)(2,1)} %param.14) | copy-start | bytes 393220
  217.1 70.1 %copy-start.8 = (f32[12]{0:T(128)S(1)}, f32[12]{0:T(128)}, u32[]{:S(2)}) copy-start(f32[12]{0:T(128)} %param.16) | copy-start | bytes 148
  292.6 0.7 copy-start.7
  292.6 52.1 %copy-start.6 = (f32[1536]{0:T(1024)S(1)}, f32[1536]{0:T(1024)}, u32[]{:S(2)}) copy-start(f32[1536]{0:T(1024)} %param.18) | copy-start | bytes 18436
Sparse Core Ops, SparseCore 0:
  83.5 126.5 all-gather.3
  292.7 50.7 reduce-scatter.1
where the time goes:
time: 402 us; the launch traced here: 397 us
  blocking collectives  165 us (41%)
  other arithmetic  76.6 us (19%)
  local copies, waits for them, and re-layouts  61.7 us (15%)
  waiting for transfers between devices  49.9 us (12%)
  matrix products  27.2 us (7%)
  between operations  14.2 us (4%)
    unnamed x1, blocking collectives  125 us
    select_n x64, other arithmetic, lap(): return jax.tree.map(lambda a, b: jnp.where(reached, a, b), new, before)  67.3 us
    reduce_scatter x1, waiting for transfers between devices, shards(): lax.psum_scatter(jnp.dot(mixed_out, w_out, preferred_element_type=jnp.flo...  49.8 us
    all_to_all x1, blocking collectives, shards(): lax.all_to_all(outgoing, ('tm', 'farm'), split_axis=0, concat_axis=0, til...  40.2 us
    dynamic_update_slice x4, local copies, waits for them, and re-layouts, shards(): local_state, local_out = lax.scan(span_step, start_state, pieces)  36.9 us
    dot_general x2, matrix products, span_step(): jnp.einsum('hts,shp->thp', mixing, inputs_block, precision=lax.Precision....  9.28 us
  transfers between devices with their start and end apart: 2, of which 1 were waited for; matrix products, arithmetic and copies ran while one was open for 2% of the time, Pallas kernels for 0%

commit v1 on v0

v1 whole, which is shorter than its diff:
```python
import functools
import jax
import jax.numpy as jnp
from jax import lax
from jax.experimental import pallas as pl
from jax.experimental.pallas import tpu as pltpu
from jax.sharding import PartitionSpec as P

SPAN = 64
LANES = 128
F32 = jnp.float32
BF16 = jnp.bfloat16
FIRST = (((0,), (0,)), ((), ()))
LAST = (((1,), (1,)), ((), ()))


def mm(a, b):
    return jnp.dot(a, b, preferred_element_type=F32)


def split2(value):
    high = value.astype(BF16)
    return high, (value - high.astype(F32)).astype(BF16)


def split3(value):
    high = value.astype(BF16)
    rest = value - high.astype(F32)
    middle = rest.astype(BF16)
    return high, middle, (rest - middle.astype(F32)).astype(BF16)


def head_spread(rows, width, group):
    head = lax.broadcasted_iota(jnp.int32, (rows, width), 0) * group
    lane = lax.broadcasted_iota(jnp.int32, (rows, width), 1)
    return ((lane >= head) & (lane < head + group)).astype(BF16)


def spread(value, matrix):
    high, low = split2(value)
    return mm(high, matrix) + mm(low, matrix)


def state_kernel(x_ref, b_ref, decay_ref, out_ref, sums_ref, wx_ref, state_ref):
    steps, width = x_ref.shape
    heads = decay_ref.shape[1]
    spans = steps // SPAN
    parts = split3(decay_ref[...])
    row = lax.broadcasted_iota(jnp.int32, (SPAN, SPAN), 0)
    column = lax.broadcasted_iota(jnp.int32, (SPAN, SPAN), 1)
    lower = (row >= column).astype(BF16)
    matrix = head_spread(heads, width, width // heads)
    sums = []
    for k in range(spans):
        rows = slice(k * SPAN, (k + 1) * SPAN)
        local = sum(mm(lower, part[rows]) for part in parts)
        sums_ref[rows, :] = local
        sums.append(local)
    later = jnp.zeros((1, heads), F32)
    for k in reversed(range(spans)):
        rows = slice(k * SPAN, (k + 1) * SPAN)
        total = sums[k][SPAN - 1 : SPAN, :]
        weight = jnp.exp(total - sums[k] + later)
        wx_ref[rows, :] = (x_ref[rows, :].astype(F32) * spread(weight, matrix)).astype(BF16)
        later = later + total
    state_ref[...] = lax.dot_general(b_ref[...], wx_ref[...], FIRST, preferred_element_type=F32)
    parcels = out_ref.shape[0]
    depth = out_ref.shape[1]
    unit = head_spread(heads, LANES, 1)
    high, low = split2(later)
    tail = jnp.concatenate([mm(high, unit), mm(low, unit)], axis=0).astype(BF16)
    for k in range(parcels):
        out_ref[k, :, :width] = state_ref[k * depth : (k + 1) * depth, :].astype(BF16)
        out_ref[k, :, width:] = tail


def prefix_kernel(heads, in_ref, out_ref, log_ref):
    parcels, depth, width = out_ref.shape
    matrix = head_spread(LANES, width, width // heads)
    logs = in_ref[:, :, width:].reshape(parcels * depth, LANES)
    log_ref[...] = mm(logs, matrix)
    carried = jnp.zeros((depth, width), F32)
    for k in range(parcels):
        out_ref[k] = carried.astype(BF16)
        both = log_ref[k * depth : (k + 1) * depth, :]
        factor = jnp.exp(both[0:1, :] + both[1:2, :])
        carried = factor * carried + in_ref[k, :, :width].astype(F32)


def project_kernel(
    index_ref, x_ref, b_ref, c_ref, sums_ref, skip_ref, prior_ref, w_ref, *rest
):
    outs, (state_ref, mixed_ref) = rest[:-2], rest[-2:]
    steps, width = x_ref.shape
    heads = sums_ref.shape[1]
    spans = steps // SPAN
    pieces = len(outs)
    piece_spans = spans // pieces
    parcels, depth, _ = prior_ref.shape
    for k in range(parcels):
        state_ref[k * depth : (k + 1) * depth, :] = prior_ref[k].astype(F32)
    matrix = head_spread(heads, width, width // heads)
    row = lax.broadcasted_iota(jnp.int32, (SPAN, SPAN), 0)
    column = lax.broadcasted_iota(jnp.int32, (SPAN, SPAN), 1)
    causal = row >= column
    skip = spread(skip_ref[...], matrix)
    mine = index_ref[0]
    for k in range(spans):
        rows = slice(k * SPAN, (k + 1) * SPAN)
        local = sums_ref[rows, :]
        middle = 0.5 * local[SPAN - 1 : SPAN, :]
        up = spread(jnp.exp(local - middle), matrix)
        down = spread(jnp.exp(middle - local), matrix)
        half = up[SPAN - 1 : SPAN, :]
        x = x_ref[rows, :].astype(F32)
        b = b_ref[rows, :]
        c = c_ref[rows, :]
        scaled = (x * down).astype(BF16)
        scores = lax.dot_general(c, b, LAST, preferred_element_type=F32)
        scores = jnp.where(causal, scores, 0.0).astype(BF16)
        state = state_ref[...]
        y = mm(scores, scaled) + mm(c, (state * half).astype(BF16))
        y = up * y + skip * x
        slot = lax.rem(k // piece_spans - mine + pieces, pieces)
        start = pl.multiple_of((slot * piece_spans + k % piece_spans) * SPAN, SPAN)
        mixed_ref[pl.ds(start, SPAN), :] = y.astype(BF16)
        if k < spans - 1:
            update = lax.dot_general(b, scaled, FIRST, preferred_element_type=F32)
            state_ref[...] = half * (half * state + update)
    block = steps // pieces
    tile = 256
    for j in range(w_ref.shape[1] // tile):
        columns = slice(j * tile, (j + 1) * tile)
        product = mm(mixed_ref[...], w_ref[:, columns]).astype(BF16)
        for d in range(pieces):
            outs[d][:, columns] = product[d * block : (d + 1) * block, :]


def regroup_kernel(across_ref, down_ref, gain_ref, *rest):
    parts, out_ref = rest[:-1], rest[-1]
    owners, capacity, width = out_ref.shape
    rows = parts[0].shape[0]
    projected = sum(part[...].astype(F32) for part in parts)
    scale = lax.rsqrt(jnp.mean(projected * projected, axis=1, keepdims=True) + 1e-06)
    normed = (projected * scale * gain_ref[...]).astype(BF16)
    across = across_ref[...]
    earlier = lax.broadcasted_iota(jnp.int32, (rows, rows), 0) < lax.broadcasted_iota(
        jnp.int32, (rows, rows), 1
    )
    same = (down_ref[...] == across) & earlier
    slot = jnp.sum(same.astype(jnp.int32), axis=0, keepdims=True)
    target = across * capacity + slot
    place = lax.broadcasted_iota(jnp.int32, (owners * capacity, rows), 0)
    select = (place == target).astype(BF16)
    out_ref[...] = mm(select, normed).astype(BF16).reshape(owners, capacity, width)


def call(kernel, outs, scratch, flops, moved, *args, smem=0):
    vmem = pl.BlockSpec(memory_space=pltpu.VMEM)
    specs = [pl.BlockSpec(memory_space=pltpu.SMEM)] * smem + [vmem] * (len(args) - smem)
    return pl.pallas_call(
        kernel,
        out_shape=outs,
        in_specs=specs,
        out_specs=jax.tree.map(lambda _: vmem, outs),
        scratch_shapes=scratch,
        cost_estimate=pl.CostEstimate(flops=flops, bytes_accessed=moved, transcendentals=0),
        compiler_params=pltpu.CompilerParams(vmem_limit_bytes=32 * 1024 * 1024),
    )(*args)


def shards(head_inputs, b_proj, c_proj, log_decay, skip_gain, w_out, norm_gain, owner_ids):
    x, b, c, decays = head_inputs[0], b_proj[0], c_proj[0], log_decay[0]
    steps, width = x.shape
    heads = decays.shape[1]
    state_dim = b.shape[1]
    width_out = w_out.shape[1]
    times = lax.axis_size("tm")
    pieces = lax.axis_size("head")
    owners = times * lax.axis_size("farm")
    block = steps // pieces
    capacity = max(2, 2 * block // owners)
    depth = state_dim // times
    spec = jax.ShapeDtypeStruct
    parcel, sums = call(
        state_kernel,
        (spec((times, depth, width + LANES), BF16), spec((steps, heads), F32)),
        [pltpu.VMEM((steps, width), BF16), pltpu.VMEM((state_dim, width), F32)],
        2 * steps * width * state_dim,
        2 * steps * width,
        x,
        b,
        decays,
    )
    parcel = lax.all_to_all(parcel, "tm", split_axis=0, concat_axis=0, tiled=True)
    prior = call(
        functools.partial(prefix_kernel, heads),
        spec((times, depth, width), BF16),
        [pltpu.VMEM((times * depth, width), F32)],
        2 * state_dim * width * LANES,
        4 * state_dim * width,
        parcel,
    )
    prior = lax.all_to_all(prior, "tm", split_axis=0, concat_axis=0, tiled=True)
    index = lax.axis_index("head").astype(jnp.int32).reshape(1)
    parts = call(
        project_kernel,
        (spec((block, width_out), BF16),) * pieces,
        [pltpu.VMEM((state_dim, width), F32), pltpu.VMEM((steps, width), BF16)],
        2 * steps * width * (width_out + 2 * state_dim),
        2 * steps * (width + width_out) + 2 * width * width_out,
        index,
        x,
        b,
        c,
        sums,
        skip_gain[None, :],
        prior,
        w_out,
        smem=1,
    )
    ring = range(pieces)
    parts = [parts[0]] + [
        lax.ppermute(parts[d], "head", [(k, (k + d) % pieces) for k in ring])
        for d in range(1, pieces)
    ]
    outgoing = call(
        regroup_kernel,
        spec((owners, capacity, width_out), BF16),
        [],
        2 * owners * capacity * block * width_out,
        12 * block * width_out,
        owner_ids[0, :, 0][None, :],
        owner_ids[0],
        norm_gain[None, :],
        *parts,
    )
    result = lax.all_to_all(outgoing, ("tm", "farm"), split_axis=0, concat_axis=0, tiled=True)
    return result[None, None]


def solution(mesh):
    placed = (
        P("farm", "tm", "head"),
        P("farm", "tm", None),
        P("farm", "tm", None),
        P("farm", "tm", "head"),
        P("head"),
        P("head", None),
        P(),
        P("farm", ("tm", "head"), None),
    )
    return jax.shard_map(
        shards,
        mesh=mesh,
        in_specs=placed,
        out_specs=P(("tm", "farm"), "head", None, None, None),
        check_vma=False,
    )
```

time: 402 us -> 116 us (0.29)
  blocking collectives: 165 us -> 62 us
  other arithmetic: 76.6 us -> 0 us
  local copies, waits for them, and re-layouts: 61.7 us -> 5.63 us
  matrix products: 27.2 us -> 0 us
  waiting for transfers between devices: 49.9 us -> 23.3 us
  starting transfers between devices: 0.04 us -> 16.3 us
  between operations: 14.2 us -> 0.13 us
  Pallas kernels: 0 us -> 7.23 us
    unnamed x1 -> x0, blocking collectives: 125 us -> none
    select_n x64 -> x0, other arithmetic: 67.3 us -> none  [lap(): return jax.tree.map(lambda a, b: jnp.where(reached, a, b), new, before)]
    reduce_scatter x1 -> x0, waiting for transfers between devices: 49.8 us -> none  [shards(): lax.psum_scatter(jnp.dot(mixed_out, w_out, preferred_element_type=jnp.flo...]
    dynamic_update_slice x4 -> x0, local copies, waits for them, and re-layouts: 36.9 us -> none  [shards(): local_state, local_out = lax.scan(span_step, start_state, pieces)]
    all_to_all x0 -> x1, blocking collectives: none -> 29 us  [shards(): lax.all_to_all(parcel, 'tm', split_axis=0, concat_axis=0, tiled=True)]
    dot_general x11 -> x0, matrix products: 27.2 us -> none  [the longest x2 9.28 us: span_step(): jnp.einsum('hts,shp->thp', mixing, inputs_block, precision=lax.Precision....]
    all_to_all x0 -> x1, waiting for transfers between devices: none -> 11.8 us  [shards(): prior = lax.all_to_all(prior, 'tm', split_axis=0, concat_axis=0, tiled=True)]
    ppermute x0 -> x3, waiting for transfers between devices: none -> 11.4 us  [shards(): lax.ppermute(parts[d], 'head', [(k, (k + d) % pieces) for k in ring])]
  transfers between devices with their start and end apart: 2 -> 4, of which waited for: 1 -> 3; matrix products, arithmetic and copies ran while one was open for 2% -> 0% of each run, Pallas kernels for 0% -> 0%
where the time goes in v1:
time: 116 us; the launch traced here: 115 us
  blocking collectives  62 us (53%)
  waiting for transfers between devices  23.3 us (20%)
  starting transfers between devices  16.3 us (14%)
  Pallas kernels  7.23 us (6%)
  local copies, waits for them, and re-layouts  5.63 us (5%)
    all_to_all x1, blocking collectives, shards(): lax.all_to_all(outgoing, ('tm', 'farm'), split_axis=0, concat_axis=0, til...  33 us
    all_to_all x1, blocking collectives, shards(): lax.all_to_all(parcel, 'tm', split_axis=0, concat_axis=0, tiled=True)  29 us
    all_to_all x1, waiting for transfers between devices, shards(): prior = lax.all_to_all(prior, 'tm', split_axis=0, concat_axis=0, tiled=True)  11.8 us
    ppermute x3, waiting for transfers between devices, shards(): lax.ppermute(parts[d], 'head', [(k, (k + d) % pieces) for k in ring])  11.4 us
    ppermute x3, starting transfers between devices, shards(): lax.ppermute(parts[d], 'head', [(k, (k + d) % pieces) for k in ring])  10.5 us
    pallas_call x4, Pallas kernels, call(): pl.pallas_call(kernel, out_shape=outs, in_specs=specs, out_specs=jax.tree...  7.23 us
    all_to_all x1, starting transfers between devices, shards(): prior = lax.all_to_all(prior, 'tm', split_axis=0, concat_axis=0, tiled=True)  5.79 us
    unnamed x20, local copies, waits for them, and re-layouts  5.51 us
  transfers between devices with their start and end apart: 4, of which 3 were waited for; matrix products, arithmetic and copies ran while one was open for 0% of the time, Pallas kernels for 0%

profile of v1, /device:TPU:1, one launch (start us, length us, event | category | flops | bytes accessed | tf_op | source)
XLA Modules:
  0.0 114.6 jit_solution(4359399420010734266)
XLA Ops:
  0.0 0.0 copy-start.3
  0.0 0.0 copy-start.7
  0.0 0.0 copy-start.6
  0.0 0.9 copy.9
  0.9 0.0 copy-start
  0.9 1.1 copy-done
  2.1 0.0 copy-start.2
  2.1 0.9 copy-done.2
  3.0 0.0 copy-start.1
  3.0 1.2 %shard_map.82 = (bf16[64,2,896]{2,1,0:T(2,128)(2,1)S(1)}, f32[512,12]{1,0:T(8,128)S(1)}) custom-call(bf16[512,768]{1,0:T(8,128)(2,1)S(1)} %bitcast.10, bf16[512,128]{1,0:T(8,128)(2,1)S(1)} %bitcast.12, f32[512,12]{1,0:T(8,128)S(1)} %bitcast.9), custom_call_target="tpu_custom_call" | custom-call | flops 100663296 | bytes 786432 | tf_op jit(solution)/shard_map/pallas_call | solution.py:161
  4.1 29.0 %all_to_all.15.in_ref = bf16[64,2,896]{2,1,0:T(2,128)(2,1)S(1)} all-to-all(bf16[64,2,896]{2,1,0:T(2,128)(2,1)S(1)} %get-tuple-element.12), channel_id=1, replica_groups=mesh['tm'=64,'head'=4,'farm'=2] {'tm'}, dimensions={0} | all-to-all | bytes 458752 | tf_op jit(solution)/shard_map/all_to_all | solution.py:195
  33.1 1.3 %shard_map.83 = bf16[64,2,768]{2,1,0:T(2,128)(2,1)} custom-call(bf16[64,2,896]{2,1,0:T(2,128)(2,1)S(1)} %all_to_all.15.in_ref), custom_call_target="tpu_custom_call" | custom-call | flops 25165824 | bytes 393216 | tf_op jit(solution)/shard_map/pallas_call | solution.py:161
  34.5 5.8 %all-to-all-start.1 = ((bf16[64,2,768]{2,1,0:T(2,128)(2,1)}), bf16[64,2,768]{2,1,0:T(2,128)(2,1)S(1)}, u32[]{:S(2)}, u32[]{:S(2)}) async-start(bf16[64,2,768]{2,1,0:T(2,128)(2,1)} %shard_map.83), calls=%async_computation.1 | async-start | bytes 393216 | tf_op jit(solution)/shard_map/all_to_all | solution.py:204
  40.3 11.8 %all-to-all-done.1.prior_ref = bf16[64,2,768]{2,1,0:T(2,128)(2,1)S(1)} async-done(((bf16[64,2,768]{2,1,0:T(2,128)(2,1)}), bf16[64,2,768]{2,1,0:T(2,128)(2,1)S(1)}, u32[]{:S(2)}, u32[]{:S(2)}) %all-to-all-start.1) | async-done | bytes 196640 | tf_op jit(solution)/shard_map/all_to_all | solution.py:204
  52.1 0.0 copy-done.3
  52.1 0.0 copy-done.7
  52.1 0.0 copy-done.6
  52.1 0.0 copy-done.1
  52.2 0.0 copy-start.5
  52.2 1.7 %copy-done.5 = bf16[768,1536]{1,0:T(8,128)(2,1)S(1)} copy-done((bf16[768,1536]{1,0:T(8,128)(2,1)S(1)}, bf16[768,1536]{1,0:T(8,128)(2,1)}, u32[]{:S(2)}) %copy-start.5) | copy-done | bytes 2359320
  53.8 0.0 copy-start.8
  53.8 0.0 copy-start.4
  53.8 4.0 %shard_map.84 = (bf16[128,1536]{1,0:T(8,128)(2,1)S(1)}, bf16[128,1536]{1,0:T(8,128)(2,1)S(1)}, bf16[128,1536]{1,0:T(8,128)(2,1)S(1)}, bf16[128,1536]{1,0:T(8,128)(2,1)S(1)}) custom-call(s32[1]{0:T(128)} %bitcast.2.index_ref, bf16[512,768]{1,0:T(8,128)(2,1)S(1)} %bitcast.11, bf16[512,128]{1,0:T(8,128)(2,1)S(1)} %bitcast.13, bf16[512,128]{1,0:T(8,128)(2,1)S(1)} %bitcast.16, ...), custom_call_target="tpu_custom_call" | custom-call | flops 1409286144 | bytes 4718592 | tf_op jit(solution)/shard_map/pallas_call | solution.py:161
  57.9 3.1 %collective-permute-start = (bf16[128,1536]{1,0:T(8,128)(2,1)S(1)}, bf16[128,1536]{1,0:T(8,128)(2,1)S(1)}, u32[]{:S(2)}, u32[]{:S(2)}) collective-permute-start(bf16[128,1536]{1,0:T(8,128)(2,1)S(1)} %get-tuple-element.14), channel_id=1, source_target_pairs={{0,2},{2,4},{4,6},{6,0},{1,3},{3,5},{5,7},{7,1},{8,10},{10,12},{12... | collective-permute-start | bytes 1179656 | tf_op jit(solution)/shard_map/ppermute | solution.py:224
  61.0 4.4 %collective-permute-start.1 = (bf16[128,1536]{1,0:T(8,128)(2,1)S(1)}, bf16[128,1536]{1,0:T(8,128)(2,1)S(1)}, u32[]{:S(2)}, u32[]{:S(2)}) collective-permute-start(bf16[128,1536]{1,0:T(8,128)(2,1)S(1)} %get-tuple-element.15), channel_id=1, source_target_pairs={{0,4},{2,6},{4,0},{6,2},{1,5},{3,7},{5,1},{7,3},{8,12},{10,14},{12... | collective-permute-start | bytes 1179656 | tf_op jit(solution)/shard_map/ppermute | solution.py:224
  65.4 3.0 %collective-permute-start.2 = (bf16[128,1536]{1,0:T(8,128)(2,1)S(1)}, bf16[128,1536]{1,0:T(8,128)(2,1)S(1)}, u32[]{:S(2)}, u32[]{:S(2)}) collective-permute-start(bf16[128,1536]{1,0:T(8,128)(2,1)S(1)} %get-tuple-element.16), channel_id=1, source_target_pairs={{0,6},{2,0},{4,2},{6,4},{1,7},{3,1},{5,3},{7,5},{8,14},{10,8},{12,... | collective-permute-start | bytes 1179656 | tf_op jit(solution)/shard_map/ppermute | solution.py:224
  68.4 0.0 copy-done.8
  68.4 0.0 copy-done.4
  68.5 0.1 copy.10.down_ref
  68.6 0.0 collective-permute-done.rest_1_
  68.6 9.1 %collective-permute-done.1.rest_2_ = bf16[128,1536]{1,0:T(8,128)(2,1)S(1)} collective-permute-done((bf16[128,1536]{1,0:T(8,128)(2,1)S(1)}, bf16[128,1536]{1,0:T(8,128)(2,1)S(1)}, u32[]{:S(2)}, u32[]{:S(2)}) %collective-permute-start.1) | collective-permute-done | bytes 393248 | tf_op jit(solution)/shard_map/ppermute | solution.py:224
  77.6 2.4 %collective-permute-done.2.rest_3_ = bf16[128,1536]{1,0:T(8,128)(2,1)S(1)} collective-permute-done((bf16[128,1536]{1,0:T(8,128)(2,1)S(1)}, bf16[128,1536]{1,0:T(8,128)(2,1)S(1)}, u32[]{:S(2)}, u32[]{:S(2)}) %collective-permute-start.2) | collective-permute-done | bytes 393248 | tf_op jit(solution)/shard_map/ppermute | solution.py:224
  80.0 0.7 shard_map.85
  80.7 33.0 %all_to_all.16 = bf16[128,2,1536]{2,1,0:T(2,128)(2,1)S(1)} all-to-all(bf16[128,2,1536]{2,1,0:T(2,128)(2,1)S(1)} %shard_map.85), channel_id=1, replica_groups=mesh['tm'=64,'head'=4,'farm'=2] {'tm','farm'}, dimensions={0} | all-to-all | bytes 1572864 | tf_op jit(solution)/shard_map/all_to_all | solution.py:238
  113.7 0.9 copy.12
  (1 shorter events, 0.0 us)
Async XLA Ops:
  0.0 52.1 %copy-start.3 = (bf16[1,512,128]{2,1,0:T(8,128)(2,1)S(1)}, bf16[1,512,128]{2,1,0:T(8,128)(2,1)}, u32[]{:S(2)}) copy-start(bf16[1,512,128]{2,1,0:T(8,128)(2,1)} %param.9) | copy-start | bytes 393220
  0.0 52.1 %copy-start.7 = (f32[12]{0:T(128)S(1)}, f32[12]{0:T(128)}, u32[]{:S(2)}) copy-start(f32[12]{0:T(128)} %param.12) | copy-start | bytes 148
  0.0 52.1 %copy-start.6 = (bf16[1,512,128]{2,1,0:T(8,128)(2,1)S(1)}, bf16[1,512,128]{2,1,0:T(8,128)(2,1)}, u32[]{:S(2)}) copy-start(bf16[1,512,128]{2,1,0:T(8,128)(2,1)} %param.10) | copy-start | bytes 393220
  0.9 1.1 copy-start
  2.1 0.9 copy-start.2
  3.0 49.2 %copy-start.1 = (bf16[1,512,768]{2,1,0:T(8,128)(2,1)S(1)}, bf16[1,512,768]{2,1,0:T(8,128)(2,1)}, u32[]{:S(2)}) copy-start(bf16[1,512,768]{2,1,0:T(8,128)(2,1)} %param.8) | copy-start | bytes 2359300
  34.5 17.6 %all-to-all-start.1 = ((bf16[64,2,768]{2,1,0:T(2,128)(2,1)}), bf16[64,2,768]{2,1,0:T(2,128)(2,1)S(1)}, u32[]{:S(2)}, u32[]{:S(2)}) async-start(bf16[64,2,768]{2,1,0:T(2,128)(2,1)} %shard_map.83), calls=%async_computation.1 | async-start | bytes 393216 | tf_op jit(solution)/shard_map/all_to_all | solution.py:204
  52.2 1.7 %copy-start.5 = (bf16[768,1536]{1,0:T(8,128)(2,1)S(1)}, bf16[768,1536]{1,0:T(8,128)(2,1)}, u32[]{:S(2)}) copy-start(bf16[768,1536]{1,0:T(8,128)(2,1)} %w_ref.1) | copy-start | bytes 7077892
  53.8 14.6 %copy-start.8 = (f32[1536]{0:T(1024)S(1)}, f32[1536]{0:T(1024)}, u32[]{:S(2)}) copy-start(f32[1536]{0:T(1024)} %param.14) | copy-start | bytes 18436
  53.8 14.6 %copy-start.4 = (s32[1,128,1]{1,2,0:T(1,128)S(1)}, s32[1,128,1]{1,2,0:T(1,128)}, u32[]{:S(2)}) copy-start(s32[1,128,1]{1,2,0:T(1,128)} %param.15) | copy-start | bytes 1540
  57.9 10.7 %collective-permute-start = (bf16[128,1536]{1,0:T(8,128)(2,1)S(1)}, bf16[128,1536]{1,0:T(8,128)(2,1)S(1)}, u32[]{:S(2)}, u32[]{:S(2)}) collective-permute-start(bf16[128,1536]{1,0:T(8,128)(2,1)S(1)} %get-tuple-element.14), channel_id=1, source_target_pairs={{0,2},{2,4},{4,6},{6,0},{1,3},{3,5},{5,7},{7,1},{8,10},{10,12},{12... | collective-permute-start | bytes 1179656 | tf_op jit(solution)/shard_map/ppermute | solution.py:224
  61.0 16.6 %collective-permute-start.1 = (bf16[128,1536]{1,0:T(8,128)(2,1)S(1)}, bf16[128,1536]{1,0:T(8,128)(2,1)S(1)}, u32[]{:S(2)}, u32[]{:S(2)}) collective-permute-start(bf16[128,1536]{1,0:T(8,128)(2,1)S(1)} %get-tuple-element.15), channel_id=1, source_target_pairs={{0,4},{2,6},{4,0},{6,2},{1,5},{3,7},{5,1},{7,3},{8,12},{10,14},{12... | collective-permute-start | bytes 1179656 | tf_op jit(solution)/shard_map/ppermute | solution.py:224
  65.4 14.6 %collective-permute-start.2 = (bf16[128,1536]{1,0:T(8,128)(2,1)S(1)}, bf16[128,1536]{1,0:T(8,128)(2,1)S(1)}, u32[]{:S(2)}, u32[]{:S(2)}) collective-permute-start(bf16[128,1536]{1,0:T(8,128)(2,1)S(1)} %get-tuple-element.16), channel_id=1, source_target_pairs={{0,6},{2,0},{4,2},{6,4},{1,7},{3,1},{5,3},{7,5},{8,14},{10,8},{12,... | collective-permute-start | bytes 1179656 | tf_op jit(solution)/shard_map/ppermute | solution.py:224

commit v2 on v1

v2 whole, which is shorter than its diff:
```python
import functools
import jax
import jax.numpy as jnp
from jax import lax
from jax.experimental import pallas as pl
from jax.experimental.pallas import tpu as pltpu
from jax.sharding import PartitionSpec as P

SPAN = 64
LANES = 128
F32 = jnp.float32
BF16 = jnp.bfloat16
FIRST = (((0,), (0,)), ((), ()))
LAST = (((1,), (1,)), ((), ()))


def mm(a, b):
    return jnp.dot(a, b, preferred_element_type=F32)


def split2(value):
    high = value.astype(BF16)
    return high, (value - high.astype(F32)).astype(BF16)


def split3(value):
    high = value.astype(BF16)
    rest = value - high.astype(F32)
    middle = rest.astype(BF16)
    return high, middle, (rest - middle.astype(F32)).astype(BF16)


def head_spread(rows, width, group):
    head = lax.broadcasted_iota(jnp.int32, (rows, width), 0) * group
    lane = lax.broadcasted_iota(jnp.int32, (rows, width), 1)
    return ((lane >= head) & (lane < head + group)).astype(BF16)


def spread(value, matrix):
    high, low = split2(value)
    return lax.dot_general(high, matrix, FIRST, preferred_element_type=F32) + lax.dot_general(
        low, matrix, FIRST, preferred_element_type=F32
    )


def running(values, keep):
    length = values.shape[1]
    s = lax.broadcasted_iota(jnp.int32, (length, length), 0)
    t = lax.broadcasted_iota(jnp.int32, (length, length), 1)
    chosen = keep(s, t).astype(BF16)
    return sum(mm(part, chosen) for part in split3(values))


def fetch(pairs, sems):
    copies = [pltpu.make_async_copy(a, b, sems.at[i]) for i, (a, b) in enumerate(pairs)]
    for copy in copies:
        copy.start()
    return copies


def state_kernel(x_hbm, b_hbm, decay_ref, out_ref, x_ref, b_ref, wx_ref, state_ref, sems):
    copies = fetch(((x_hbm, x_ref), (b_hbm, b_ref)), sems)
    heads, _, steps = decay_ref.shape
    width = x_ref.shape[1]
    matrix = head_spread(heads, width, width // heads)
    later = jnp.zeros((heads, 1), F32)
    weights = [None] * (steps // LANES)
    for k in reversed(range(steps // LANES)):
        values = decay_ref[:, 0, k * LANES : (k + 1) * LANES]
        weights[k] = jnp.exp(running(values, lambda s, t: s > t) + later)
        later = later + jnp.sum(values, axis=1, keepdims=True)
    for copy in copies:
        copy.wait()
    for k, weight in enumerate(weights):
        rows = slice(k * LANES, (k + 1) * LANES)
        wx_ref[rows, :] = (x_ref[rows, :].astype(F32) * spread(weight, matrix)).astype(BF16)
    state_ref[...] = lax.dot_general(b_ref[...], wx_ref[...], FIRST, preferred_element_type=F32)
    parcels, depth, _ = out_ref.shape
    unit = head_spread(heads, LANES, 1)
    tail = [
        lax.dot_general(part, unit, FIRST, preferred_element_type=F32)[0:1]
        for part in split2(jnp.broadcast_to(later, (heads, LANES)))
    ]
    out_ref[:, :, :width] = state_ref[...].astype(BF16).reshape(parcels, depth, width)
    tail = jnp.concatenate(tail, axis=0).astype(BF16)
    for k in range(parcels):
        out_ref[k, :, width:] = tail


def prefix_kernel(heads, in_ref, out_ref, log_ref):
    parcels, depth, width = out_ref.shape
    matrix = head_spread(LANES, width, width // heads)
    logs = in_ref[:, :, width:].reshape(parcels * depth, LANES)
    log_ref[...] = mm(logs, matrix)
    carried = jnp.zeros((depth, width), F32)
    for k in range(parcels):
        out_ref[k] = carried.astype(BF16)
        both = log_ref[k * depth : (k + 1) * depth, :]
        factor = jnp.exp(both[0:1, :] + both[1:2, :])
        carried = factor * carried + in_ref[k, :, :width].astype(F32)


def local_kernel(
    x_ref, b_ref, c_ref, w_hbm, decay_ref, skip_ref, out_ref, w_ref, state_ref, sems
):
    copies = fetch(((w_hbm, w_ref),), sems)
    heads, _, steps = decay_ref.shape
    width = x_ref.shape[1]
    matrix = head_spread(heads, width, width // heads)
    row = lax.broadcasted_iota(jnp.int32, (SPAN, SPAN), 0)
    column = lax.broadcasted_iota(jnp.int32, (SPAN, SPAN), 1)
    causal = row >= column
    first = lax.broadcasted_iota(jnp.int32, (heads, LANES), 1) < SPAN
    skip = spread(jnp.broadcast_to(skip_ref[...], (heads, LANES)), matrix)[0:1]
    for k in range(steps // LANES):
        values = decay_ref[:, 0, k * LANES : (k + 1) * LANES]
        local = running(values, lambda s, t: (s <= t) & ((s < SPAN) == (t < SPAN)))
        middle = 0.5 * jnp.where(
            first, local[:, SPAN - 1 : SPAN], local[:, LANES - 1 : LANES]
        )
        ups = spread(jnp.exp(local - middle), matrix)
        downs = spread(jnp.exp(middle - local), matrix)
        for part in range(LANES // SPAN):
            inner = slice(part * SPAN, (part + 1) * SPAN)
            rows = slice(k * LANES + part * SPAN, k * LANES + (part + 1) * SPAN)
            up = ups[inner]
            half = up[SPAN - 1 : SPAN, :]
            x = x_ref[rows, :].astype(F32)
            b = b_ref[rows, :]
            c = c_ref[rows, :]
            scaled = (x * downs[inner]).astype(BF16)
            scores = lax.dot_general(c, b, LAST, preferred_element_type=F32)
            scores = jnp.where(causal, scores, 0.0).astype(BF16)
            y = mm(scores, scaled)
            update = lax.dot_general(b, scaled, FIRST, preferred_element_type=F32)
            if rows.start == 0:
                state_ref[...] = half * update
            else:
                state = state_ref[...]
                y = y + mm(c, (state * half).astype(BF16))
                state_ref[...] = half * (half * state + update)
            out_ref[rows, :width] = (up * y + skip * x).astype(BF16)
            out_ref[rows, width:] = c
    for copy in copies:
        copy.wait()


def project_kernel(local_ref, decay_ref, prior_ref, w_ref, out_hbm, mixed_ref, send_ref, sems):
    heads, _, steps = decay_ref.shape
    parcels, depth, width = prior_ref.shape
    pieces, block, width_out = send_ref.shape
    state = prior_ref[...].reshape(parcels * depth, width)
    matrix = head_spread(heads, width, width // heads)
    before = jnp.zeros((heads, 1), F32)
    reaches = []
    for k in range(steps // LANES):
        values = decay_ref[:, 0, k * LANES : (k + 1) * LANES]
        reaches.append(jnp.exp(running(values, lambda s, t: s <= t) + before))
        before = before + jnp.sum(values, axis=1, keepdims=True)
    for k, reach in enumerate(reaches):
        rows = slice(k * LANES, (k + 1) * LANES)
        carried = spread(reach, matrix) * mm(local_ref[rows, width:], state)
        mixed_ref[rows, :] = (local_ref[rows, :width].astype(F32) + carried).astype(BF16)
    tile = 256
    sends = []
    for j in range(width_out // tile):
        columns = slice(j * tile, (j + 1) * tile)
        product = mm(mixed_ref[...], w_ref[:, columns]).astype(BF16)
        for d in range(pieces):
            send_ref[d, :, columns] = product[d * block : (d + 1) * block, :]
        sends += fetch(
            ((send_ref.at[:, :, columns], out_hbm.at[:, :, columns]),), sems.at[pl.ds(j, 1)]
        )
    for send in sends:
        send.wait()


def regroup_kernel(across_ref, down_ref, gain_ref, parts_ref, out_ref):
    owners, capacity, width = out_ref.shape
    pieces, rows, _ = parts_ref.shape
    projected = sum(parts_ref[k].astype(F32) for k in range(pieces))
    scale = lax.rsqrt(jnp.mean(projected * projected, axis=1, keepdims=True) + 1e-06)
    normed = (projected * scale * gain_ref[...]).astype(BF16)
    across = across_ref[...]
    earlier = lax.broadcasted_iota(jnp.int32, (rows, rows), 0) < lax.broadcasted_iota(
        jnp.int32, (rows, rows), 1
    )
    same = (down_ref[...] == across) & earlier
    slot = jnp.sum(same.astype(jnp.int32), axis=0, keepdims=True)
    target = across * capacity + slot
    place = lax.broadcasted_iota(jnp.int32, (owners * capacity, rows), 0)
    select = (place == target).astype(BF16)
    out_ref[...] = mm(select, normed).astype(BF16).reshape(owners, capacity, width)


def call(kernel, outs, scratch, flops, moved, limit, *args, far=(), out_far=False):
    vmem = pl.BlockSpec(memory_space=pltpu.VMEM)
    hbm = pl.BlockSpec(memory_space=pltpu.HBM)
    return pl.pallas_call(
        kernel,
        out_shape=outs,
        in_specs=[hbm if k in far else vmem for k in range(len(args))],
        out_specs=jax.tree.map(lambda _: hbm if out_far else vmem, outs),
        scratch_shapes=scratch,
        cost_estimate=pl.CostEstimate(flops=flops, bytes_accessed=moved, transcendentals=0),
        compiler_params=pltpu.CompilerParams(vmem_limit_bytes=int(limit * 1024 * 1024)),
    )(*args)


def shards(head_inputs, b_proj, c_proj, log_decay, skip_gain, w_out, norm_gain, owner_ids):
    x, b, c, decays = head_inputs[0], b_proj[0], c_proj[0], log_decay.transpose(2, 0, 1)
    steps, width = x.shape
    heads = decays.shape[0]
    state_dim = b.shape[1]
    width_out = w_out.shape[1]
    times = lax.axis_size("tm")
    pieces = lax.axis_size("head")
    owners = times * lax.axis_size("farm")
    block = steps // pieces
    capacity = max(2, 2 * block // owners)
    depth = state_dim // times
    spec = jax.ShapeDtypeStruct
    wide = pltpu.VMEM((steps, width), BF16)
    narrow = pltpu.VMEM((steps, state_dim), BF16)
    state = pltpu.VMEM((state_dim, width), F32)
    parcel = call(
        state_kernel,
        spec((times, depth, width + LANES), BF16),
        [wide, narrow, wide, state, pltpu.SemaphoreType.DMA((2,))],
        2 * steps * width * state_dim,
        2 * steps * width,
        63.4,
        x,
        b,
        decays,
        far=(0, 1),
    )
    parcel = lax.all_to_all(parcel, "tm", split_axis=0, concat_axis=0, tiled=True)
    local, weights = call(
        local_kernel,
        (spec((steps, width + state_dim), BF16), spec(w_out.shape, BF16)),
        [state, pltpu.SemaphoreType.DMA((1,))],
        6 * steps * width * state_dim,
        8 * steps * width,
        24,
        x,
        b,
        c,
        w_out,
        decays,
        skip_gain[:, None],
        far=(3,),
    )
    prior = call(
        functools.partial(prefix_kernel, heads),
        spec((times, depth, width), BF16),
        [pltpu.VMEM((times * depth, width), F32)],
        2 * state_dim * width * LANES,
        4 * state_dim * width,
        16,
        parcel,
    )
    prior = lax.all_to_all(prior, "tm", split_axis=0, concat_axis=0, tiled=True)
    parts = call(
        project_kernel,
        spec((pieces, block, width_out), BF16),
        [
            wide,
            pltpu.VMEM((pieces, block, width_out), BF16),
            pltpu.SemaphoreType.DMA((width_out // 256,)),
        ],
        2 * steps * width * (width_out + state_dim),
        2 * steps * (width + width_out) + 2 * width * width_out,
        24,
        local,
        decays,
        prior,
        weights,
        out_far=True,
    )
    parts = lax.all_to_all(parts, "head", split_axis=0, concat_axis=0, tiled=True)
    outgoing = call(
        regroup_kernel,
        spec((owners, capacity, width_out), BF16),
        [],
        2 * owners * capacity * block * width_out,
        12 * block * width_out,
        16,
        owner_ids[0, :, 0][None, :],
        owner_ids[0],
        norm_gain[None, :],
        parts,
    )
    result = lax.all_to_all(outgoing, ("tm", "farm"), split_axis=0, concat_axis=0, tiled=True)
    return result[None, None]


def solution(mesh):
    placed = (
        P("farm", "tm", "head"),
        P("farm", "tm", None),
        P("farm", "tm", None),
        P("farm", "tm", "head"),
        P("head"),
        P("head", None),
        P(),
        P("farm", ("tm", "head"), None),
    )
    return jax.shard_map(
        shards,
        mesh=mesh,
        in_specs=placed,
        out_specs=P(("tm", "farm"), "head", None, None, None),
        check_vma=False,
    )
```

time: 116 us -> 117 us (level)
  starting transfers between devices: 16.3 us -> 9.82 us
  blocking collectives: 62 us -> 68.3 us
  Pallas kernels: 7.23 us -> 12.6 us
  waiting for transfers between devices: 23.3 us -> 20.1 us
    all_to_all x0 -> x1, waiting for transfers between devices: none -> 16.9 us  [shards(): lax.all_to_all(parts, 'head', split_axis=0, concat_axis=0, tiled=True)]
    ppermute x3 -> x0, waiting for transfers between devices: 11.4 us -> none  [shards(): lax.ppermute(parts[d], 'head', [(k, (k + d) % pieces) for k in ring])]
    ppermute x3 -> x0, starting transfers between devices: 10.5 us -> none  [shards(): lax.ppermute(parts[d], 'head', [(k, (k + d) % pieces) for k in ring])]
    all_to_all x1, waiting for transfers between devices: 11.8 us -> 3.21 us  [shards(): prior = lax.all_to_all(prior, 'tm', split_axis=0, concat_axis=0, tiled=True)]
    all_to_all x1, blocking collectives: 33 us -> 39.1 us  [shards(): lax.all_to_all(outgoing, ('tm', 'farm'), split_axis=0, concat_axis=0, til...]
    pallas_call x4 -> x5, Pallas kernels: 7.23 us -> 12.6 us  [call(): pl.pallas_call(kernel, out_shape=outs, in_specs=[hbm if k in far else vme...]
    all_to_all x0 -> x1, starting transfers between devices: none -> 4.04 us  [shards(): lax.all_to_all(parts, 'head', split_axis=0, concat_axis=0, tiled=True)]
    unnamed x20 -> x17, local copies, waits for them, and re-layouts: 5.51 us -> 5.51 us
  transfers between devices with their start and end apart: 4 -> 2, of which waited for: 3 -> 2; matrix products, arithmetic and copies ran while one was open for 0% -> 0% of each run, Pallas kernels for 0% -> 3%
where the time goes in v2:
time: 117 us
  blocking collectives  68.3 us (58%)
  waiting for transfers between devices  20.1 us (17%)
  Pallas kernels  12.6 us (11%)
  starting transfers between devices  9.82 us (8%)
  local copies, waits for them, and re-layouts  5.72 us (5%)
    all_to_all x1, blocking collectives, shards(): lax.all_to_all(outgoing, ('tm', 'farm'), split_axis=0, concat_axis=0, til...  39.1 us
    all_to_all x1, blocking collectives, shards(): lax.all_to_all(parcel, 'tm', split_axis=0, concat_axis=0, tiled=True)  29.2 us
    all_to_all x1, waiting for transfers between devices, shards(): lax.all_to_all(parts, 'head', split_axis=0, concat_axis=0, tiled=True)  16.9 us
    pallas_call x5, Pallas kernels, call(): pl.pallas_call(kernel, out_shape=outs, in_specs=[hbm if k in far else vme...  12.6 us
    all_to_all x1, starting transfers between devices, shards(): prior = lax.all_to_all(prior, 'tm', split_axis=0, concat_axis=0, tiled=True)  5.78 us
    unnamed x17, local copies, waits for them, and re-layouts  5.51 us
    all_to_all x1, starting transfers between devices, shards(): lax.all_to_all(parts, 'head', split_axis=0, concat_axis=0, tiled=True)  4.04 us
    all_to_all x1, waiting for transfers between devices, shards(): prior = lax.all_to_all(prior, 'tm', split_axis=0, concat_axis=0, tiled=True)  3.21 us
  transfers between devices with their start and end apart: 2, of which 2 were waited for; matrix products, arithmetic and copies ran while one was open for 0% of the time, Pallas kernels for 3%

profile of v2, /device:TPU:1, one launch (start us, length us, event | category | flops | bytes accessed | tf_op | source)
XLA Modules:
  0.0 116.7 jit_solution(16611455431736056739)
XLA Ops:
  0.0 0.0 copy-start.3
  0.0 0.0 copy-start.7
  0.0 3.5 %shard_map.83 = bf16[64,2,896]{2,1,0:T(2,128)(2,1)} custom-call(bf16[512,768]{1,0:T(8,128)(2,1)} %bitcast.8, bf16[512,128]{1,0:T(8,128)(2,1)} %bitcast.10, f32[12,1,512]{2,1,0:T(1,128)} %bitcast.12), custom_call_target="tpu_custom_call" | custom-call | flops 100663296 | bytes 786432 | tf_op jit(solution)/shard_map/pallas_call | solution.py:199
  3.5 29.2 %all_to_all.20.in_ref = bf16[64,2,896]{2,1,0:T(2,128)(2,1)S(1)} all-to-all(bf16[64,2,896]{2,1,0:T(2,128)(2,1)} %shard_map.83), channel_id=1, replica_groups=mesh['tm'=64,'head'=4,'farm'=2] {'tm'}, dimensions={0} | all-to-all | bytes 458752 | tf_op jit(solution)/shard_map/all_to_all | solution.py:238
  32.7 1.3 %shard_map.84 = bf16[64,2,768]{2,1,0:T(2,128)(2,1)} custom-call(bf16[64,2,896]{2,1,0:T(2,128)(2,1)S(1)} %all_to_all.20.in_ref), custom_call_target="tpu_custom_call" | custom-call | flops 25165824 | bytes 393216 | tf_op jit(solution)/shard_map/pallas_call | solution.py:199
  34.0 5.8 %all-to-all-start.1 = ((bf16[64,2,768]{2,1,0:T(2,128)(2,1)}), bf16[64,2,768]{2,1,0:T(2,128)(2,1)S(1)}, u32[]{:S(2)}, u32[]{:S(2)}) async-start(bf16[64,2,768]{2,1,0:T(2,128)(2,1)} %shard_map.84), calls=%async_computation.1 | async-start | bytes 393216 | tf_op jit(solution)/shard_map/all_to_all | solution.py:263
  39.8 0.0 copy-done.7
  39.8 0.1 copy.9.skip_ref
  39.9 0.0 copy-done.3
  39.9 0.0 copy-start
  39.9 1.1 copy-done
  41.1 0.0 copy-start.1
  41.1 1.7 %copy-done.1 = bf16[768,1536]{1,0:T(8,128)(2,1)S(1)} copy-done((bf16[768,1536]{1,0:T(8,128)(2,1)S(1)}, bf16[768,1536]{1,0:T(8,128)(2,1)}, u32[]{:S(2)}) %copy-start.1) | copy-done | bytes 2359320
  42.7 0.0 copy-start.2
  42.7 0.9 copy-done.2
  43.6 0.0 copy-start.4
  43.6 0.9 copy-done.4
  44.5 3.9 %shard_map.82 = (bf16[512,896]{1,0:T(8,128)(2,1)S(1)}, bf16[768,1536]{1,0:T(8,128)(2,1)S(1)}) custom-call(bf16[512,768]{1,0:T(8,128)(2,1)S(1)} %bitcast.9, bf16[512,128]{1,0:T(8,128)(2,1)S(1)} %bitcast.11, bf16[512,128]{1,0:T(8,128)(2,1)S(1)} %bitcast.15, bf16[768,1536]{1,0:T(8,128)(2,1)S(1)} %copy-done.1, f32[12,1,512]{2,1,0:T(1,128)S(1)} %bitcast.13, ...), custom_call_target="tpu_custom_call" | custom-call | flops 301989888 | bytes 3145728 | tf_op jit(solution)/shard_map/pallas_call | solution.py:199
  48.5 3.2 %all-to-all-done.1.prior_ref = bf16[64,2,768]{2,1,0:T(2,128)(2,1)S(1)} async-done(((bf16[64,2,768]{2,1,0:T(2,128)(2,1)}), bf16[64,2,768]{2,1,0:T(2,128)(2,1)S(1)}, u32[]{:S(2)}, u32[]{:S(2)}) %all-to-all-start.1) | async-done | bytes 196640 | tf_op jit(solution)/shard_map/all_to_all | solution.py:263
  51.7 3.2 %shard_map.85 = bf16[4,128,1536]{2,1,0:T(8,128)(2,1)} custom-call(bf16[512,896]{1,0:T(8,128)(2,1)S(1)} %get-tuple-element.7.local_ref, f32[12,1,512]{2,1,0:T(1,128)S(1)} %bitcast.14, bf16[64,2,768]{2,1,0:T(2,128)(2,1)S(1)} %all-to-all-done.1.prior_ref, bf16[768,1536]{1,0:T(8,128)(2,1)S(1)} %get-tuple-element.8.w_ref), custom_call_target="tpu_custom_call" | custom-call | flops 1308622848 | bytes 4718592 | tf_op jit(solution)/shard_map/pallas_call | solution.py:199
  54.9 0.0 copy-start.5
  54.9 0.0 copy-start.6
  54.9 4.0 %all-to-all-start.2 = ((bf16[4,128,1536]{2,1,0:T(8,128)(2,1)}), bf16[4,128,1536]{2,1,0:T(8,128)(2,1)S(1)}, u32[]{:S(2)}, u32[]{:S(2)}) async-start(bf16[4,128,1536]{2,1,0:T(8,128)(2,1)} %shard_map.85), calls=%async_computation.2 | async-start | bytes 3145728 | tf_op jit(solution)/shard_map/all_to_all | solution.py:281
  58.9 0.0 copy-done.5
  58.9 0.1 copy.10.down_ref
  59.1 0.0 copy-done.6
  59.1 16.9 %all-to-all-done.2.parts_ref = bf16[4,128,1536]{2,1,0:T(8,128)(2,1)S(1)} async-done(((bf16[4,128,1536]{2,1,0:T(8,128)(2,1)}), bf16[4,128,1536]{2,1,0:T(8,128)(2,1)S(1)}, u32[]{:S(2)}, u32[]{:S(2)}) %all-to-all-start.2) | async-done | bytes 1572896 | tf_op jit(solution)/shard_map/all_to_all | solution.py:281
  76.0 0.7 shard_map.86
  76.7 39.1 %all_to_all.21 = bf16[128,2,1536]{2,1,0:T(2,128)(2,1)S(1)} all-to-all(bf16[128,2,1536]{2,1,0:T(2,128)(2,1)S(1)} %shard_map.86), channel_id=1, replica_groups=mesh['tm'=64,'head'=4,'farm'=2] {'tm','farm'}, dimensions={0} | all-to-all | bytes 1572864 | tf_op jit(solution)/shard_map/all_to_all | solution.py:294
  115.8 0.9 copy.12
  (1 shorter events, 0.0 us)
Async XLA Ops:
  0.0 39.9 %copy-start.3 = (f32[1,512,12]{1,0,2:T(1,128)S(1)}, f32[1,512,12]{1,0,2:T(1,128)}, u32[]{:S(2)}) copy-start(f32[1,512,12]{1,0,2:T(1,128)} %param.11) | copy-start | bytes 73732
  0.0 39.8 %copy-start.7 = (f32[12]{0:T(128)S(1)}, f32[12]{0:T(128)}, u32[]{:S(2)}) copy-start(f32[12]{0:T(128)} %param.12) | copy-start | bytes 148
  34.0 17.6 %all-to-all-start.1 = ((bf16[64,2,768]{2,1,0:T(2,128)(2,1)}), bf16[64,2,768]{2,1,0:T(2,128)(2,1)S(1)}, u32[]{:S(2)}, u32[]{:S(2)}) async-start(bf16[64,2,768]{2,1,0:T(2,128)(2,1)} %shard_map.84), calls=%async_computation.1 | async-start | bytes 393216 | tf_op jit(solution)/shard_map/all_to_all | solution.py:263
  39.9 1.1 copy-start
  41.1 1.7 %copy-start.1 = (bf16[768,1536]{1,0:T(8,128)(2,1)S(1)}, bf16[768,1536]{1,0:T(8,128)(2,1)}, u32[]{:S(2)}) copy-start(bf16[768,1536]{1,0:T(8,128)(2,1)} %w_hbm.1) | copy-start | bytes 7077892
  42.7 0.9 copy-start.2
  43.6 0.9 copy-start.4
  54.9 4.1 %copy-start.5 = (s32[1,128,1]{1,2,0:T(1,128)S(1)}, s32[1,128,1]{1,2,0:T(1,128)}, u32[]{:S(2)}) copy-start(s32[1,128,1]{1,2,0:T(1,128)} %param.15) | copy-start | bytes 1540
  54.9 4.2 %copy-start.6 = (f32[1536]{0:T(1024)S(1)}, f32[1536]{0:T(1024)}, u32[]{:S(2)}) copy-start(f32[1536]{0:T(1024)} %param.14) | copy-start | bytes 18436
  54.9 21.1 %all-to-all-start.2 = ((bf16[4,128,1536]{2,1,0:T(8,128)(2,1)}), bf16[4,128,1536]{2,1,0:T(8,128)(2,1)S(1)}, u32[]{:S(2)}, u32[]{:S(2)}) async-start(bf16[4,128,1536]{2,1,0:T(8,128)(2,1)} %shard_map.85), calls=%async_computation.2 | async-start | bytes 3145728 | tf_op jit(solution)/shard_map/all_to_all | solution.py:281

commit v3 on v2

--- a/solution.py
+++ b/solution.py
@@ -8,6 +8,7 @@
 
 SPAN = 64
 LANES = 128
+ROWS = 16
 F32 = jnp.float32
 BF16 = jnp.bfloat16
 FIRST = (((0,), (0,)), ((), ()))
@@ -58,22 +59,31 @@
     return copies
 
 
-def state_kernel(x_hbm, b_hbm, decay_ref, out_ref, x_ref, b_ref, wx_ref, state_ref, sems):
-    copies = fetch(((x_hbm, x_ref), (b_hbm, b_ref)), sems)
+def state_kernel(
+    x_hbm, b_hbm, decay_hbm, out_ref, x_ref, b_ref, decay_ref, wx_ref, state_ref, sems
+):
     heads, _, steps = decay_ref.shape
     width = x_ref.shape[1]
+    blocks = [slice(k * LANES, (k + 1) * LANES) for k in range(steps // LANES)]
+    first, *others, last = fetch(
+        [(decay_hbm, decay_ref)]
+        + [(x_hbm.at[rows, :], x_ref.at[rows, :]) for rows in blocks]
+        + [(b_hbm, b_ref)],
+        sems,
+    )
     matrix = head_spread(heads, width, width // heads)
     later = jnp.zeros((heads, 1), F32)
-    weights = [None] * (steps // LANES)
-    for k in reversed(range(steps // LANES)):
-        values = decay_ref[:, 0, k * LANES : (k + 1) * LANES]
+    weights = [None] * len(blocks)
+    first.wait()
+    for k in reversed(range(len(blocks))):
+        values = decay_ref[:, 0, blocks[k]]
         weights[k] = jnp.exp(running(values, lambda s, t: s > t) + later)
         later = later + jnp.sum(values, axis=1, keepdims=True)
-    for copy in copies:
+    for rows, weight, copy in zip(blocks, weights, others):
+        weight = spread(weight, matrix)
         copy.wait()
-    for k, weight in enumerate(weights):
-        rows = slice(k * LANES, (k + 1) * LANES)
-        wx_ref[rows, :] = (x_ref[rows, :].astype(F32) * spread(weight, matrix)).astype(BF16)
+        wx_ref[rows, :] = (x_ref[rows, :].astype(F32) * weight).astype(BF16)
+    last.wait()
     state_ref[...] = lax.dot_general(b_ref[...], wx_ref[...], FIRST, preferred_element_type=F32)
     parcels, depth, _ = out_ref.shape
     unit = head_spread(heads, LANES, 1)
@@ -100,10 +110,7 @@
         carried = factor * carried + in_ref[k, :, :width].astype(F32)
 
 
-def local_kernel(
-    x_ref, b_ref, c_ref, w_hbm, decay_ref, skip_ref, out_ref, w_ref, state_ref, sems
-):
-    copies = fetch(((w_hbm, w_ref),), sems)
+def local_kernel(x_ref, b_ref, c_ref, decay_ref, skip_ref, out_ref, state_ref):
     heads, _, steps = decay_ref.shape
     width = x_ref.shape[1]
     matrix = head_spread(heads, width, width // heads)
@@ -112,8 +119,15 @@
     causal = row >= column
     first = lax.broadcasted_iota(jnp.int32, (heads, LANES), 1) < SPAN
     skip = spread(jnp.broadcast_to(skip_ref[...], (heads, LANES)), matrix)[0:1]
+    before = jnp.zeros((heads, 1), F32)
     for k in range(steps // LANES):
-        values = decay_ref[:, 0, k * LANES : (k + 1) * LANES]
+        lanes = slice(k * LANES, (k + 1) * LANES)
+        values = decay_ref[:, 0, lanes]
+        reach = jnp.exp(running(values, lambda s, t: s <= t) + before)
+        reach = jnp.concatenate([reach, jnp.zeros((ROWS - heads, LANES), F32)], axis=0)
+        for part, half in enumerate(split2(reach)):
+            out_ref[steps + part * ROWS : steps + (part + 1) * ROWS, lanes] = half
+        before = before + jnp.sum(values, axis=1, keepdims=True)
         local = running(values, lambda s, t: (s <= t) & ((s < SPAN) == (t < SPAN)))
         middle = 0.5 * jnp.where(
             first, local[:, SPAN - 1 : SPAN], local[:, LANES - 1 : LANES]
@@ -141,66 +155,70 @@
                 state_ref[...] = half * (half * state + update)
             out_ref[rows, :width] = (up * y + skip * x).astype(BF16)
             out_ref[rows, width:] = c
-    for copy in copies:
-        copy.wait()
-
-
-def project_kernel(local_ref, decay_ref, prior_ref, w_ref, out_hbm, mixed_ref, send_ref, sems):
-    heads, _, steps = decay_ref.shape
+
+
+def early_kernel(
+    capacity, w_hbm, across_ref, down_ref, gain_ref, w_ref, target_ref, gain_out_ref, sems
+):
+    (copy,) = fetch(((w_hbm, w_ref),), sems)
+    across = across_ref[...]
+    rows = across.shape[1]
+    earlier = lax.broadcasted_iota(jnp.int32, (rows, rows), 0) < lax.broadcasted_iota(
+        jnp.int32, (rows, rows), 1
+    )
+    same = (down_ref[...] == across) & earlier
+    slot = jnp.sum(same.astype(jnp.int32), axis=0, keepdims=True)
+    target_ref[...] = across * capacity + slot
+    gain_out_ref[...] = gain_ref[...]
+    copy.wait()
+
+
+def project_kernel(heads, local_ref, prior_ref, w_ref, out_ref, mixed_ref):
+    steps = mixed_ref.shape[0]
     parcels, depth, width = prior_ref.shape
-    pieces, block, width_out = send_ref.shape
+    pieces, block, width_out = out_ref.shape
     state = prior_ref[...].reshape(parcels * depth, width)
-    matrix = head_spread(heads, width, width // heads)
-    before = jnp.zeros((heads, 1), F32)
-    reaches = []
+    matrix = head_spread(ROWS, width, width // heads)
     for k in range(steps // LANES):
-        values = decay_ref[:, 0, k * LANES : (k + 1) * LANES]
-        reaches.append(jnp.exp(running(values, lambda s, t: s <= t) + before))
-        before = before + jnp.sum(values, axis=1, keepdims=True)
-    for k, reach in enumerate(reaches):
         rows = slice(k * LANES, (k + 1) * LANES)
-        carried = spread(reach, matrix) * mm(local_ref[rows, width:], state)
+        reach = sum(
+            lax.dot_general(
+                local_ref[steps + part * ROWS : steps + (part + 1) * ROWS, rows],
+                matrix,
+                FIRST,
+                preferred_element_type=F32,
+            )
+            for part in range(2)
+        )
+        carried = reach * mm(local_ref[rows, width:], state)
         mixed_ref[rows, :] = (local_ref[rows, :width].astype(F32) + carried).astype(BF16)
     tile = 256
-    sends = []
     for j in range(width_out // tile):
         columns = slice(j * tile, (j + 1) * tile)
         product = mm(mixed_ref[...], w_ref[:, columns]).astype(BF16)
         for d in range(pieces):
-            send_ref[d, :, columns] = product[d * block : (d + 1) * block, :]
-        sends += fetch(
-            ((send_ref.at[:, :, columns], out_hbm.at[:, :, columns]),), sems.at[pl.ds(j, 1)]
-        )
-    for send in sends:
-        send.wait()
-
-
-def regroup_kernel(across_ref, down_ref, gain_ref, parts_ref, out_ref):
+            out_ref[d, :, columns] = product[d * block : (d + 1) * block, :]
+
+
+def regroup_kernel(target_ref, gain_ref, parts_ref, out_ref):
     owners, capacity, width = out_ref.shape
     pieces, rows, _ = parts_ref.shape
     projected = sum(parts_ref[k].astype(F32) for k in range(pieces))
     scale = lax.rsqrt(jnp.mean(projected * projected, axis=1, keepdims=True) + 1e-06)
     normed = (projected * scale * gain_ref[...]).astype(BF16)
-    across = across_ref[...]
-    earlier = lax.broadcasted_iota(jnp.int32, (rows, rows), 0) < lax.broadcasted_iota(
-        jnp.int32, (rows, rows), 1
-    )
-    same = (down_ref[...] == across) & earlier
-    slot = jnp.sum(same.astype(jnp.int32), axis=0, keepdims=True)
-    target = across * capacity + slot
     place = lax.broadcasted_iota(jnp.int32, (owners * capacity, rows), 0)
-    select = (place == target).astype(BF16)
+    select = (place == target_ref[...]).astype(BF16)
     out_ref[...] = mm(select, normed).astype(BF16).reshape(owners, capacity, width)
 
 
-def call(kernel, outs, scratch, flops, moved, limit, *args, far=(), out_far=False):
+def call(kernel, outs, scratch, flops, moved, limit, *args, far=()):
     vmem = pl.BlockSpec(memory_space=pltpu.VMEM)
     hbm = pl.BlockSpec(memory_space=pltpu.HBM)
     return pl.pallas_call(
         kernel,
         out_shape=outs,
         in_specs=[hbm if k in far else vmem for k in range(len(args))],
-        out_specs=jax.tree.map(lambda _: hbm if out_far else vmem, outs),
+        out_specs=jax.tree.map(lambda _: vmem, outs),
         scratch_shapes=scratch,
         cost_estimate=pl.CostEstimate(flops=flops, bytes_accessed=moved, transcendentals=0),
         compiler_params=pltpu.CompilerParams(vmem_limit_bytes=int(limit * 1024 * 1024)),
@@ -226,30 +244,49 @@
     parcel = call(
         state_kernel,
         spec((times, depth, width + LANES), BF16),
-        [wide, narrow, wide, state, pltpu.SemaphoreType.DMA((2,))],
+        [
+            wide,
+            narrow,
+            pltpu.VMEM(decays.shape, F32),
+            wide,
+            state,
+            pltpu.SemaphoreType.DMA((2 + steps // LANES,)),
+        ],
         2 * steps * width * state_dim,
         2 * steps * width,
         63.4,
         x,
         b,
         decays,
-        far=(0, 1),
+        far=(0, 1, 2),
     )
     parcel = lax.all_to_all(parcel, "tm", split_axis=0, concat_axis=0, tiled=True)
-    local, weights = call(
+    local = call(
         local_kernel,
-        (spec((steps, width + state_dim), BF16), spec(w_out.shape, BF16)),
-        [state, pltpu.SemaphoreType.DMA((1,))],
+        spec((steps + 2 * ROWS, width + state_dim), BF16),
+        [state],
         6 * steps * width * state_dim,
         8 * steps * width,
         24,
         x,
         b,
         c,
-        w_out,
         decays,
         skip_gain[:, None],
-        far=(3,),
+    )
+    parcel, local, w_late = lax.optimization_barrier((parcel, local, w_out))
+    weights, target, gain = call(
+        functools.partial(early_kernel, capacity),
+        (spec(w_out.shape, BF16), spec((1, block), jnp.int32), spec((1, width_out), F32)),
+        [pltpu.SemaphoreType.DMA((1,))],
+        0,
+        4 * width * width_out,
+        16,
+        w_late,
+        owner_ids[0, :, 0][None, :],
+        owner_ids[0],
+        norm_gain[None, :],
+        far=(0,),
     )
     prior = call(
         functools.partial(prefix_kernel, heads),
@@ -262,21 +299,15 @@
     )
     prior = lax.all_to_all(prior, "tm", split_axis=0, concat_axis=0, tiled=True)
     parts = call(
-        project_kernel,
+        functools.partial(project_kernel, heads),
         spec((pieces, block, width_out), BF16),
-        [
-            wide,
-            pltpu.VMEM((pieces, block, width_out), BF16),
-            pltpu.SemaphoreType.DMA((width_out // 256,)),
-        ],
+        [wide],
         2 * steps * width * (width_out + state_dim),
         2 * steps * (width + width_out) + 2 * width * width_out,
         24,
         local,
-        decays,
         prior,
         weights,
-        out_far=True,
     )
     parts = lax.all_to_all(parts, "head", split_axis=0, concat_axis=0, tiled=True)
     outgoing = call(
@@ -286,9 +317,8 @@
         2 * owners * capacity * block * width_out,
         12 * block * width_out,
         16,
-        owner_ids[0, :, 0][None, :],
-        owner_ids[0],
-        norm_gain[None, :],
+        target,
+        gain,
         parts,
     )
     result = lax.all_to_all(outgoing, ("tm", "farm"), split_axis=0, concat_axis=0, tiled=True)

time: 117 us -> 114 us (0.974)
  starting transfers between devices: 9.82 us -> 25.6 us
  blocking collectives: 68.3 us -> 55.3 us
  waiting for transfers between devices: 20.1 us -> 12.1 us
  local copies, waits for them, and re-layouts: 5.72 us -> 8.56 us
    all_to_all x1, waiting for transfers between devices: 16.9 us -> 3.71 us  [shards(): lax.all_to_all(parcel, 'tm', split_axis=0, concat_axis=0, tiled=True)]
    all_to_all x1, starting transfers between devices: 4.04 us -> 17.1 us  [shards(): lax.all_to_all(parcel, 'tm', split_axis=0, concat_axis=0, tiled=True)]
    all_to_all x1, blocking collectives: 29.2 us -> 21.5 us  [shards(): lax.all_to_all(parts, 'head', split_axis=0, concat_axis=0, tiled=True)]
    all_to_all x1, blocking collectives: 39.1 us -> 33.8 us  [shards(): lax.all_to_all(outgoing, ('tm', 'farm'), split_axis=0, concat_axis=0, til...]
    all_to_all x1, waiting for transfers between devices: 3.21 us -> 8.39 us  [shards(): prior = lax.all_to_all(prior, 'tm', split_axis=0, concat_axis=0, tiled=True)]
    all_to_all x1, starting transfers between devices: 5.78 us -> 8.43 us  [shards(): prior = lax.all_to_all(prior, 'tm', split_axis=0, concat_axis=0, tiled=True)]
    unnamed x17, local copies, waits for them, and re-layouts: 5.51 us -> 7.07 us
    pallas_call x5 -> x6, Pallas kernels: 12.6 us -> 11.7 us  [call(): pl.pallas_call(kernel, out_shape=outs, in_specs=[hbm if k in far else vme...]
  transfers between devices with their start and end apart: 2 -> 2, of which waited for: 2 -> 2; matrix products, arithmetic and copies ran while one was open for 0% -> 1% of each run, Pallas kernels for 3% -> 4%
where the time goes in v3:
time: 114 us; the launch traced here: 113 us
  blocking collectives  55.3 us (49%)
  starting transfers between devices  25.6 us (22%)
  waiting for transfers between devices  12.1 us (11%)
  Pallas kernels  11.7 us (10%)
  local copies, waits for them, and re-layouts  8.56 us (8%)
    all_to_all x1, blocking collectives, shards(): lax.all_to_all(outgoing, ('tm', 'farm'), split_axis=0, concat_axis=0, til...  33.8 us
    all_to_all x1, blocking collectives, shards(): lax.all_to_all(parts, 'head', split_axis=0, concat_axis=0, tiled=True)  21.5 us
    all_to_all x1, starting transfers between devices, shards(): lax.all_to_all(parcel, 'tm', split_axis=0, concat_axis=0, tiled=True)  17.1 us
    pallas_call x6, Pallas kernels, call(): pl.pallas_call(kernel, out_shape=outs, in_specs=[hbm if k in far else vme...  11.7 us
    all_to_all x1, starting transfers between devices, shards(): prior = lax.all_to_all(prior, 'tm', split_axis=0, concat_axis=0, tiled=True)  8.43 us
    all_to_all x1, waiting for transfers between devices, shards(): prior = lax.all_to_all(prior, 'tm', split_axis=0, concat_axis=0, tiled=True)  8.39 us
    unnamed x17, local copies, waits for them, and re-layouts  7.07 us
    all_to_all x1, waiting for transfers between devices, shards(): lax.all_to_all(parcel, 'tm', split_axis=0, concat_axis=0, tiled=True)  3.71 us
  transfers between devices with their start and end apart: 2, of which 2 were waited for; matrix products, arithmetic and copies ran while one was open for 1% of the time, Pallas kernels for 4%

profile of v3, /device:TPU:1, one launch (start us, length us, event | category | flops | bytes accessed | tf_op | source)
XLA Modules:
  0.0 113.3 jit_solution(10293637549196888002)
XLA Ops:
  0.0 0.0 copy-start.7
  0.0 0.0 copy-start.6
  0.0 3.4 %shard_map.82 = bf16[64,2,896]{2,1,0:T(2,128)(2,1)} custom-call(bf16[512,768]{1,0:T(8,128)(2,1)} %bitcast.8, bf16[512,128]{1,0:T(8,128)(2,1)} %bitcast.10, f32[12,1,512]{2,1,0:T(1,128)} %bitcast.13), custom_call_target="tpu_custom_call" | custom-call | flops 100663296 | bytes 786432 | tf_op jit(solution)/shard_map/pallas_call | solution.py:217
  3.4 17.1 %all-to-all-start = ((bf16[64,2,896]{2,1,0:T(2,128)(2,1)}), bf16[64,2,896]{2,1,0:T(2,128)(2,1)S(1)}, u32[]{:S(2)}, u32[]{:S(2)}) async-start(bf16[64,2,896]{2,1,0:T(2,128)(2,1)} %shard_map.82), calls=%async_computation | async-start | bytes 458752 | tf_op jit(solution)/shard_map/all_to_all | solution.py:263
  20.6 0.7 copy.9.skip_ref
  21.3 0.0 copy-start
  21.3 1.1 copy-done
  22.5 0.0 copy-start.2
  22.5 0.9 copy-done.2
  23.4 0.0 copy-start.4
  23.4 0.9 copy-done.4
  24.3 0.0 copy-start.5
  24.3 0.7 copy-done.5
  25.0 3.9 %shard_map.83.local_ref = bf16[544,896]{1,0:T(8,128)(2,1)S(1)} custom-call(bf16[512,768]{1,0:T(8,128)(2,1)S(1)} %bitcast.9, bf16[512,128]{1,0:T(8,128)(2,1)S(1)} %bitcast.11, bf16[512,128]{1,0:T(8,128)(2,1)S(1)} %bitcast.12, f32[12,1,512]{2,1,0:T(1,128)S(1)} %bitcast.14, f32[12,1]{1,0:T(8,128)S(1)} %copy.9.skip_ref), custom_call_target="tpu_custom_call" | custom-call | flops 301989888 | bytes 3145728 | tf_op jit(solution)/shard_map/pallas_call | solution.py:217
  29.0 3.7 %all-to-all-done.in_ref = bf16[64,2,896]{2,1,0:T(2,128)(2,1)S(1)} async-done(((bf16[64,2,896]{2,1,0:T(2,128)(2,1)}), bf16[64,2,896]{2,1,0:T(2,128)(2,1)S(1)}, u32[]{:S(2)}, u32[]{:S(2)}) %all-to-all-start) | async-done | bytes 229408 | tf_op jit(solution)/shard_map/all_to_all | solution.py:263
  32.7 1.3 %shard_map.85 = bf16[64,2,768]{2,1,0:T(2,128)(2,1)} custom-call(bf16[64,2,896]{2,1,0:T(2,128)(2,1)S(1)} %all-to-all-done.in_ref), custom_call_target="tpu_custom_call" | custom-call | flops 25165824 | bytes 393216 | tf_op jit(solution)/shard_map/pallas_call | solution.py:217
  34.0 8.4 %all-to-all-start.1 = ((bf16[64,2,768]{2,1,0:T(2,128)(2,1)}), bf16[64,2,768]{2,1,0:T(2,128)(2,1)S(1)}, u32[]{:S(2)}, u32[]{:S(2)}) async-start(bf16[64,2,768]{2,1,0:T(2,128)(2,1)} %shard_map.85), calls=%async_computation.1 | async-start | bytes 393216 | tf_op jit(solution)/shard_map/all_to_all | solution.py:300
  42.5 0.0 copy-done.7
  42.5 0.0 copy-done.6
  42.5 0.7 copy.10.down_ref
  43.2 0.0 copy-start.1
  43.2 1.7 %copy-done.1 = bf16[768,1536]{1,0:T(8,128)(2,1)S(1)} copy-done((bf16[768,1536]{1,0:T(8,128)(2,1)S(1)}, bf16[768,1536]{1,0:T(8,128)(2,1)}, u32[]{:S(2)}) %copy-start.1) | copy-done | bytes 2359320
  44.9 0.0 copy-start.3
  44.9 0.8 copy-done.3
  45.7 0.3 shard_map.84
  46.0 8.4 %all-to-all-done.1.prior_ref = bf16[64,2,768]{2,1,0:T(2,128)(2,1)S(1)} async-done(((bf16[64,2,768]{2,1,0:T(2,128)(2,1)}), bf16[64,2,768]{2,1,0:T(2,128)(2,1)S(1)}, u32[]{:S(2)}, u32[]{:S(2)}) %all-to-all-start.1) | async-done | bytes 196640 | tf_op jit(solution)/shard_map/all_to_all | solution.py:300
  54.4 2.0 %shard_map.86 = bf16[4,128,1536]{2,1,0:T(8,128)(2,1)S(1)} custom-call(bf16[544,896]{1,0:T(8,128)(2,1)S(1)} %shard_map.83.local_ref, bf16[64,2,768]{2,1,0:T(2,128)(2,1)S(1)} %all-to-all-done.1.prior_ref, bf16[768,1536]{1,0:T(8,128)(2,1)S(1)} %get-tuple-element.16.w_ref), custom_call_target="tpu_custom_call" | custom-call | flops 1308622848 | bytes 4718592 | tf_op jit(solution)/shard_map/pallas_call | solution.py:217
  56.4 21.5 %all_to_all.20.parts_ref = bf16[4,128,1536]{2,1,0:T(8,128)(2,1)S(1)} all-to-all(bf16[4,128,1536]{2,1,0:T(8,128)(2,1)S(1)} %shard_map.86), channel_id=1, replica_groups=mesh['tm'=64,'head'=4,'farm'=2] {'head'}, dimensions={0} | all-to-all | bytes 3145728 | tf_op jit(solution)/shard_map/all_to_all | solution.py:312
  77.9 0.7 shard_map.87
  78.6 33.8 %all_to_all.21 = bf16[128,2,1536]{2,1,0:T(2,128)(2,1)S(1)} all-to-all(bf16[128,2,1536]{2,1,0:T(2,128)(2,1)S(1)} %shard_map.87), channel_id=1, replica_groups=mesh['tm'=64,'head'=4,'farm'=2] {'tm','farm'}, dimensions={0} | all-to-all | bytes 1572864 | tf_op jit(solution)/shard_map/all_to_all | solution.py:324
  112.4 0.9 copy.12
  (1 shorter events, 0.0 us)
Async XLA Ops:
  0.0 42.5 %copy-start.7 = (f32[1536]{0:T(1024)S(1)}, f32[1536]{0:T(1024)}, u32[]{:S(2)}) copy-start(f32[1536]{0:T(1024)} %param.14) | copy-start | bytes 18436
  0.0 42.5 %copy-start.6 = (s32[1,128,1]{1,2,0:T(1,128)S(1)}, s32[1,128,1]{1,2,0:T(1,128)}, u32[]{:S(2)}) copy-start(s32[1,128,1]{1,2,0:T(1,128)} %param.15) | copy-start | bytes 1540
  3.4 29.2 %all-to-all-start = ((bf16[64,2,896]{2,1,0:T(2,128)(2,1)}), bf16[64,2,896]{2,1,0:T(2,128)(2,1)S(1)}, u32[]{:S(2)}, u32[]{:S(2)}) async-start(bf16[64,2,896]{2,1,0:T(2,128)(2,1)} %shard_map.82), calls=%async_computation | async-start | bytes 458752 | tf_op jit(solution)/shard_map/all_to_all | solution.py:263
  21.3 1.1 %copy-start = (bf16[1,512,768]{2,1,0:T(8,128)(2,1)S(1)}, bf16[1,512,768]{2,1,0:T(8,128)(2,1)}, u32[]{:S(2)}) copy-start(bf16[1,512,768]{2,1,0:T(8,128)(2,1)} %param.8) | copy-start | bytes 2359300
  22.5 0.9 copy-start.2
  23.4 0.9 copy-start.4
  24.3 0.7 copy-start.5
  34.0 20.4 %all-to-all-start.1 = ((bf16[64,2,768]{2,1,0:T(2,128)(2,1)}), bf16[64,2,768]{2,1,0:T(2,128)(2,1)S(1)}, u32[]{:S(2)}, u32[]{:S(2)}) async-start(bf16[64,2,768]{2,1,0:T(2,128)(2,1)} %shard_map.85), calls=%async_computation.1 | async-start | bytes 393216 | tf_op jit(solution)/shard_map/all_to_all | solution.py:300
  43.2 1.7 %copy-start.1 = (bf16[768,1536]{1,0:T(8,128)(2,1)S(1)}, bf16[768,1536]{1,0:T(8,128)(2,1)}, u32[]{:S(2)}) copy-start(bf16[768,1536]{1,0:T(8,128)(2,1)} %w_hbm) | copy-start | bytes 7077892
  44.9 0.8 copy-start.3

commit v4 on v3

--- a/solution.py
+++ b/solution.py
@@ -110,7 +110,23 @@
         carried = factor * carried + in_ref[k, :, :width].astype(F32)
 
 
-def local_kernel(x_ref, b_ref, c_ref, decay_ref, skip_ref, out_ref, state_ref):
+def local_kernel(
+    x_hbm,
+    b_hbm,
+    c_hbm,
+    decay_hbm,
+    skip_ref,
+    out_ref,
+    x_ref,
+    b_ref,
+    c_ref,
+    decay_ref,
+    state_ref,
+    sems,
+):
+    copies = fetch(
+        ((decay_hbm, decay_ref), (x_hbm, x_ref), (b_hbm, b_ref), (c_hbm, c_ref)), sems
+    )
     heads, _, steps = decay_ref.shape
     width = x_ref.shape[1]
     matrix = head_spread(heads, width, width // heads)
@@ -118,7 +134,9 @@
     column = lax.broadcasted_iota(jnp.int32, (SPAN, SPAN), 1)
     causal = row >= column
     first = lax.broadcasted_iota(jnp.int32, (heads, LANES), 1) < SPAN
-    skip = spread(jnp.broadcast_to(skip_ref[...], (heads, LANES)), matrix)[0:1]
+    skip = sum(mm(part, matrix) for part in split3(skip_ref[...]))
+    for copy in copies:
+        copy.wait()
     before = jnp.zeros((heads, 1), F32)
     for k in range(steps // LANES):
         lanes = slice(k * LANES, (k + 1) * LANES)
@@ -158,19 +176,31 @@
 
 
 def early_kernel(
-    capacity, w_hbm, across_ref, down_ref, gain_ref, w_ref, target_ref, gain_out_ref, sems
+    owners,
+    capacity,
+    w_hbm,
+    local_hbm,
+    routes_ref,
+    gain_ref,
+    w_ref,
+    local_ref,
+    target_ref,
+    gain_out_ref,
+    sems,
 ):
-    (copy,) = fetch(((w_hbm, w_ref),), sems)
-    across = across_ref[...]
-    rows = across.shape[1]
-    earlier = lax.broadcasted_iota(jnp.int32, (rows, rows), 0) < lax.broadcasted_iota(
+    copies = fetch(((w_hbm, w_ref), (local_hbm, local_ref)), sems)
+    routes = routes_ref[...]
+    rows = routes.shape[1]
+    named = lax.broadcasted_iota(jnp.int32, (owners, rows), 0) == routes
+    before = lax.broadcasted_iota(jnp.int32, (rows, rows), 0) < lax.broadcasted_iota(
         jnp.int32, (rows, rows), 1
     )
-    same = (down_ref[...] == across) & earlier
-    slot = jnp.sum(same.astype(jnp.int32), axis=0, keepdims=True)
-    target_ref[...] = across * capacity + slot
+    earlier = mm(named.astype(BF16), before.astype(BF16))
+    slot = jnp.sum(jnp.where(named, earlier, 0.0), axis=0, keepdims=True)
+    target_ref[...] = routes * capacity + slot.astype(jnp.int32)
     gain_out_ref[...] = gain_ref[...]
-    copy.wait()
+    for copy in copies:
+        copy.wait()
 
 
 def project_kernel(heads, local_ref, prior_ref, w_ref, out_ref, mixed_ref):
@@ -264,29 +294,42 @@
     local = call(
         local_kernel,
         spec((steps + 2 * ROWS, width + state_dim), BF16),
-        [state],
+        [
+            wide,
+            narrow,
+            narrow,
+            pltpu.VMEM(decays.shape, F32),
+            state,
+            pltpu.SemaphoreType.DMA((4,)),
+        ],
         6 * steps * width * state_dim,
         8 * steps * width,
-        24,
+        61.5,
         x,
         b,
         c,
         decays,
-        skip_gain[:, None],
+        skip_gain[None, :],
+        far=(0, 1, 2, 3),
     )
     parcel, local, w_late = lax.optimization_barrier((parcel, local, w_out))
-    weights, target, gain = call(
-        functools.partial(early_kernel, capacity),
-        (spec(w_out.shape, BF16), spec((1, block), jnp.int32), spec((1, width_out), F32)),
-        [pltpu.SemaphoreType.DMA((1,))],
-        0,
+    weights, local, target, gain = call(
+        functools.partial(early_kernel, owners, capacity),
+        (
+            spec(w_out.shape, BF16),
+            spec(local.shape, BF16),
+            spec((1, block), jnp.int32),
+            spec((1, width_out), F32),
+        ),
+        [pltpu.SemaphoreType.DMA((2,))],
+        2 * owners * block * block,
         4 * width * width_out,
         16,
         w_late,
+        local,
         owner_ids[0, :, 0][None, :],
-        owner_ids[0],
         norm_gain[None, :],
-        far=(0,),
+        far=(0, 1),
     )
     prior = call(
         functools.partial(prefix_kernel, heads),

time: 114 us -> 112 us (0.982)
  local copies, waits for them, and re-layouts: 8.56 us -> 3.75 us
  Pallas kernels: 11.7 us -> 14.6 us
  starting transfers between devices: 25.6 us -> 23.7 us
  waiting for transfers between devices: 12.1 us -> 13.9 us
    unnamed x17 -> x9, local copies, waits for them, and re-layouts: 7.07 us -> 3.74 us
    pallas_call x6, Pallas kernels: 11.7 us -> 14.6 us  [call(): pl.pallas_call(kernel, out_shape=outs, in_specs=[hbm if k in far else vme...]
    all_to_all x1, waiting for transfers between devices: 3.71 us -> 5.55 us  [shards(): lax.all_to_all(parcel, 'tm', split_axis=0, concat_axis=0, tiled=True)]
    all_to_all x1, starting transfers between devices: 8.43 us -> 6.6 us  [shards(): prior = lax.all_to_all(prior, 'tm', split_axis=0, concat_axis=0, tiled=True)]
  transfers between devices with their start and end apart: 2 -> 2, of which waited for: 2 -> 2; matrix products, arithmetic and copies ran while one was open for 1% -> 0% of each run, Pallas kernels for 4% -> 6%
where the time goes in v4:
time: 112 us; the launch traced here: 111 us
  blocking collectives  55.4 us (49%)
  starting transfers between devices  23.7 us (21%)
  Pallas kernels  14.6 us (13%)
  waiting for transfers between devices  13.9 us (12%)
  local copies, waits for them, and re-layouts  3.75 us (3%)
    all_to_all x1, blocking collectives, shards(): lax.all_to_all(outgoing, ('tm', 'farm'), split_axis=0, concat_axis=0, til...  33.9 us
    all_to_all x1, blocking collectives, shards(): lax.all_to_all(parts, 'head', split_axis=0, concat_axis=0, tiled=True)  21.5 us
    all_to_all x1, starting transfers between devices, shards(): lax.all_to_all(parcel, 'tm', split_axis=0, concat_axis=0, tiled=True)  17.1 us
    pallas_call x6, Pallas kernels, call(): pl.pallas_call(kernel, out_shape=outs, in_specs=[hbm if k in far else vme...  14.6 us
    all_to_all x1, waiting for transfers between devices, shards(): prior = lax.all_to_all(prior, 'tm', split_axis=0, concat_axis=0, tiled=True)  8.34 us
    all_to_all x1, starting transfers between devices, shards(): prior = lax.all_to_all(prior, 'tm', split_axis=0, concat_axis=0, tiled=True)  6.6 us
    all_to_all x1, waiting for transfers between devices, shards(): lax.all_to_all(parcel, 'tm', split_axis=0, concat_axis=0, tiled=True)  5.55 us
    unnamed x9, local copies, waits for them, and re-layouts  3.74 us
  transfers between devices with their start and end apart: 2, of which 2 were waited for; matrix products, arithmetic and copies ran while one was open for 0% of the time, Pallas kernels for 6%

profile of v4, /device:TPU:1, one launch (start us, length us, event | category | flops | bytes accessed | tf_op | source)
XLA Modules:
  0.0 111.5 jit_solution(5259663360644491759)
XLA Ops:
  0.0 0.0 copy-start.3
  0.0 0.0 copy-start.2
  0.0 3.4 %shard_map.82 = bf16[64,2,896]{2,1,0:T(2,128)(2,1)} custom-call(bf16[512,768]{1,0:T(8,128)(2,1)} %bitcast.8, bf16[512,128]{1,0:T(8,128)(2,1)} %bitcast.11, f32[12,1,512]{2,1,0:T(1,128)} %bitcast.14), custom_call_target="tpu_custom_call" | custom-call | flops 100663296 | bytes 786432 | tf_op jit(solution)/shard_map/pallas_call | solution.py:247
  3.4 17.1 %all-to-all-start = ((bf16[64,2,896]{2,1,0:T(2,128)(2,1)}), bf16[64,2,896]{2,1,0:T(2,128)(2,1)S(1)}, u32[]{:S(2)}, u32[]{:S(2)}) async-start(bf16[64,2,896]{2,1,0:T(2,128)(2,1)} %shard_map.82), calls=%async_computation | async-start | bytes 458752 | tf_op jit(solution)/shard_map/all_to_all | solution.py:293
  20.6 6.5 %shard_map.83.local_hbm = bf16[544,896]{1,0:T(8,128)(2,1)} custom-call(bf16[512,768]{1,0:T(8,128)(2,1)} %bitcast.9, bf16[512,128]{1,0:T(8,128)(2,1)} %bitcast.12, bf16[512,128]{1,0:T(8,128)(2,1)} %bitcast.13, f32[12,1,512]{2,1,0:T(1,128)} %bitcast.15, f32[1,12]{1,0:T(1,128)} %bitcast.16), custom_call_target="tpu_custom_call" | custom-call | flops 301989888 | bytes 3145728 | tf_op jit(solution)/shard_map/pallas_call | solution.py:247
  27.1 5.6 %all-to-all-done.in_ref = bf16[64,2,896]{2,1,0:T(2,128)(2,1)S(1)} async-done(((bf16[64,2,896]{2,1,0:T(2,128)(2,1)}), bf16[64,2,896]{2,1,0:T(2,128)(2,1)S(1)}, u32[]{:S(2)}, u32[]{:S(2)}) %all-to-all-start) | async-done | bytes 229408 | tf_op jit(solution)/shard_map/all_to_all | solution.py:293
  32.7 1.3 %shard_map.85 = bf16[64,2,768]{2,1,0:T(2,128)(2,1)} custom-call(bf16[64,2,896]{2,1,0:T(2,128)(2,1)S(1)} %all-to-all-done.in_ref), custom_call_target="tpu_custom_call" | custom-call | flops 25165824 | bytes 393216 | tf_op jit(solution)/shard_map/pallas_call | solution.py:247
  34.0 6.6 %all-to-all-start.1 = ((bf16[64,2,768]{2,1,0:T(2,128)(2,1)}), bf16[64,2,768]{2,1,0:T(2,128)(2,1)S(1)}, u32[]{:S(2)}, u32[]{:S(2)}) async-start(bf16[64,2,768]{2,1,0:T(2,128)(2,1)} %shard_map.85), calls=%async_computation.1 | async-start | bytes 393216 | tf_op jit(solution)/shard_map/all_to_all | solution.py:343
  40.6 0.0 copy-done.3
  40.6 0.0 copy-done.2
  40.7 0.0 copy-start
  40.7 1.2 %copy-done = bf16[544,896]{1,0:T(8,128)(2,1)S(1)} copy-done((bf16[544,896]{1,0:T(8,128)(2,1)S(1)}, bf16[544,896]{1,0:T(8,128)(2,1)}, u32[]{:S(2)}) %copy-start) | copy-done | bytes 974872
  41.9 0.0 copy-start.1
  41.9 1.7 %copy-done.1 = bf16[768,1536]{1,0:T(8,128)(2,1)S(1)} copy-done((bf16[768,1536]{1,0:T(8,128)(2,1)S(1)}, bf16[768,1536]{1,0:T(8,128)(2,1)}, u32[]{:S(2)}) %copy-start.1) | copy-done | bytes 2359320
  43.5 0.6 shard_map.84
  44.2 8.3 %all-to-all-done.1.prior_ref = bf16[64,2,768]{2,1,0:T(2,128)(2,1)S(1)} async-done(((bf16[64,2,768]{2,1,0:T(2,128)(2,1)}), bf16[64,2,768]{2,1,0:T(2,128)(2,1)S(1)}, u32[]{:S(2)}, u32[]{:S(2)}) %all-to-all-start.1) | async-done | bytes 196640 | tf_op jit(solution)/shard_map/all_to_all | solution.py:343
  52.5 2.0 %shard_map.86 = bf16[4,128,1536]{2,1,0:T(8,128)(2,1)S(1)} custom-call(bf16[544,896]{1,0:T(8,128)(2,1)S(1)} %get-tuple-element.16.local_ref, bf16[64,2,768]{2,1,0:T(2,128)(2,1)S(1)} %all-to-all-done.1.prior_ref, bf16[768,1536]{1,0:T(8,128)(2,1)S(1)} %get-tuple-element.18.w_ref), custom_call_target="tpu_custom_call" | custom-call | flops 1308622848 | bytes 4718592 | tf_op jit(solution)/shard_map/pallas_call | solution.py:247
  54.5 21.5 %all_to_all.20.parts_ref = bf16[4,128,1536]{2,1,0:T(8,128)(2,1)S(1)} all-to-all(bf16[4,128,1536]{2,1,0:T(8,128)(2,1)S(1)} %shard_map.86), channel_id=1, replica_groups=mesh['tm'=64,'head'=4,'farm'=2] {'head'}, dimensions={0} | all-to-all | bytes 3145728 | tf_op jit(solution)/shard_map/all_to_all | solution.py:355
  76.0 0.7 shard_map.87
  76.7 33.9 %all_to_all.21 = bf16[128,2,1536]{2,1,0:T(2,128)(2,1)S(1)} all-to-all(bf16[128,2,1536]{2,1,0:T(2,128)(2,1)S(1)} %shard_map.87), channel_id=1, replica_groups=mesh['tm'=64,'head'=4,'farm'=2] {'tm','farm'}, dimensions={0} | all-to-all | bytes 1572864 | tf_op jit(solution)/shard_map/all_to_all | solution.py:367
  110.6 0.9 copy.10
  (1 shorter events, 0.0 us)
Async XLA Ops:
  0.0 40.6 %copy-start.3 = (f32[1536]{0:T(1024)S(1)}, f32[1536]{0:T(1024)}, u32[]{:S(2)}) copy-start(f32[1536]{0:T(1024)} %param.14) | copy-start | bytes 18436
  0.0 40.6 %copy-start.2 = (s32[1,128,1]{1,2,0:T(1,128)S(1)}, s32[1,128,1]{1,2,0:T(1,128)}, u32[]{:S(2)}) copy-start(s32[1,128,1]{1,2,0:T(1,128)} %param.15) | copy-start | bytes 1540
  3.4 29.2 %all-to-all-start = ((bf16[64,2,896]{2,1,0:T(2,128)(2,1)}), bf16[64,2,896]{2,1,0:T(2,128)(2,1)S(1)}, u32[]{:S(2)}, u32[]{:S(2)}) async-start(bf16[64,2,896]{2,1,0:T(2,128)(2,1)} %shard_map.82), calls=%async_computation | async-start | bytes 458752 | tf_op jit(solution)/shard_map/all_to_all | solution.py:293
  34.0 18.5 %all-to-all-start.1 = ((bf16[64,2,768]{2,1,0:T(2,128)(2,1)}), bf16[64,2,768]{2,1,0:T(2,128)(2,1)S(1)}, u32[]{:S(2)}, u32[]{:S(2)}) async-start(bf16[64,2,768]{2,1,0:T(2,128)(2,1)} %shard_map.85), calls=%async_computation.1 | async-start | bytes 393216 | tf_op jit(solution)/shard_map/all_to_all | solution.py:343
  40.7 1.2 %copy-start = (bf16[544,896]{1,0:T(8,128)(2,1)S(1)}, bf16[544,896]{1,0:T(8,128)(2,1)}, u32[]{:S(2)}) copy-start(bf16[544,896]{1,0:T(8,128)(2,1)} %shard_map.83.local_hbm) | copy-start | bytes 2924548
  41.9 1.7 %copy-start.1 = (bf16[768,1536]{1,0:T(8,128)(2,1)S(1)}, bf16[768,1536]{1,0:T(8,128)(2,1)}, u32[]{:S(2)}) copy-start(bf16[768,1536]{1,0:T(8,128)(2,1)} %w_hbm) | copy-start | bytes 7077892

commit v5 on v4

--- a/solution.py
+++ b/solution.py
@@ -9,6 +9,7 @@
 SPAN = 64
 LANES = 128
 ROWS = 16
+TILE = 256
 F32 = jnp.float32
 BF16 = jnp.bfloat16
 FIRST = (((0,), (0,)), ((), ()))
@@ -178,17 +179,15 @@
 def early_kernel(
     owners,
     capacity,
-    w_hbm,
     local_hbm,
     routes_ref,
     gain_ref,
-    w_ref,
     local_ref,
     target_ref,
     gain_out_ref,
     sems,
 ):
-    copies = fetch(((w_hbm, w_ref), (local_hbm, local_ref)), sems)
+    copies = fetch(((local_hbm, local_ref),), sems)
     routes = routes_ref[...]
     rows = routes.shape[1]
     named = lax.broadcasted_iota(jnp.int32, (owners, rows), 0) == routes
@@ -203,14 +202,17 @@
         copy.wait()
 
 
-def project_kernel(heads, local_ref, prior_ref, w_ref, out_ref, mixed_ref):
+def project_kernel(heads, index_ref, local_ref, prior_ref, w_ref, *rest):
+    outs, mixed_ref = rest[:-1], rest[-1]
+    tiles = [slice(k, k + TILE) for k in range(0, w_ref.shape[1], TILE)]
     steps = mixed_ref.shape[0]
     parcels, depth, width = prior_ref.shape
-    pieces, block, width_out = out_ref.shape
+    pieces = len(outs)
+    block, width_out = outs[0].shape
     state = prior_ref[...].reshape(parcels * depth, width)
     matrix = head_spread(ROWS, width, width // heads)
-    for k in range(steps // LANES):
-        rows = slice(k * LANES, (k + 1) * LANES)
+    for k in range(pieces):
+        rows = slice(k * block, (k + 1) * block)
         reach = sum(
             lax.dot_general(
                 local_ref[steps + part * ROWS : steps + (part + 1) * ROWS, rows],
@@ -221,19 +223,21 @@
             for part in range(2)
         )
         carried = reach * mm(local_ref[rows, width:], state)
-        mixed_ref[rows, :] = (local_ref[rows, :width].astype(F32) + carried).astype(BF16)
-    tile = 256
-    for j in range(width_out // tile):
-        columns = slice(j * tile, (j + 1) * tile)
+        ahead = lax.rem(k - index_ref[0] + pieces, pieces)
+        mixed_ref[pl.ds(pl.multiple_of(ahead * block, block), block), :] = (
+            local_ref[rows, :width].astype(F32) + carried
+        ).astype(BF16)
+    for columns in tiles:
         product = mm(mixed_ref[...], w_ref[:, columns]).astype(BF16)
         for d in range(pieces):
-            out_ref[d, :, columns] = product[d * block : (d + 1) * block, :]
-
-
-def regroup_kernel(target_ref, gain_ref, parts_ref, out_ref):
+            outs[d][:, columns] = product[d * block : (d + 1) * block, :]
+
+
+def regroup_kernel(target_ref, gain_ref, *rest):
+    parts, out_ref = rest[:-1], rest[-1]
     owners, capacity, width = out_ref.shape
-    pieces, rows, _ = parts_ref.shape
-    projected = sum(parts_ref[k].astype(F32) for k in range(pieces))
+    rows = parts[0].shape[0]
+    projected = sum(part[...].astype(F32) for part in parts)
     scale = lax.rsqrt(jnp.mean(projected * projected, axis=1, keepdims=True) + 1e-06)
     normed = (projected * scale * gain_ref[...]).astype(BF16)
     place = lax.broadcasted_iota(jnp.int32, (owners * capacity, rows), 0)
@@ -241,13 +245,14 @@
     out_ref[...] = mm(select, normed).astype(BF16).reshape(owners, capacity, width)
 
 
-def call(kernel, outs, scratch, flops, moved, limit, *args, far=()):
+def call(kernel, outs, scratch, flops, moved, limit, *args, far=(), scalars=()):
     vmem = pl.BlockSpec(memory_space=pltpu.VMEM)
     hbm = pl.BlockSpec(memory_space=pltpu.HBM)
+    smem = pl.BlockSpec(memory_space=pltpu.SMEM)
     return pl.pallas_call(
         kernel,
         out_shape=outs,
-        in_specs=[hbm if k in far else vmem for k in range(len(args))],
+        in_specs=[hbm if k in far else smem if k in scalars else vmem for k in range(len(args))],
         out_specs=jax.tree.map(lambda _: vmem, outs),
         scratch_shapes=scratch,
         cost_estimate=pl.CostEstimate(flops=flops, bytes_accessed=moved, transcendentals=0),
@@ -312,24 +317,22 @@
         skip_gain[None, :],
         far=(0, 1, 2, 3),
     )
-    parcel, local, w_late = lax.optimization_barrier((parcel, local, w_out))
-    weights, local, target, gain = call(
+    parcel, local = lax.optimization_barrier((parcel, local))
+    local, target, gain = call(
         functools.partial(early_kernel, owners, capacity),
         (
-            spec(w_out.shape, BF16),
             spec(local.shape, BF16),
             spec((1, block), jnp.int32),
             spec((1, width_out), F32),
         ),
-        [pltpu.SemaphoreType.DMA((2,))],
+        [pltpu.SemaphoreType.DMA((1,))],
         2 * owners * block * block,
-        4 * width * width_out,
+        4 * steps * width,
         16,
-        w_late,
         local,
         owner_ids[0, :, 0][None, :],
         norm_gain[None, :],
-        far=(0, 1),
+        far=(0,),
     )
     prior = call(
         functools.partial(prefix_kernel, heads),
@@ -341,18 +344,24 @@
         parcel,
     )
     prior = lax.all_to_all(prior, "tm", split_axis=0, concat_axis=0, tiled=True)
+    index = lax.axis_index("head").astype(jnp.int32).reshape(1)
     parts = call(
         functools.partial(project_kernel, heads),
-        spec((pieces, block, width_out), BF16),
+        (spec((block, width_out), BF16),) * pieces,
         [wide],
         2 * steps * width * (width_out + state_dim),
         2 * steps * (width + width_out) + 2 * width * width_out,
         24,
+        index,
         local,
         prior,
-        weights,
-    )
-    parts = lax.all_to_all(parts, "head", split_axis=0, concat_axis=0, tiled=True)
+        w_out,
+        scalars=(0,),
+    )
+    ring = range(pieces)
+    moved = [
+        lax.ppermute(parts[d], "head", [(k, (k + d) % pieces) for k in ring]) for d in (2, 1, 3)
+    ]
     outgoing = call(
         regroup_kernel,
         spec((owners, capacity, width_out), BF16),
@@ -362,7 +371,8 @@
         16,
         target,
         gain,
-        parts,
+        parts[0],
+        *moved,
     )
     result = lax.all_to_all(outgoing, ("tm", "farm"), split_axis=0, concat_axis=0, tiled=True)
     return result[None, None]

time: 112 us -> 112 us (level)
  blocking collectives: 55.4 us -> 31.9 us
  waiting for transfers between devices: 13.9 us -> 26 us
  starting transfers between devices: 23.7 us -> 34.9 us
    all_to_all x1 -> x0, blocking collectives: 21.5 us -> none  [shards(): lax.all_to_all(parts, 'head', split_axis=0, concat_axis=0, tiled=True)]
    ppermute x0 -> x3, starting transfers between devices: none -> 11.2 us  [shards(): lax.ppermute(parts[d], 'head', [(k, (k + d) % pieces) for k in ring])]
    ppermute x0 -> x3, waiting for transfers between devices: none -> 10.3 us  [shards(): lax.ppermute(parts[d], 'head', [(k, (k + d) % pieces) for k in ring])]
    all_to_all x1, blocking collectives: 33.9 us -> 31.9 us  [shards(): lax.all_to_all(outgoing, ('tm', 'farm'), split_axis=0, concat_axis=0, til...]
    all_to_all x1, waiting for transfers between devices: 8.34 us -> 10.2 us  [shards(): prior = lax.all_to_all(prior, 'tm', split_axis=0, concat_axis=0, tiled=True)]
  transfers between devices with their start and end apart: 2 -> 5, of which waited for: 2 -> 3; matrix products, arithmetic and copies ran while one was open for 0% -> 0% of each run, Pallas kernels for 6% -> 6%
where the time goes in v5:
time: 112 us; the launch traced here: 111 us
  starting transfers between devices  34.9 us (31%)
  blocking collectives  31.9 us (28%)
  waiting for transfers between devices  26 us (23%)
  Pallas kernels  14.5 us (13%)
  local copies, waits for them, and re-layouts  3.75 us (3%)
    all_to_all x1, blocking collectives, shards(): lax.all_to_all(outgoing, ('tm', 'farm'), split_axis=0, concat_axis=0, til...  31.9 us
    all_to_all x1, starting transfers between devices, shards(): lax.all_to_all(parcel, 'tm', split_axis=0, concat_axis=0, tiled=True)  17.1 us
    pallas_call x6, Pallas kernels, call(): pl.pallas_call(kernel, out_shape=outs, in_specs=[hbm if k in far else sme...  14.5 us
    ppermute x3, starting transfers between devices, shards(): lax.ppermute(parts[d], 'head', [(k, (k + d) % pieces) for k in ring])  11.2 us
    ppermute x3, waiting for transfers between devices, shards(): lax.ppermute(parts[d], 'head', [(k, (k + d) % pieces) for k in ring])  10.3 us
    all_to_all x1, waiting for transfers between devices, shards(): prior = lax.all_to_all(prior, 'tm', split_axis=0, concat_axis=0, tiled=True)  10.2 us
    all_to_all x1, starting transfers between devices, shards(): prior = lax.all_to_all(prior, 'tm', split_axis=0, concat_axis=0, tiled=True)  6.6 us
    all_to_all x1, waiting for transfers between devices, shards(): lax.all_to_all(parcel, 'tm', split_axis=0, concat_axis=0, tiled=True)  5.55 us
  transfers between devices with their start and end apart: 5, of which 3 were waited for; matrix products, arithmetic and copies ran while one was open for 0% of the time, Pallas kernels for 6%

profile of v5, /device:TPU:1, one launch (start us, length us, event | category | flops | bytes accessed | tf_op | source)
XLA Modules:
  0.0 111.2 jit_solution(7837860060930030056)
XLA Ops:
  0.0 0.0 copy-start.3
  0.0 0.0 copy-start.1
  0.0 3.4 %shard_map.82 = bf16[64,2,896]{2,1,0:T(2,128)(2,1)} custom-call(bf16[512,768]{1,0:T(8,128)(2,1)} %bitcast.9, bf16[512,128]{1,0:T(8,128)(2,1)} %bitcast.12, f32[12,1,512]{2,1,0:T(1,128)} %bitcast.15), custom_call_target="tpu_custom_call" | custom-call | flops 100663296 | bytes 786432 | tf_op jit(solution)/shard_map/pallas_call | solution.py:252
  3.4 17.1 %all-to-all-start = ((bf16[64,2,896]{2,1,0:T(2,128)(2,1)}), bf16[64,2,896]{2,1,0:T(2,128)(2,1)S(1)}, u32[]{:S(2)}, u32[]{:S(2)}) async-start(bf16[64,2,896]{2,1,0:T(2,128)(2,1)} %shard_map.82), calls=%async_computation | async-start | bytes 458752 | tf_op jit(solution)/shard_map/all_to_all | solution.py:298
  20.6 6.5 %shard_map.83.local_hbm = bf16[544,896]{1,0:T(8,128)(2,1)} custom-call(bf16[512,768]{1,0:T(8,128)(2,1)} %bitcast.10, bf16[512,128]{1,0:T(8,128)(2,1)} %bitcast.13, bf16[512,128]{1,0:T(8,128)(2,1)} %bitcast.14, f32[12,1,512]{2,1,0:T(1,128)} %bitcast.16, f32[1,12]{1,0:T(1,128)} %bitcast.17), custom_call_target="tpu_custom_call" | custom-call | flops 301989888 | bytes 3145728 | tf_op jit(solution)/shard_map/pallas_call | solution.py:252
  27.1 5.6 %all-to-all-done.in_ref = bf16[64,2,896]{2,1,0:T(2,128)(2,1)S(1)} async-done(((bf16[64,2,896]{2,1,0:T(2,128)(2,1)}), bf16[64,2,896]{2,1,0:T(2,128)(2,1)S(1)}, u32[]{:S(2)}, u32[]{:S(2)}) %all-to-all-start) | async-done | bytes 229408 | tf_op jit(solution)/shard_map/all_to_all | solution.py:298
  32.7 1.3 %shard_map.85 = bf16[64,2,768]{2,1,0:T(2,128)(2,1)} custom-call(bf16[64,2,896]{2,1,0:T(2,128)(2,1)S(1)} %all-to-all-done.in_ref), custom_call_target="tpu_custom_call" | custom-call | flops 25165824 | bytes 393216 | tf_op jit(solution)/shard_map/pallas_call | solution.py:252
  34.0 6.6 %all-to-all-start.1 = ((bf16[64,2,768]{2,1,0:T(2,128)(2,1)}), bf16[64,2,768]{2,1,0:T(2,128)(2,1)S(1)}, u32[]{:S(2)}, u32[]{:S(2)}) async-start(bf16[64,2,768]{2,1,0:T(2,128)(2,1)} %shard_map.85), calls=%async_computation.1 | async-start | bytes 393216 | tf_op jit(solution)/shard_map/all_to_all | solution.py:346
  40.6 0.0 copy-done.3
  40.6 0.0 copy-done.1
  40.7 0.0 copy-start
  40.7 1.2 %copy-done = bf16[544,896]{1,0:T(8,128)(2,1)S(1)} copy-done((bf16[544,896]{1,0:T(8,128)(2,1)S(1)}, bf16[544,896]{1,0:T(8,128)(2,1)}, u32[]{:S(2)}) %copy-start) | copy-done | bytes 974872
  41.9 0.5 shard_map.84
  42.3 10.2 %all-to-all-done.1.prior_ref = bf16[64,2,768]{2,1,0:T(2,128)(2,1)S(1)} async-done(((bf16[64,2,768]{2,1,0:T(2,128)(2,1)}), bf16[64,2,768]{2,1,0:T(2,128)(2,1)S(1)}, u32[]{:S(2)}, u32[]{:S(2)}) %all-to-all-start.1) | async-done | bytes 196640 | tf_op jit(solution)/shard_map/all_to_all | solution.py:346
  52.5 0.0 copy-start.2
  52.5 1.7 %copy-done.2 = bf16[768,1536]{1,0:T(8,128)(2,1)S(1)} copy-done((bf16[768,1536]{1,0:T(8,128)(2,1)S(1)}, bf16[768,1536]{1,0:T(8,128)(2,1)}, u32[]{:S(2)}) %copy-start.2) | copy-done | bytes 2359320
  54.2 2.1 %shard_map.86 = (bf16[128,1536]{1,0:T(8,128)(2,1)S(1)}, bf16[128,1536]{1,0:T(8,128)(2,1)S(1)}, bf16[128,1536]{1,0:T(8,128)(2,1)S(1)}, bf16[128,1536]{1,0:T(8,128)(2,1)S(1)}) custom-call(s32[1]{0:T(128)} %bitcast.6.index_ref, bf16[544,896]{1,0:T(8,128)(2,1)S(1)} %get-tuple-element.17.local_ref, bf16[64,2,768]{2,1,0:T(2,128)(2,1)S(1)} %all-to-all-done.1.prior_ref, ...), custom_call_target="tpu_custom_call" | custom-call | flops 1308622848 | bytes 4718592 | tf_op jit(solution)/shard_map/pallas_call | solution.py:252
  56.3 4.7 %collective-permute-start = (bf16[128,1536]{1,0:T(8,128)(2,1)S(1)}, bf16[128,1536]{1,0:T(8,128)(2,1)S(1)}, u32[]{:S(2)}, u32[]{:S(2)}) collective-permute-start(bf16[128,1536]{1,0:T(8,128)(2,1)S(1)} %get-tuple-element.20), channel_id=1, source_target_pairs={{0,4},{2,6},{4,0},{6,2},{1,5},{3,7},{5,1},{7,3},{8,12},{10,14},{12... | collective-permute-start | bytes 1179656 | tf_op jit(solution)/shard_map/ppermute | solution.py:363
  61.0 2.3 %collective-permute-start.1 = (bf16[128,1536]{1,0:T(8,128)(2,1)S(1)}, bf16[128,1536]{1,0:T(8,128)(2,1)S(1)}, u32[]{:S(2)}, u32[]{:S(2)}) collective-permute-start(bf16[128,1536]{1,0:T(8,128)(2,1)S(1)} %get-tuple-element.21), channel_id=1, source_target_pairs={{0,2},{2,4},{4,6},{6,0},{1,3},{3,5},{5,7},{7,1},{8,10},{10,12},{12... | collective-permute-start | bytes 1179656 | tf_op jit(solution)/shard_map/ppermute | solution.py:363
  63.2 4.2 %collective-permute-start.2 = (bf16[128,1536]{1,0:T(8,128)(2,1)S(1)}, bf16[128,1536]{1,0:T(8,128)(2,1)S(1)}, u32[]{:S(2)}, u32[]{:S(2)}) collective-permute-start(bf16[128,1536]{1,0:T(8,128)(2,1)S(1)} %get-tuple-element.22), channel_id=1, source_target_pairs={{0,6},{2,0},{4,2},{6,4},{1,7},{3,1},{5,3},{7,5},{8,14},{10,8},{12,... | collective-permute-start | bytes 1179656 | tf_op jit(solution)/shard_map/ppermute | solution.py:363
  67.5 0.0 collective-permute-done.rest_1_
  67.5 10.3 %collective-permute-done.1.rest_2_ = bf16[128,1536]{1,0:T(8,128)(2,1)S(1)} collective-permute-done((bf16[128,1536]{1,0:T(8,128)(2,1)S(1)}, bf16[128,1536]{1,0:T(8,128)(2,1)S(1)}, u32[]{:S(2)}, u32[]{:S(2)}) %collective-permute-start.1) | collective-permute-done | bytes 393248 | tf_op jit(solution)/shard_map/ppermute | solution.py:363
  77.7 0.0 collective-permute-done.2.rest_3_
  77.7 0.7 shard_map.87
  78.4 31.9 %all_to_all.15 = bf16[128,2,1536]{2,1,0:T(2,128)(2,1)S(1)} all-to-all(bf16[128,2,1536]{2,1,0:T(2,128)(2,1)S(1)} %shard_map.87), channel_id=1, replica_groups=mesh['tm'=64,'head'=4,'farm'=2] {'tm','farm'}, dimensions={0} | all-to-all | bytes 1572864 | tf_op jit(solution)/shard_map/all_to_all | solution.py:377
  110.3 0.9 copy.10
  (1 shorter events, 0.0 us)
Async XLA Ops:
  0.0 40.6 %copy-start.3 = (f32[1536]{0:T(1024)S(1)}, f32[1536]{0:T(1024)}, u32[]{:S(2)}) copy-start(f32[1536]{0:T(1024)} %param.14) | copy-start | bytes 18436
  0.0 40.6 %copy-start.1 = (s32[1,128,1]{1,2,0:T(1,128)S(1)}, s32[1,128,1]{1,2,0:T(1,128)}, u32[]{:S(2)}) copy-start(s32[1,128,1]{1,2,0:T(1,128)} %param.15) | copy-start | bytes 1540
  3.4 29.2 %all-to-all-start = ((bf16[64,2,896]{2,1,0:T(2,128)(2,1)}), bf16[64,2,896]{2,1,0:T(2,128)(2,1)S(1)}, u32[]{:S(2)}, u32[]{:S(2)}) async-start(bf16[64,2,896]{2,1,0:T(2,128)(2,1)} %shard_map.82), calls=%async_computation | async-start | bytes 458752 | tf_op jit(solution)/shard_map/all_to_all | solution.py:298
  34.0 18.5 %all-to-all-start.1 = ((bf16[64,2,768]{2,1,0:T(2,128)(2,1)}), bf16[64,2,768]{2,1,0:T(2,128)(2,1)S(1)}, u32[]{:S(2)}, u32[]{:S(2)}) async-start(bf16[64,2,768]{2,1,0:T(2,128)(2,1)} %shard_map.85), calls=%async_computation.1 | async-start | bytes 393216 | tf_op jit(solution)/shard_map/all_to_all | solution.py:346
  40.7 1.2 %copy-start = (bf16[544,896]{1,0:T(8,128)(2,1)S(1)}, bf16[544,896]{1,0:T(8,128)(2,1)}, u32[]{:S(2)}) copy-start(bf16[544,896]{1,0:T(8,128)(2,1)} %shard_map.83.local_hbm) | copy-start | bytes 2924548
  52.5 1.7 %copy-start.2 = (bf16[768,1536]{1,0:T(8,128)(2,1)S(1)}, bf16[768,1536]{1,0:T(8,128)(2,1)}, u32[]{:S(2)}) copy-start(bf16[768,1536]{1,0:T(8,128)(2,1)} %w_ref.1) | copy-start | bytes 7077892
  56.3 11.2 %collective-permute-start = (bf16[128,1536]{1,0:T(8,128)(2,1)S(1)}, bf16[128,1536]{1,0:T(8,128)(2,1)S(1)}, u32[]{:S(2)}, u32[]{:S(2)}) collective-permute-start(bf16[128,1536]{1,0:T(8,128)(2,1)S(1)} %get-tuple-element.20), channel_id=1, source_target_pairs={{0,4},{2,6},{4,0},{6,2},{1,5},{3,7},{5,1},{7,3},{8,12},{10,14},{12... | collective-permute-start | bytes 1179656 | tf_op jit(solution)/shard_map/ppermute | solution.py:363
  61.0 16.8 %collective-permute-start.1 = (bf16[128,1536]{1,0:T(8,128)(2,1)S(1)}, bf16[128,1536]{1,0:T(8,128)(2,1)S(1)}, u32[]{:S(2)}, u32[]{:S(2)}) collective-permute-start(bf16[128,1536]{1,0:T(8,128)(2,1)S(1)} %get-tuple-element.21), channel_id=1, source_target_pairs={{0,2},{2,4},{4,6},{6,0},{1,3},{3,5},{5,7},{7,1},{8,10},{10,12},{12... | collective-permute-start | bytes 1179656 | tf_op jit(solution)/shard_map/ppermute | solution.py:363
  63.2 14.5 %collective-permute-start.2 = (bf16[128,1536]{1,0:T(8,128)(2,1)S(1)}, bf16[128,1536]{1,0:T(8,128)(2,1)S(1)}, u32[]{:S(2)}, u32[]{:S(2)}) collective-permute-start(bf16[128,1536]{1,0:T(8,128)(2,1)S(1)} %get-tuple-element.22), channel_id=1, source_target_pairs={{0,6},{2,0},{4,2},{6,4},{1,7},{3,1},{5,3},{7,5},{8,14},{10,8},{12,... | collective-permute-start | bytes 1179656 | tf_op jit(solution)/shard_map/ppermute | solution.py:363

commit v6 on v5

--- a/solution.py
+++ b/solution.py
@@ -9,6 +9,7 @@
 SPAN = 64
 LANES = 128
 ROWS = 16
+SHELF = 12288
 TILE = 256
 F32 = jnp.float32
 BF16 = jnp.bfloat16
@@ -66,10 +67,9 @@
     heads, _, steps = decay_ref.shape
     width = x_ref.shape[1]
     blocks = [slice(k * LANES, (k + 1) * LANES) for k in range(steps // LANES)]
-    first, *others, last = fetch(
-        [(decay_hbm, decay_ref)]
-        + [(x_hbm.at[rows, :], x_ref.at[rows, :]) for rows in blocks]
-        + [(b_hbm, b_ref)],
+    first, second, *others = fetch(
+        [(decay_hbm, decay_ref), (b_hbm, b_ref)]
+        + [(x_hbm.at[rows, :], x_ref.at[rows, :]) for rows in blocks],
         sems,
     )
     matrix = head_spread(heads, width, width // heads)
@@ -80,12 +80,13 @@
         values = decay_ref[:, 0, blocks[k]]
         weights[k] = jnp.exp(running(values, lambda s, t: s > t) + later)
         later = later + jnp.sum(values, axis=1, keepdims=True)
+    second.wait()
+    across = b_ref[...].T
     for rows, weight, copy in zip(blocks, weights, others):
         weight = spread(weight, matrix)
         copy.wait()
         wx_ref[rows, :] = (x_ref[rows, :].astype(F32) * weight).astype(BF16)
-    last.wait()
-    state_ref[...] = lax.dot_general(b_ref[...], wx_ref[...], FIRST, preferred_element_type=F32)
+    state_ref[...] = mm(across, wx_ref[...])
     parcels, depth, _ = out_ref.shape
     unit = head_spread(heads, LANES, 1)
     tail = [
@@ -98,17 +99,16 @@
         out_ref[k, :, width:] = tail
 
 
-def prefix_kernel(heads, in_ref, out_ref, log_ref):
+def prefix_kernel(heads, in_ref, out_ref, factor_ref):
     parcels, depth, width = out_ref.shape
     matrix = head_spread(LANES, width, width // heads)
-    logs = in_ref[:, :, width:].reshape(parcels * depth, LANES)
-    log_ref[...] = mm(logs, matrix)
+    pairs = head_spread(parcels, parcels * depth, depth)
+    logs = mm(pairs, in_ref[:, :, width:].reshape(parcels * depth, LANES))
+    factor_ref[...] = sum(mm(part, matrix) for part in split2(jnp.exp(logs)))
     carried = jnp.zeros((depth, width), F32)
     for k in range(parcels):
         out_ref[k] = carried.astype(BF16)
-        both = log_ref[k * depth : (k + 1) * depth, :]
-        factor = jnp.exp(both[0:1, :] + both[1:2, :])
-        carried = factor * carried + in_ref[k, :, :width].astype(F32)
+        carried = factor_ref[k : k + 1, :] * carried + in_ref[k, :, :width].astype(F32)
 
 
 def local_kernel(
@@ -180,14 +180,19 @@
     owners,
     capacity,
     local_hbm,
+    w_hbm,
     routes_ref,
     gain_ref,
     local_ref,
+    shelf_hbm,
     target_ref,
     gain_out_ref,
     sems,
 ):
-    copies = fetch(((local_hbm, local_ref),), sems)
+    depth, width_out = w_hbm.shape
+    copies = fetch(
+        ((local_hbm, local_ref), (w_hbm, shelf_hbm.at[pl.ds(0, depth), :])), sems
+    )
     routes = routes_ref[...]
     rows = routes.shape[1]
     named = lax.broadcasted_iota(jnp.int32, (owners, rows), 0) == routes
@@ -202,9 +207,11 @@
         copy.wait()
 
 
-def project_kernel(heads, index_ref, local_ref, prior_ref, w_ref, *rest):
-    outs, mixed_ref = rest[:-1], rest[-1]
+def project_kernel(heads, index_ref, local_ref, prior_ref, w_hbm, *rest):
+    outs, (mixed_ref, w_ref, sems) = rest[:-3], rest[-3:]
     tiles = [slice(k, k + TILE) for k in range(0, w_ref.shape[1], TILE)]
+    taken = pl.ds(0, w_ref.shape[0])
+    copies = fetch([(w_hbm.at[taken, lanes], w_ref.at[:, lanes]) for lanes in tiles], sems)
     steps = mixed_ref.shape[0]
     parcels, depth, width = prior_ref.shape
     pieces = len(outs)
@@ -227,7 +234,8 @@
         mixed_ref[pl.ds(pl.multiple_of(ahead * block, block), block), :] = (
             local_ref[rows, :width].astype(F32) + carried
         ).astype(BF16)
-    for columns in tiles:
+    for columns, copy in zip(tiles, copies):
+        copy.wait()
         product = mm(mixed_ref[...], w_ref[:, columns]).astype(BF16)
         for d in range(pieces):
             outs[d][:, columns] = product[d * block : (d + 1) * block, :]
@@ -245,7 +253,7 @@
     out_ref[...] = mm(select, normed).astype(BF16).reshape(owners, capacity, width)
 
 
-def call(kernel, outs, scratch, flops, moved, limit, *args, far=(), scalars=()):
+def call(kernel, outs, scratch, flops, moved, limit, *args, far=(), far_out=(), scalars=()):
     vmem = pl.BlockSpec(memory_space=pltpu.VMEM)
     hbm = pl.BlockSpec(memory_space=pltpu.HBM)
     smem = pl.BlockSpec(memory_space=pltpu.SMEM)
@@ -253,7 +261,9 @@
         kernel,
         out_shape=outs,
         in_specs=[hbm if k in far else smem if k in scalars else vmem for k in range(len(args))],
-        out_specs=jax.tree.map(lambda _: vmem, outs),
+        out_specs=tuple(hbm if k in far_out else vmem for k in range(len(outs)))
+        if isinstance(outs, tuple)
+        else vmem,
         scratch_shapes=scratch,
         cost_estimate=pl.CostEstimate(flops=flops, bytes_accessed=moved, transcendentals=0),
         compiler_params=pltpu.CompilerParams(vmem_limit_bytes=int(limit * 1024 * 1024)),
@@ -317,27 +327,30 @@
         skip_gain[None, :],
         far=(0, 1, 2, 3),
     )
-    parcel, local = lax.optimization_barrier((parcel, local))
-    local, target, gain = call(
+    parcel, local, w_late = lax.optimization_barrier((parcel, local, w_out))
+    local, shelf, target, gain = call(
         functools.partial(early_kernel, owners, capacity),
         (
             spec(local.shape, BF16),
+            spec((SHELF, width_out), BF16),
             spec((1, block), jnp.int32),
             spec((1, width_out), F32),
         ),
-        [pltpu.SemaphoreType.DMA((1,))],
+        [pltpu.SemaphoreType.DMA((2,))],
         2 * owners * block * block,
-        4 * steps * width,
+        4 * width * width_out,
         16,
         local,
+        w_late,
         owner_ids[0, :, 0][None, :],
         norm_gain[None, :],
-        far=(0,),
+        far=(0, 1),
+        far_out=(1,),
     )
     prior = call(
         functools.partial(prefix_kernel, heads),
         spec((times, depth, width), BF16),
-        [pltpu.VMEM((times * depth, width), F32)],
+        [pltpu.VMEM((times, width), F32)],
         2 * state_dim * width * LANES,
         4 * state_dim * width,
         16,
@@ -348,14 +361,19 @@
     parts = call(
         functools.partial(project_kernel, heads),
         (spec((block, width_out), BF16),) * pieces,
-        [wide],
+        [
+            wide,
+            pltpu.VMEM(w_out.shape, BF16),
+            pltpu.SemaphoreType.DMA((width_out // TILE,)),
+        ],
         2 * steps * width * (width_out + state_dim),
         2 * steps * (width + width_out) + 2 * width * width_out,
-        24,
+        40,
         index,
         local,
         prior,
-        w_out,
+        shelf,
+        far=(3,),
         scalars=(0,),
     )
     ring = range(pieces)

time: 112 us -> 114 us (1.018)
  waiting for transfers between devices: 26 us -> 21.9 us
  Pallas kernels: 14.5 us -> 18.1 us
  blocking collectives: 31.9 us -> 33.7 us
  local copies, waits for them, and re-layouts: 3.75 us -> 5.1 us
    all_to_all x1, waiting for transfers between devices: 10.2 us -> 5.99 us  [shards(): prior = lax.all_to_all(prior, 'tm', split_axis=0, concat_axis=0, tiled=True)]
    pallas_call x6, Pallas kernels: 14.5 us -> 18.1 us  [call(): pl.pallas_call(kernel, out_shape=outs, in_specs=[hbm if k in far else sme...]
    all_to_all x1, blocking collectives: 31.9 us -> 33.7 us  [shards(): lax.all_to_all(outgoing, ('tm', 'farm'), split_axis=0, concat_axis=0, til...]
    unnamed x9 -> x7, local copies, waits for them, and re-layouts: 3.74 us -> 4.4 us
  transfers between devices with their start and end apart: 5 -> 5, of which waited for: 3 -> 3; matrix products, arithmetic and copies ran while one was open for 0% -> 1% of each run, Pallas kernels for 6% -> 7%
where the time goes in v6:
time: 114 us
  starting transfers between devices  34.9 us (31%)
  blocking collectives  33.7 us (30%)
  waiting for transfers between devices  21.9 us (19%)
  Pallas kernels  18.1 us (16%)
  local copies, waits for them, and re-layouts  5.1 us (4%)
    all_to_all x1, blocking collectives, shards(): lax.all_to_all(outgoing, ('tm', 'farm'), split_axis=0, concat_axis=0, til...  33.7 us
    pallas_call x6, Pallas kernels, call(): pl.pallas_call(kernel, out_shape=outs, in_specs=[hbm if k in far else sme...  18.1 us
    all_to_all x1, starting transfers between devices, shards(): lax.all_to_all(parcel, 'tm', split_axis=0, concat_axis=0, tiled=True)  17.2 us
    ppermute x3, starting transfers between devices, shards(): lax.ppermute(parts[d], 'head', [(k, (k + d) % pieces) for k in ring])  11.1 us
    ppermute x3, waiting for transfers between devices, shards(): lax.ppermute(parts[d], 'head', [(k, (k + d) % pieces) for k in ring])  10.3 us
    all_to_all x1, starting transfers between devices, shards(): prior = lax.all_to_all(prior, 'tm', split_axis=0, concat_axis=0, tiled=True)  6.6 us
    all_to_all x1, waiting for transfers between devices, shards(): prior = lax.all_to_all(prior, 'tm', split_axis=0, concat_axis=0, tiled=True)  5.99 us
    all_to_all x1, waiting for transfers between devices, shards(): lax.all_to_all(parcel, 'tm', split_axis=0, concat_axis=0, tiled=True)  5.55 us
  transfers between devices with their start and end apart: 5, of which 3 were waited for; matrix products, arithmetic and copies ran while one was open for 1% of the time, Pallas kernels for 7%

profile of v6, /device:TPU:1, one launch (start us, length us, event | category | flops | bytes accessed | tf_op | source)
XLA Modules:
  0.0 113.7 jit_solution(14927756017122747417)
XLA Ops:
  0.0 3.3 %shard_map.82 = bf16[64,2,896]{2,1,0:T(2,128)(2,1)} custom-call(bf16[512,768]{1,0:T(8,128)(2,1)} %bitcast.9, bf16[512,128]{1,0:T(8,128)(2,1)} %bitcast.12, f32[12,1,512]{2,1,0:T(1,128)} %bitcast.15), custom_call_target="tpu_custom_call" | custom-call | flops 100663296 | bytes 786432 | tf_op jit(solution)/shard_map/pallas_call | solution.py:260
  3.3 17.2 %all-to-all-start = ((bf16[64,2,896]{2,1,0:T(2,128)(2,1)}), bf16[64,2,896]{2,1,0:T(2,128)(2,1)S(1)}, u32[]{:S(2)}, u32[]{:S(2)}) async-start(bf16[64,2,896]{2,1,0:T(2,128)(2,1)} %shard_map.82), calls=%async_computation | async-start | bytes 458752 | tf_op jit(solution)/shard_map/all_to_all | solution.py:308
  20.5 6.5 %shard_map.83.local_hbm = bf16[544,896]{1,0:T(8,128)(2,1)} custom-call(bf16[512,768]{1,0:T(8,128)(2,1)} %bitcast.10, bf16[512,128]{1,0:T(8,128)(2,1)} %bitcast.13, bf16[512,128]{1,0:T(8,128)(2,1)} %bitcast.14, f32[12,1,512]{2,1,0:T(1,128)} %bitcast.16, f32[1,12]{1,0:T(1,128)} %bitcast.17), custom_call_target="tpu_custom_call" | custom-call | flops 301989888 | bytes 3145728 | tf_op jit(solution)/shard_map/pallas_call | solution.py:260
  27.0 5.5 %all-to-all-done.in_ref = bf16[64,2,896]{2,1,0:T(2,128)(2,1)S(1)} async-done(((bf16[64,2,896]{2,1,0:T(2,128)(2,1)}), bf16[64,2,896]{2,1,0:T(2,128)(2,1)S(1)}, u32[]{:S(2)}, u32[]{:S(2)}) %all-to-all-start) | async-done | bytes 229408 | tf_op jit(solution)/shard_map/all_to_all | solution.py:308
  32.6 1.3 %shard_map.85 = bf16[64,2,768]{2,1,0:T(2,128)(2,1)} custom-call(bf16[64,2,896]{2,1,0:T(2,128)(2,1)S(1)} %all-to-all-done.in_ref), custom_call_target="tpu_custom_call" | custom-call | flops 25165824 | bytes 393216 | tf_op jit(solution)/shard_map/pallas_call | solution.py:260
  33.9 6.6 %all-to-all-start.1 = ((bf16[64,2,768]{2,1,0:T(2,128)(2,1)}), bf16[64,2,768]{2,1,0:T(2,128)(2,1)S(1)}, u32[]{:S(2)}, u32[]{:S(2)}) async-start(bf16[64,2,768]{2,1,0:T(2,128)(2,1)} %shard_map.85), calls=%async_computation.1 | async-start | bytes 393216 | tf_op jit(solution)/shard_map/all_to_all | solution.py:359
  40.5 0.7 broadcast_in_dim.10.gain_ref
  41.2 0.0 copy-start
  41.2 1.2 %copy-done = bf16[544,896]{1,0:T(8,128)(2,1)S(1)} copy-done((bf16[544,896]{1,0:T(8,128)(2,1)S(1)}, bf16[544,896]{1,0:T(8,128)(2,1)}, u32[]{:S(2)}) %copy-start) | copy-done | bytes 974872
  42.4 0.0 copy-start.1
  42.4 1.7 %copy-done.1 = bf16[768,1536]{1,0:T(8,128)(2,1)S(1)} copy-done((bf16[768,1536]{1,0:T(8,128)(2,1)S(1)}, bf16[768,1536]{1,0:T(8,128)(2,1)}, u32[]{:S(2)}) %copy-start.1) | copy-done | bytes 2359320
  44.1 0.0 copy-start.2
  44.1 0.7 copy-done.2
  44.7 1.7 %shard_map.84 = (bf16[544,896]{1,0:T(8,128)(2,1)S(1)}, bf16[12288,1536]{1,0:T(8,128)(2,1)}, s32[1,128]{1,0:T(1,128)S(1)}, f32[1,1536]{1,0:T(1,128)S(1)}) custom-call(bf16[544,896]{1,0:T(8,128)(2,1)S(1)} %copy-done, bf16[768,1536]{1,0:T(8,128)(2,1)S(1)} %copy-done.1, s32[1,128]{1,0:T(1,128)S(1)} %bitcast.8, f32[1,1536]{1,0:T(1,128)S(1)} %broadcast_in_dim.10.gain_ref), custom_call_target="tpu_custom_call" | custom-call | flops 4194304 | bytes 4718592 | tf_op jit(solution)/shard_map/pallas_call | solution.py:260
  46.4 6.0 %all-to-all-done.1.prior_ref = bf16[64,2,768]{2,1,0:T(2,128)(2,1)S(1)} async-done(((bf16[64,2,768]{2,1,0:T(2,128)(2,1)}), bf16[64,2,768]{2,1,0:T(2,128)(2,1)S(1)}, u32[]{:S(2)}, u32[]{:S(2)}) %all-to-all-start.1) | async-done | bytes 196640 | tf_op jit(solution)/shard_map/all_to_all | solution.py:359
  52.4 4.6 %shard_map.86 = (bf16[128,1536]{1,0:T(8,128)(2,1)S(1)}, bf16[128,1536]{1,0:T(8,128)(2,1)S(1)}, bf16[128,1536]{1,0:T(8,128)(2,1)S(1)}, bf16[128,1536]{1,0:T(8,128)(2,1)S(1)}) custom-call(s32[1]{0:T(128)} %bitcast.6.index_ref, bf16[544,896]{1,0:T(8,128)(2,1)S(1)} %get-tuple-element.20.local_ref, bf16[64,2,768]{2,1,0:T(2,128)(2,1)S(1)} %all-to-all-done.1.prior_ref, ...), custom_call_target="tpu_custom_call" | custom-call | flops 1308622848 | bytes 4718592 | tf_op jit(solution)/shard_map/pallas_call | solution.py:260
  57.0 4.6 %collective-permute-start = (bf16[128,1536]{1,0:T(8,128)(2,1)S(1)}, bf16[128,1536]{1,0:T(8,128)(2,1)S(1)}, u32[]{:S(2)}, u32[]{:S(2)}) collective-permute-start(bf16[128,1536]{1,0:T(8,128)(2,1)S(1)} %get-tuple-element.24), channel_id=1, source_target_pairs={{0,4},{2,6},{4,0},{6,2},{1,5},{3,7},{5,1},{7,3},{8,12},{10,14},{12... | collective-permute-start | bytes 1179656 | tf_op jit(solution)/shard_map/ppermute | solution.py:381
  61.7 2.2 %collective-permute-start.1 = (bf16[128,1536]{1,0:T(8,128)(2,1)S(1)}, bf16[128,1536]{1,0:T(8,128)(2,1)S(1)}, u32[]{:S(2)}, u32[]{:S(2)}) collective-permute-start(bf16[128,1536]{1,0:T(8,128)(2,1)S(1)} %get-tuple-element.25), channel_id=1, source_target_pairs={{0,2},{2,4},{4,6},{6,0},{1,3},{3,5},{5,7},{7,1},{8,10},{10,12},{12... | collective-permute-start | bytes 1179656 | tf_op jit(solution)/shard_map/ppermute | solution.py:381
  63.9 4.3 %collective-permute-start.2 = (bf16[128,1536]{1,0:T(8,128)(2,1)S(1)}, bf16[128,1536]{1,0:T(8,128)(2,1)S(1)}, u32[]{:S(2)}, u32[]{:S(2)}) collective-permute-start(bf16[128,1536]{1,0:T(8,128)(2,1)S(1)} %get-tuple-element.26), channel_id=1, source_target_pairs={{0,6},{2,0},{4,2},{6,4},{1,7},{3,1},{5,3},{7,5},{8,14},{10,8},{12,... | collective-permute-start | bytes 1179656 | tf_op jit(solution)/shard_map/ppermute | solution.py:381
  68.2 0.0 collective-permute-done.rest_1_
  68.2 10.3 %collective-permute-done.1.rest_2_ = bf16[128,1536]{1,0:T(8,128)(2,1)S(1)} collective-permute-done((bf16[128,1536]{1,0:T(8,128)(2,1)S(1)}, bf16[128,1536]{1,0:T(8,128)(2,1)S(1)}, u32[]{:S(2)}, u32[]{:S(2)}) %collective-permute-start.1) | collective-permute-done | bytes 393248 | tf_op jit(solution)/shard_map/ppermute | solution.py:381
  78.5 0.0 collective-permute-done.2.rest_3_
  78.5 0.7 shard_map.87
  79.2 33.7 %all_to_all.15 = bf16[128,2,1536]{2,1,0:T(2,128)(2,1)S(1)} all-to-all(bf16[128,2,1536]{2,1,0:T(2,128)(2,1)S(1)} %shard_map.87), channel_id=1, replica_groups=mesh['tm'=64,'head'=4,'farm'=2] {'tm','farm'}, dimensions={0} | all-to-all | bytes 1572864 | tf_op jit(solution)/shard_map/all_to_all | solution.py:395
  112.8 0.9 copy.10
Async XLA Ops:
  3.3 29.2 %all-to-all-start = ((bf16[64,2,896]{2,1,0:T(2,128)(2,1)}), bf16[64,2,896]{2,1,0:T(2,128)(2,1)S(1)}, u32[]{:S(2)}, u32[]{:S(2)}) async-start(bf16[64,2,896]{2,1,0:T(2,128)(2,1)} %shard_map.82), calls=%async_computation | async-start | bytes 458752 | tf_op jit(solution)/shard_map/all_to_all | solution.py:308
  33.9 18.6 %all-to-all-start.1 = ((bf16[64,2,768]{2,1,0:T(2,128)(2,1)}), bf16[64,2,768]{2,1,0:T(2,128)(2,1)S(1)}, u32[]{:S(2)}, u32[]{:S(2)}) async-start(bf16[64,2,768]{2,1,0:T(2,128)(2,1)} %shard_map.85), calls=%async_computation.1 | async-start | bytes 393216 | tf_op jit(solution)/shard_map/all_to_all | solution.py:359
  41.2 1.2 %copy-start = (bf16[544,896]{1,0:T(8,128)(2,1)S(1)}, bf16[544,896]{1,0:T(8,128)(2,1)}, u32[]{:S(2)}) copy-start(bf16[544,896]{1,0:T(8,128)(2,1)} %shard_map.83.local_hbm) | copy-start | bytes 2924548
  42.4 1.7 %copy-start.1 = (bf16[768,1536]{1,0:T(8,128)(2,1)S(1)}, bf16[768,1536]{1,0:T(8,128)(2,1)}, u32[]{:S(2)}) copy-start(bf16[768,1536]{1,0:T(8,128)(2,1)} %w_hbm) | copy-start | bytes 7077892
  44.1 0.7 copy-start.2
  57.0 11.2 %collective-permute-start = (bf16[128,1536]{1,0:T(8,128)(2,1)S(1)}, bf16[128,1536]{1,0:T(8,128)(2,1)S(1)}, u32[]{:S(2)}, u32[]{:S(2)}) collective-permute-start(bf16[128,1536]{1,0:T(8,128)(2,1)S(1)} %get-tuple-element.24), channel_id=1, source_target_pairs={{0,4},{2,6},{4,0},{6,2},{1,5},{3,7},{5,1},{7,3},{8,12},{10,14},{12... | collective-permute-start | bytes 1179656 | tf_op jit(solution)/shard_map/ppermute | solution.py:381
  61.7 16.8 %collective-permute-start.1 = (bf16[128,1536]{1,0:T(8,128)(2,1)S(1)}, bf16[128,1536]{1,0:T(8,128)(2,1)S(1)}, u32[]{:S(2)}, u32[]{:S(2)}) collective-permute-start(bf16[128,1536]{1,0:T(8,128)(2,1)S(1)} %get-tuple-element.25), channel_id=1, source_target_pairs={{0,2},{2,4},{4,6},{6,0},{1,3},{3,5},{5,7},{7,1},{8,10},{10,12},{12... | collective-permute-start | bytes 1179656 | tf_op jit(solution)/shard_map/ppermute | solution.py:381
  63.9 14.6 %collective-permute-start.2 = (bf16[128,1536]{1,0:T(8,128)(2,1)S(1)}, bf16[128,1536]{1,0:T(8,128)(2,1)S(1)}, u32[]{:S(2)}, u32[]{:S(2)}) collective-permute-start(bf16[128,1536]{1,0:T(8,128)(2,1)S(1)} %get-tuple-element.26), channel_id=1, source_target_pairs={{0,6},{2,0},{4,2},{6,4},{1,7},{3,1},{5,3},{7,5},{8,14},{10,8},{12,... | collective-permute-start | bytes 1179656 | tf_op jit(solution)/shard_map/ppermute | solution.py:381

commit v7 on v4

--- a/solution.py
+++ b/solution.py
@@ -186,6 +186,7 @@
     local_ref,
     target_ref,
     gain_out_ref,
+    token_ref,
     sems,
 ):
     copies = fetch(((w_hbm, w_ref), (local_hbm, local_ref)), sems)
@@ -199,11 +200,12 @@
     slot = jnp.sum(jnp.where(named, earlier, 0.0), axis=0, keepdims=True)
     target_ref[...] = routes * capacity + slot.astype(jnp.int32)
     gain_out_ref[...] = gain_ref[...]
+    token_ref[...] = jnp.zeros(token_ref.shape, BF16)
     for copy in copies:
         copy.wait()
 
 
-def project_kernel(heads, local_ref, prior_ref, w_ref, out_ref, mixed_ref):
+def project_kernel(heads, local_ref, prior_ref, w_ref, token_ref, out_ref, mixed_ref):
     steps = mixed_ref.shape[0]
     parcels, depth, width = prior_ref.shape
     pieces, block, width_out = out_ref.shape
@@ -313,18 +315,19 @@
         far=(0, 1, 2, 3),
     )
     parcel, local, w_late = lax.optimization_barrier((parcel, local, w_out))
-    weights, local, target, gain = call(
+    weights, local, target, gain, token = call(
         functools.partial(early_kernel, owners, capacity),
         (
             spec(w_out.shape, BF16),
             spec(local.shape, BF16),
             spec((1, block), jnp.int32),
             spec((1, width_out), F32),
+            spec((ROWS, LANES), BF16),
         ),
         [pltpu.SemaphoreType.DMA((2,))],
         2 * owners * block * block,
         4 * width * width_out,
-        16,
+        48,
         w_late,
         local,
         owner_ids[0, :, 0][None, :],
@@ -341,6 +344,9 @@
         parcel,
     )
     prior = lax.all_to_all(prior, "tm", split_axis=0, concat_axis=0, tiled=True)
+    prior, token = lax.optimization_barrier((prior, token))
+    token = lax.ppermute(token, "farm", [(0, 1), (1, 0)])
+    prior, token = lax.optimization_barrier((prior, token))
     parts = call(
         functools.partial(project_kernel, heads),
         spec((pieces, block, width_out), BF16),
@@ -351,6 +357,7 @@
         local,
         prior,
         weights,
+        token,
     )
     parts = lax.all_to_all(parts, "head", split_axis=0, concat_axis=0, tiled=True)
     outgoing = call(

time: 112 us -> 117 us (1.045)
  starting transfers between devices: 23.7 us -> 28.5 us
  local copies, waits for them, and re-layouts: 3.75 us -> 2.09 us
  waiting for transfers between devices: 13.9 us -> 15.3 us
    ppermute x0 -> x1, starting transfers between devices: none -> 4.76 us  [shards(): token = lax.ppermute(token, 'farm', [(0, 1), (1, 0)])]
    all_to_all x1, blocking collectives: 33.9 us -> 31.4 us  [shards(): lax.all_to_all(outgoing, ('tm', 'farm'), split_axis=0, concat_axis=0, til...]
    all_to_all x1, blocking collectives: 21.5 us -> 23.6 us  [shards(): lax.all_to_all(parts, 'head', split_axis=0, concat_axis=0, tiled=True)]
    unnamed x9 -> x7, local copies, waits for them, and re-layouts: 3.74 us -> 2.08 us
  transfers between devices with their start and end apart: 2 -> 3, of which waited for: 2 -> 3; matrix products, arithmetic and copies ran while one was open for 0% -> 0% of each run, Pallas kernels for 6% -> 7%
where the time goes in v7:
time: 117 us
  blocking collectives  55 us (47%)
  starting transfers between devices  28.5 us (24%)
  Pallas kernels  15.6 us (13%)
  waiting for transfers between devices  15.3 us (13%)
  local copies, waits for them, and re-layouts  2.09 us (2%)
    all_to_all x1, blocking collectives, shards(): lax.all_to_all(outgoing, ('tm', 'farm'), split_axis=0, concat_axis=0, til...  31.4 us
    all_to_all x1, blocking collectives, shards(): lax.all_to_all(parts, 'head', split_axis=0, concat_axis=0, tiled=True)  23.6 us
    all_to_all x1, starting transfers between devices, shards(): lax.all_to_all(parcel, 'tm', split_axis=0, concat_axis=0, tiled=True)  17.1 us
    pallas_call x6, Pallas kernels, call(): pl.pallas_call(kernel, out_shape=outs, in_specs=[hbm if k in far else vme...  15.6 us
    all_to_all x1, waiting for transfers between devices, shards(): prior = lax.all_to_all(prior, 'tm', split_axis=0, concat_axis=0, tiled=True)  8.95 us
    all_to_all x1, starting transfers between devices, shards(): prior = lax.all_to_all(prior, 'tm', split_axis=0, concat_axis=0, tiled=True)  6.6 us
    all_to_all x1, waiting for transfers between devices, shards(): lax.all_to_all(parcel, 'tm', split_axis=0, concat_axis=0, tiled=True)  5.55 us
    ppermute x1, starting transfers between devices, shards(): token = lax.ppermute(token, 'farm', [(0, 1), (1, 0)])  4.76 us
  transfers between devices with their start and end apart: 3, of which 3 were waited for; matrix products, arithmetic and copies ran while one was open for 0% of the time, Pallas kernels for 7%

profile of v7, /device:TPU:1, one launch (start us, length us, event | category | flops | bytes accessed | tf_op | source)
XLA Modules:
  0.0 116.7 jit_solution(7303278470848165278)
XLA Ops:
  0.0 0.0 copy-start.2
  0.0 0.0 copy-start.1
  0.0 3.4 %shard_map.82 = bf16[64,2,896]{2,1,0:T(2,128)(2,1)} custom-call(bf16[512,768]{1,0:T(8,128)(2,1)} %bitcast.8, bf16[512,128]{1,0:T(8,128)(2,1)} %bitcast.11, f32[12,1,512]{2,1,0:T(1,128)} %bitcast.14), custom_call_target="tpu_custom_call" | custom-call | flops 100663296 | bytes 786432 | tf_op jit(solution)/shard_map/pallas_call | solution.py:249
  3.4 17.1 %all-to-all-start = ((bf16[64,2,896]{2,1,0:T(2,128)(2,1)}), bf16[64,2,896]{2,1,0:T(2,128)(2,1)S(1)}, u32[]{:S(2)}, u32[]{:S(2)}) async-start(bf16[64,2,896]{2,1,0:T(2,128)(2,1)} %shard_map.82), calls=%async_computation | async-start | bytes 458752 | tf_op jit(solution)/shard_map/all_to_all | solution.py:295
  20.6 6.5 %shard_map.83.local_hbm = bf16[544,896]{1,0:T(8,128)(2,1)} custom-call(bf16[512,768]{1,0:T(8,128)(2,1)} %bitcast.9, bf16[512,128]{1,0:T(8,128)(2,1)} %bitcast.12, bf16[512,128]{1,0:T(8,128)(2,1)} %bitcast.13, f32[12,1,512]{2,1,0:T(1,128)} %bitcast.15, f32[1,12]{1,0:T(1,128)} %bitcast.16), custom_call_target="tpu_custom_call" | custom-call | flops 301989888 | bytes 3145728 | tf_op jit(solution)/shard_map/pallas_call | solution.py:249
  27.1 5.6 %all-to-all-done.in_ref = bf16[64,2,896]{2,1,0:T(2,128)(2,1)S(1)} async-done(((bf16[64,2,896]{2,1,0:T(2,128)(2,1)}), bf16[64,2,896]{2,1,0:T(2,128)(2,1)S(1)}, u32[]{:S(2)}, u32[]{:S(2)}) %all-to-all-start) | async-done | bytes 229408 | tf_op jit(solution)/shard_map/all_to_all | solution.py:295
  32.7 1.3 %shard_map.85 = bf16[64,2,768]{2,1,0:T(2,128)(2,1)} custom-call(bf16[64,2,896]{2,1,0:T(2,128)(2,1)S(1)} %all-to-all-done.in_ref), custom_call_target="tpu_custom_call" | custom-call | flops 25165824 | bytes 393216 | tf_op jit(solution)/shard_map/pallas_call | solution.py:249
  34.0 6.6 %all-to-all-start.1 = ((bf16[64,2,768]{2,1,0:T(2,128)(2,1)}), bf16[64,2,768]{2,1,0:T(2,128)(2,1)S(1)}, u32[]{:S(2)}, u32[]{:S(2)}) async-start(bf16[64,2,768]{2,1,0:T(2,128)(2,1)} %shard_map.85), calls=%async_computation.1 | async-start | bytes 393216 | tf_op jit(solution)/shard_map/all_to_all | solution.py:346
  40.6 0.0 copy-done.2
  40.6 0.0 copy-done.1
  40.7 0.0 copy-start
  40.7 1.2 %copy-done = bf16[544,896]{1,0:T(8,128)(2,1)S(1)} copy-done((bf16[544,896]{1,0:T(8,128)(2,1)S(1)}, bf16[544,896]{1,0:T(8,128)(2,1)}, u32[]{:S(2)}) %copy-start) | copy-done | bytes 974872
  41.9 1.7 %shard_map.84 = (bf16[768,1536]{1,0:T(8,128)(2,1)S(1)}, bf16[544,896]{1,0:T(8,128)(2,1)S(1)}, s32[1,128]{1,0:T(1,128)S(1)}, f32[1,1536]{1,0:T(1,128)S(1)}, bf16[16,128]{1,0:T(8,128)(2,1)S(1)}) custom-call(bf16[768,1536]{1,0:T(8,128)(2,1)} %w_hbm, bf16[544,896]{1,0:T(8,128)(2,1)S(1)} %copy-done, s32[1,128]{1,0:T(1,128)S(1)} %bitcast.7, ...), custom_call_target="tpu_custom_call" | custom-call | flops 4194304 | bytes 4718592 | tf_op jit(solution)/shard_map/pallas_call | solution.py:249
  43.5 9.0 %all-to-all-done.1.prior_ref = bf16[64,2,768]{2,1,0:T(2,128)(2,1)S(1)} async-done(((bf16[64,2,768]{2,1,0:T(2,128)(2,1)}), bf16[64,2,768]{2,1,0:T(2,128)(2,1)S(1)}, u32[]{:S(2)}, u32[]{:S(2)}) %all-to-all-start.1) | async-done | bytes 196640 | tf_op jit(solution)/shard_map/all_to_all | solution.py:346
  52.5 4.8 %collective-permute-start = (bf16[16,128]{1,0:T(8,128)(2,1)S(1)}, bf16[16,128]{1,0:T(8,128)(2,1)S(1)}, u32[]{:S(2)}, u32[]{:S(2)}) collective-permute-start(bf16[16,128]{1,0:T(8,128)(2,1)S(1)} %get-tuple-element.25), channel_id=1, source_target_pairs={{0,1},{1,0},{2,3},{3,2},{4,5},{5,4},{6,7},{7,6},{8,9},{9,8},{10,11... | collective-permute-start | bytes 12296 | tf_op jit(solution)/shard_map/ppermute | solution.py:348
  57.3 0.8 collective-permute-done.token_ref
  58.1 2.0 %shard_map.86 = bf16[4,128,1536]{2,1,0:T(8,128)(2,1)S(1)} custom-call(bf16[544,896]{1,0:T(8,128)(2,1)S(1)} %get-tuple-element.21.local_ref, bf16[64,2,768]{2,1,0:T(2,128)(2,1)S(1)} %all-to-all-done.1.prior_ref, bf16[768,1536]{1,0:T(8,128)(2,1)S(1)} %get-tuple-element.27.w_ref, bf16[16,128]{1,0:T(8,128)(2,1)S(1)} %collective-permute-done.token_ref), custom_call_target="tpu_custom_call" | custom-call | flops 1308622848 | bytes 4718592 | tf_op jit(solution)/shard_map/pallas_call | solution.py:249
  60.1 23.6 %all_to_all.20.parts_ref = bf16[4,128,1536]{2,1,0:T(8,128)(2,1)S(1)} all-to-all(bf16[4,128,1536]{2,1,0:T(8,128)(2,1)S(1)} %shard_map.86), channel_id=1, replica_groups=mesh['tm'=64,'head'=4,'farm'=2] {'head'}, dimensions={0} | all-to-all | bytes 3145728 | tf_op jit(solution)/shard_map/all_to_all | solution.py:362
  83.7 0.7 shard_map.87
  84.4 31.4 %all_to_all.21 = bf16[128,2,1536]{2,1,0:T(2,128)(2,1)S(1)} all-to-all(bf16[128,2,1536]{2,1,0:T(2,128)(2,1)S(1)} %shard_map.87), channel_id=1, replica_groups=mesh['tm'=64,'head'=4,'farm'=2] {'tm','farm'}, dimensions={0} | all-to-all | bytes 1572864 | tf_op jit(solution)/shard_map/all_to_all | solution.py:374
  115.8 0.9 copy.10
  (1 shorter events, 0.0 us)
Async XLA Ops:
  0.0 40.6 %copy-start.2 = (f32[1536]{0:T(1024)S(1)}, f32[1536]{0:T(1024)}, u32[]{:S(2)}) copy-start(f32[1536]{0:T(1024)} %param.14) | copy-start | bytes 18436
  0.0 40.6 %copy-start.1 = (s32[1,128,1]{1,2,0:T(1,128)S(1)}, s32[1,128,1]{1,2,0:T(1,128)}, u32[]{:S(2)}) copy-start(s32[1,128,1]{1,2,0:T(1,128)} %param.15) | copy-start | bytes 1540
  3.4 29.2 %all-to-all-start = ((bf16[64,2,896]{2,1,0:T(2,128)(2,1)}), bf16[64,2,896]{2,1,0:T(2,128)(2,1)S(1)}, u32[]{:S(2)}, u32[]{:S(2)}) async-start(bf16[64,2,896]{2,1,0:T(2,128)(2,1)} %shard_map.82), calls=%async_computation | async-start | bytes 458752 | tf_op jit(solution)/shard_map/all_to_all | solution.py:295
  34.0 18.5 %all-to-all-start.1 = ((bf16[64,2,768]{2,1,0:T(2,128)(2,1)}), bf16[64,2,768]{2,1,0:T(2,128)(2,1)S(1)}, u32[]{:S(2)}, u32[]{:S(2)}) async-start(bf16[64,2,768]{2,1,0:T(2,128)(2,1)} %shard_map.85), calls=%async_computation.1 | async-start | bytes 393216 | tf_op jit(solution)/shard_map/all_to_all | solution.py:346
  40.7 1.2 %copy-start = (bf16[544,896]{1,0:T(8,128)(2,1)S(1)}, bf16[544,896]{1,0:T(8,128)(2,1)}, u32[]{:S(2)}) copy-start(bf16[544,896]{1,0:T(8,128)(2,1)} %shard_map.83.local_hbm) | copy-start | bytes 2924548
  52.5 5.6 %collective-permute-start = (bf16[16,128]{1,0:T(8,128)(2,1)S(1)}, bf16[16,128]{1,0:T(8,128)(2,1)S(1)}, u32[]{:S(2)}, u32[]{:S(2)}) collective-permute-start(bf16[16,128]{1,0:T(8,128)(2,1)S(1)} %get-tuple-element.25), channel_id=1, source_target_pairs={{0,1},{1,0},{2,3},{3,2},{4,5},{5,4},{6,7},{7,6},{8,9},{9,8},{10,11... | collective-permute-start | bytes 12296 | tf_op jit(solution)/shard_map/ppermute | solution.py:348

commit v8 on v6

--- a/solution.py
+++ b/solution.py
@@ -9,7 +9,7 @@
 SPAN = 64
 LANES = 128
 ROWS = 16
-SHELF = 12288
+SHELF = 64
 TILE = 256
 F32 = jnp.float32
 BF16 = jnp.bfloat16
@@ -176,42 +176,22 @@
             out_ref[rows, width:] = c
 
 
-def early_kernel(
-    owners,
-    capacity,
-    local_hbm,
-    w_hbm,
-    routes_ref,
-    gain_ref,
-    local_ref,
-    shelf_hbm,
-    target_ref,
-    gain_out_ref,
-    sems,
-):
-    depth, width_out = w_hbm.shape
+def early_kernel(local_hbm, w_hbm, local_ref, shelf_hbm, sems):
     copies = fetch(
-        ((local_hbm, local_ref), (w_hbm, shelf_hbm.at[pl.ds(0, depth), :])), sems
-    )
-    routes = routes_ref[...]
-    rows = routes.shape[1]
-    named = lax.broadcasted_iota(jnp.int32, (owners, rows), 0) == routes
-    before = lax.broadcasted_iota(jnp.int32, (rows, rows), 0) < lax.broadcasted_iota(
-        jnp.int32, (rows, rows), 1
-    )
-    earlier = mm(named.astype(BF16), before.astype(BF16))
-    slot = jnp.sum(jnp.where(named, earlier, 0.0), axis=0, keepdims=True)
-    target_ref[...] = routes * capacity + slot.astype(jnp.int32)
-    gain_out_ref[...] = gain_ref[...]
+        [(local_hbm, local_ref)]
+        + [
+            (w_hbm.at[:, k * TILE : (k + 1) * TILE], shelf_hbm.at[k])
+            for k in range(w_hbm.shape[1] // TILE)
+        ],
+        sems,
+    )
     for copy in copies:
         copy.wait()
 
 
 def project_kernel(heads, index_ref, local_ref, prior_ref, w_hbm, *rest):
     outs, (mixed_ref, w_ref, sems) = rest[:-3], rest[-3:]
-    tiles = [slice(k, k + TILE) for k in range(0, w_ref.shape[1], TILE)]
-    taken = pl.ds(0, w_ref.shape[0])
-    copies = fetch([(w_hbm.at[taken, lanes], w_ref.at[:, lanes]) for lanes in tiles], sems)
+    copies = fetch([(w_hbm.at[k], w_ref.at[k]) for k in range(w_ref.shape[0])], sems)
     steps = mixed_ref.shape[0]
     parcels, depth, width = prior_ref.shape
     pieces = len(outs)
@@ -234,22 +214,31 @@
         mixed_ref[pl.ds(pl.multiple_of(ahead * block, block), block), :] = (
             local_ref[rows, :width].astype(F32) + carried
         ).astype(BF16)
-    for columns, copy in zip(tiles, copies):
+    for k, copy in enumerate(copies):
+        columns = slice(k * TILE, (k + 1) * TILE)
         copy.wait()
-        product = mm(mixed_ref[...], w_ref[:, columns]).astype(BF16)
+        product = mm(mixed_ref[...], w_ref[k]).astype(BF16)
         for d in range(pieces):
             outs[d][:, columns] = product[d * block : (d + 1) * block, :]
 
 
-def regroup_kernel(target_ref, gain_ref, *rest):
+def regroup_kernel(routes_ref, gain_ref, *rest):
     parts, out_ref = rest[:-1], rest[-1]
     owners, capacity, width = out_ref.shape
     rows = parts[0].shape[0]
+    routes = routes_ref[...]
+    named = lax.broadcasted_iota(jnp.int32, (owners, rows), 0) == routes
+    before = lax.broadcasted_iota(jnp.int32, (rows, rows), 0) < lax.broadcasted_iota(
+        jnp.int32, (rows, rows), 1
+    )
+    earlier = mm(named.astype(BF16), before.astype(BF16))
+    slot = jnp.sum(jnp.where(named, earlier, 0.0), axis=0, keepdims=True)
+    target = routes * capacity + slot.astype(jnp.int32)
     projected = sum(part[...].astype(F32) for part in parts)
     scale = lax.rsqrt(jnp.mean(projected * projected, axis=1, keepdims=True) + 1e-06)
     normed = (projected * scale * gain_ref[...]).astype(BF16)
     place = lax.broadcasted_iota(jnp.int32, (owners * capacity, rows), 0)
-    select = (place == target_ref[...]).astype(BF16)
+    select = (place == target).astype(BF16)
     out_ref[...] = mm(select, normed).astype(BF16).reshape(owners, capacity, width)
 
 
@@ -328,22 +317,15 @@
         far=(0, 1, 2, 3),
     )
     parcel, local, w_late = lax.optimization_barrier((parcel, local, w_out))
-    local, shelf, target, gain = call(
-        functools.partial(early_kernel, owners, capacity),
-        (
-            spec(local.shape, BF16),
-            spec((SHELF, width_out), BF16),
-            spec((1, block), jnp.int32),
-            spec((1, width_out), F32),
-        ),
-        [pltpu.SemaphoreType.DMA((2,))],
-        2 * owners * block * block,
+    local, shelf = call(
+        early_kernel,
+        (spec(local.shape, BF16), spec((SHELF, width, TILE), BF16)),
+        [pltpu.SemaphoreType.DMA((1 + width_out // TILE,))],
+        0,
         4 * width * width_out,
-        16,
+        48,
         local,
         w_late,
-        owner_ids[0, :, 0][None, :],
-        norm_gain[None, :],
         far=(0, 1),
         far_out=(1,),
     )
@@ -363,7 +345,7 @@
         (spec((block, width_out), BF16),) * pieces,
         [
             wide,
-            pltpu.VMEM(w_out.shape, BF16),
+            pltpu.VMEM((width_out // TILE, width, TILE), BF16),
             pltpu.SemaphoreType.DMA((width_out // TILE,)),
         ],
         2 * steps * width * (width_out + state_dim),
@@ -387,8 +369,8 @@
         2 * owners * capacity * block * width_out,
         12 * block * width_out,
         16,
-        target,
-        gain,
+        owner_ids[0, :, 0][None, :],
+        norm_gain[None, :],
         parts[0],
         *moved,
     )

time: 114 us -> 113 us (level)
  local copies, waits for them, and re-layouts: 5.1 us -> 3.75 us
  blocking collectives: 33.7 us -> 32.5 us
    all_to_all x1, waiting for transfers between devices: 5.99 us -> 7.22 us  [shards(): prior = lax.all_to_all(prior, 'tm', split_axis=0, concat_axis=0, tiled=True)]
    all_to_all x1, blocking collectives: 33.7 us -> 32.5 us  [shards(): lax.all_to_all(outgoing, ('tm', 'farm'), split_axis=0, concat_axis=0, til...]
    unnamed x7 -> x9, local copies, waits for them, and re-layouts: 4.4 us -> 3.74 us
  transfers between devices with their start and end apart: 5 -> 5, of which waited for: 3 -> 3; matrix products, arithmetic and copies ran while one was open for 1% -> 0% of each run, Pallas kernels for 7% -> 7%
where the time goes in v8:
time: 113 us; the launch traced here: 112 us
  starting transfers between devices  35 us (31%)
  blocking collectives  32.5 us (29%)
  waiting for transfers between devices  22.9 us (20%)
  Pallas kernels  18 us (16%)
  local copies, waits for them, and re-layouts  3.75 us (3%)
    all_to_all x1, blocking collectives, shards(): lax.all_to_all(outgoing, ('tm', 'farm'), split_axis=0, concat_axis=0, til...  32.5 us
    pallas_call x6, Pallas kernels, call(): pl.pallas_call(kernel, out_shape=outs, in_specs=[hbm if k in far else sme...  18 us
    all_to_all x1, starting transfers between devices, shards(): lax.all_to_all(parcel, 'tm', split_axis=0, concat_axis=0, tiled=True)  17.1 us
    ppermute x3, starting transfers between devices, shards(): lax.ppermute(parts[d], 'head', [(k, (k + d) % pieces) for k in ring])  11.2 us
    ppermute x3, waiting for transfers between devices, shards(): lax.ppermute(parts[d], 'head', [(k, (k + d) % pieces) for k in ring])  10.1 us
    all_to_all x1, waiting for transfers between devices, shards(): prior = lax.all_to_all(prior, 'tm', split_axis=0, concat_axis=0, tiled=True)  7.22 us
    all_to_all x1, starting transfers between devices, shards(): prior = lax.all_to_all(prior, 'tm', split_axis=0, concat_axis=0, tiled=True)  6.59 us
    all_to_all x1, waiting for transfers between devices, shards(): lax.all_to_all(parcel, 'tm', split_axis=0, concat_axis=0, tiled=True)  5.55 us
  transfers between devices with their start and end apart: 5, of which 3 were waited for; matrix products, arithmetic and copies ran while one was open for 0% of the time, Pallas kernels for 7%

profile of v8, /device:TPU:1, one launch (start us, length us, event | category | flops | bytes accessed | tf_op | source)
XLA Modules:
  0.0 112.3 jit_solution(6716894567390875180)
XLA Ops:
  0.0 0.0 copy-start.3
  0.0 0.0 copy-start.2
  0.0 3.4 %shard_map.82 = bf16[64,2,896]{2,1,0:T(2,128)(2,1)} custom-call(bf16[512,768]{1,0:T(8,128)(2,1)} %bitcast.9, bf16[512,128]{1,0:T(8,128)(2,1)} %bitcast.12, f32[12,1,512]{2,1,0:T(1,128)} %bitcast.15), custom_call_target="tpu_custom_call" | custom-call | flops 100663296 | bytes 786432 | tf_op jit(solution)/shard_map/pallas_call | solution.py:249
  3.4 17.1 %all-to-all-start = ((bf16[64,2,896]{2,1,0:T(2,128)(2,1)}), bf16[64,2,896]{2,1,0:T(2,128)(2,1)S(1)}, u32[]{:S(2)}, u32[]{:S(2)}) async-start(bf16[64,2,896]{2,1,0:T(2,128)(2,1)} %shard_map.82), calls=%async_computation | async-start | bytes 458752 | tf_op jit(solution)/shard_map/all_to_all | solution.py:297
  20.5 6.5 %shard_map.83.local_hbm = bf16[544,896]{1,0:T(8,128)(2,1)} custom-call(bf16[512,768]{1,0:T(8,128)(2,1)} %bitcast.10, bf16[512,128]{1,0:T(8,128)(2,1)} %bitcast.13, bf16[512,128]{1,0:T(8,128)(2,1)} %bitcast.14, f32[12,1,512]{2,1,0:T(1,128)} %bitcast.16, f32[1,12]{1,0:T(1,128)} %bitcast.17), custom_call_target="tpu_custom_call" | custom-call | flops 301989888 | bytes 3145728 | tf_op jit(solution)/shard_map/pallas_call | solution.py:249
  27.0 5.6 %all-to-all-done.in_ref = bf16[64,2,896]{2,1,0:T(2,128)(2,1)S(1)} async-done(((bf16[64,2,896]{2,1,0:T(2,128)(2,1)}), bf16[64,2,896]{2,1,0:T(2,128)(2,1)S(1)}, u32[]{:S(2)}, u32[]{:S(2)}) %all-to-all-start) | async-done | bytes 229408 | tf_op jit(solution)/shard_map/all_to_all | solution.py:297
  32.6 1.3 %shard_map.85 = bf16[64,2,768]{2,1,0:T(2,128)(2,1)} custom-call(bf16[64,2,896]{2,1,0:T(2,128)(2,1)S(1)} %all-to-all-done.in_ref), custom_call_target="tpu_custom_call" | custom-call | flops 25165824 | bytes 393216 | tf_op jit(solution)/shard_map/pallas_call | solution.py:249
  33.9 6.6 %all-to-all-start.1 = ((bf16[64,2,768]{2,1,0:T(2,128)(2,1)}), bf16[64,2,768]{2,1,0:T(2,128)(2,1)S(1)}, u32[]{:S(2)}, u32[]{:S(2)}) async-start(bf16[64,2,768]{2,1,0:T(2,128)(2,1)} %shard_map.85), calls=%async_computation.1 | async-start | bytes 393216 | tf_op jit(solution)/shard_map/all_to_all | solution.py:341
  40.5 0.0 copy-start
  40.5 1.2 %copy-done = bf16[544,896]{1,0:T(8,128)(2,1)S(1)} copy-done((bf16[544,896]{1,0:T(8,128)(2,1)S(1)}, bf16[544,896]{1,0:T(8,128)(2,1)}, u32[]{:S(2)}) %copy-start) | copy-done | bytes 974872
  41.7 0.0 copy-start.1
  41.7 1.7 %copy-done.1 = bf16[768,1536]{1,0:T(8,128)(2,1)S(1)} copy-done((bf16[768,1536]{1,0:T(8,128)(2,1)S(1)}, bf16[768,1536]{1,0:T(8,128)(2,1)}, u32[]{:S(2)}) %copy-start.1) | copy-done | bytes 2359320
  43.4 1.8 %shard_map.84 = (bf16[544,896]{1,0:T(8,128)(2,1)S(1)}, bf16[64,768,256]{2,1,0:T(8,128)(2,1)}) custom-call(bf16[544,896]{1,0:T(8,128)(2,1)S(1)} %copy-done, bf16[768,1536]{1,0:T(8,128)(2,1)S(1)} %copy-done.1), custom_call_target="tpu_custom_call" | custom-call | bytes 4718592 | tf_op jit(solution)/shard_map/pallas_call | solution.py:249
  45.2 7.2 %all-to-all-done.1.prior_ref = bf16[64,2,768]{2,1,0:T(2,128)(2,1)S(1)} async-done(((bf16[64,2,768]{2,1,0:T(2,128)(2,1)}), bf16[64,2,768]{2,1,0:T(2,128)(2,1)S(1)}, u32[]{:S(2)}, u32[]{:S(2)}) %all-to-all-start.1) | async-done | bytes 196640 | tf_op jit(solution)/shard_map/all_to_all | solution.py:341
  52.4 4.4 %shard_map.86 = (bf16[128,1536]{1,0:T(8,128)(2,1)S(1)}, bf16[128,1536]{1,0:T(8,128)(2,1)S(1)}, bf16[128,1536]{1,0:T(8,128)(2,1)S(1)}, bf16[128,1536]{1,0:T(8,128)(2,1)S(1)}) custom-call(s32[1]{0:T(128)} %bitcast.1.index_ref, bf16[544,896]{1,0:T(8,128)(2,1)S(1)} %get-tuple-element.16.local_ref, bf16[64,2,768]{2,1,0:T(2,128)(2,1)S(1)} %all-to-all-done.1.prior_ref, ...), custom_call_target="tpu_custom_call" | custom-call | flops 1308622848 | bytes 4718592 | tf_op jit(solution)/shard_map/pallas_call | solution.py:249
  56.8 4.7 %collective-permute-start = (bf16[128,1536]{1,0:T(8,128)(2,1)S(1)}, bf16[128,1536]{1,0:T(8,128)(2,1)S(1)}, u32[]{:S(2)}, u32[]{:S(2)}) collective-permute-start(bf16[128,1536]{1,0:T(8,128)(2,1)S(1)} %get-tuple-element.20), channel_id=1, source_target_pairs={{0,4},{2,6},{4,0},{6,2},{1,5},{3,7},{5,1},{7,3},{8,12},{10,14},{12... | collective-permute-start | bytes 1179656 | tf_op jit(solution)/shard_map/ppermute | solution.py:363
  61.5 2.2 %collective-permute-start.1 = (bf16[128,1536]{1,0:T(8,128)(2,1)S(1)}, bf16[128,1536]{1,0:T(8,128)(2,1)S(1)}, u32[]{:S(2)}, u32[]{:S(2)}) collective-permute-start(bf16[128,1536]{1,0:T(8,128)(2,1)S(1)} %get-tuple-element.21), channel_id=1, source_target_pairs={{0,2},{2,4},{4,6},{6,0},{1,3},{3,5},{5,7},{7,1},{8,10},{10,12},{12... | collective-permute-start | bytes 1179656 | tf_op jit(solution)/shard_map/ppermute | solution.py:363
  63.8 4.3 %collective-permute-start.2 = (bf16[128,1536]{1,0:T(8,128)(2,1)S(1)}, bf16[128,1536]{1,0:T(8,128)(2,1)S(1)}, u32[]{:S(2)}, u32[]{:S(2)}) collective-permute-start(bf16[128,1536]{1,0:T(8,128)(2,1)S(1)} %get-tuple-element.22), channel_id=1, source_target_pairs={{0,6},{2,0},{4,2},{6,4},{1,7},{3,1},{5,3},{7,5},{8,14},{10,8},{12,... | collective-permute-start | bytes 1179656 | tf_op jit(solution)/shard_map/ppermute | solution.py:363
  68.0 0.0 copy-done.3
  68.1 0.0 collective-permute-done.rest_1_
  68.1 10.1 %collective-permute-done.1.rest_2_ = bf16[128,1536]{1,0:T(8,128)(2,1)S(1)} collective-permute-done((bf16[128,1536]{1,0:T(8,128)(2,1)S(1)}, bf16[128,1536]{1,0:T(8,128)(2,1)S(1)}, u32[]{:S(2)}, u32[]{:S(2)}) %collective-permute-start.1) | collective-permute-done | bytes 393248 | tf_op jit(solution)/shard_map/ppermute | solution.py:363
  78.2 0.0 collective-permute-done.2.rest_3_
  78.2 0.0 copy-done.2
  78.2 0.7 shard_map.87
  78.9 32.5 %all_to_all.15 = bf16[128,2,1536]{2,1,0:T(2,128)(2,1)S(1)} all-to-all(bf16[128,2,1536]{2,1,0:T(2,128)(2,1)S(1)} %shard_map.87), channel_id=1, replica_groups=mesh['tm'=64,'head'=4,'farm'=2] {'tm','farm'}, dimensions={0} | all-to-all | bytes 1572864 | tf_op jit(solution)/shard_map/all_to_all | solution.py:377
  111.4 0.9 copy.10
  (1 shorter events, 0.0 us)
Async XLA Ops:
  0.0 68.0 %copy-start.3 = (f32[1536]{0:T(1024)S(1)}, f32[1536]{0:T(1024)}, u32[]{:S(2)}) copy-start(f32[1536]{0:T(1024)} %param.14) | copy-start | bytes 18436
  0.0 78.2 %copy-start.2 = (s32[1,128,1]{1,2,0:T(1,128)S(1)}, s32[1,128,1]{1,2,0:T(1,128)}, u32[]{:S(2)}) copy-start(s32[1,128,1]{1,2,0:T(1,128)} %param.15) | copy-start | bytes 1540
  3.4 29.2 %all-to-all-start = ((bf16[64,2,896]{2,1,0:T(2,128)(2,1)}), bf16[64,2,896]{2,1,0:T(2,128)(2,1)S(1)}, u32[]{:S(2)}, u32[]{:S(2)}) async-start(bf16[64,2,896]{2,1,0:T(2,128)(2,1)} %shard_map.82), calls=%async_computation | async-start | bytes 458752 | tf_op jit(solution)/shard_map/all_to_all | solution.py:297
  33.9 18.5 %all-to-all-start.1 = ((bf16[64,2,768]{2,1,0:T(2,128)(2,1)}), bf16[64,2,768]{2,1,0:T(2,128)(2,1)S(1)}, u32[]{:S(2)}, u32[]{:S(2)}) async-start(bf16[64,2,768]{2,1,0:T(2,128)(2,1)} %shard_map.85), calls=%async_computation.1 | async-start | bytes 393216 | tf_op jit(solution)/shard_map/all_to_all | solution.py:341
  40.5 1.2 %copy-start = (bf16[544,896]{1,0:T(8,128)(2,1)S(1)}, bf16[544,896]{1,0:T(8,128)(2,1)}, u32[]{:S(2)}) copy-start(bf16[544,896]{1,0:T(8,128)(2,1)} %shard_map.83.local_hbm) | copy-start | bytes 2924548
  41.7 1.7 %copy-start.1 = (bf16[768,1536]{1,0:T(8,128)(2,1)S(1)}, bf16[768,1536]{1,0:T(8,128)(2,1)}, u32[]{:S(2)}) copy-start(bf16[768,1536]{1,0:T(8,128)(2,1)} %w_hbm) | copy-start | bytes 7077892
  56.8 11.3 %collective-permute-start = (bf16[128,1536]{1,0:T(8,128)(2,1)S(1)}, bf16[128,1536]{1,0:T(8,128)(2,1)S(1)}, u32[]{:S(2)}, u32[]{:S(2)}) collective-permute-start(bf16[128,1536]{1,0:T(8,128)(2,1)S(1)} %get-tuple-element.20), channel_id=1, source_target_pairs={{0,4},{2,6},{4,0},{6,2},{1,5},{3,7},{5,1},{7,3},{8,12},{10,14},{12... | collective-permute-start | bytes 1179656 | tf_op jit(solution)/shard_map/ppermute | solution.py:363
  61.5 16.7 %collective-permute-start.1 = (bf16[128,1536]{1,0:T(8,128)(2,1)S(1)}, bf16[128,1536]{1,0:T(8,128)(2,1)S(1)}, u32[]{:S(2)}, u32[]{:S(2)}) collective-permute-start(bf16[128,1536]{1,0:T(8,128)(2,1)S(1)} %get-tuple-element.21), channel_id=1, source_target_pairs={{0,2},{2,4},{4,6},{6,0},{1,3},{3,5},{5,7},{7,1},{8,10},{10,12},{12... | collective-permute-start | bytes 1179656 | tf_op jit(solution)/shard_map/ppermute | solution.py:363
  63.8 14.5 %collective-permute-start.2 = (bf16[128,1536]{1,0:T(8,128)(2,1)S(1)}, bf16[128,1536]{1,0:T(8,128)(2,1)S(1)}, u32[]{:S(2)}, u32[]{:S(2)}) collective-permute-start(bf16[128,1536]{1,0:T(8,128)(2,1)S(1)} %get-tuple-element.22), channel_id=1, source_target_pairs={{0,6},{2,0},{4,2},{6,4},{1,7},{3,1},{5,3},{7,5},{8,14},{10,8},{12,... | collective-permute-start | bytes 1179656 | tf_op jit(solution)/shard_map/ppermute | solution.py:363

commit v9 on v8

--- a/solution.py
+++ b/solution.py
@@ -9,7 +9,6 @@
 SPAN = 64
 LANES = 128
 ROWS = 16
-SHELF = 64
 TILE = 256
 F32 = jnp.float32
 BF16 = jnp.bfloat16
@@ -176,22 +175,14 @@
             out_ref[rows, width:] = c
 
 
-def early_kernel(local_hbm, w_hbm, local_ref, shelf_hbm, sems):
-    copies = fetch(
-        [(local_hbm, local_ref)]
-        + [
-            (w_hbm.at[:, k * TILE : (k + 1) * TILE], shelf_hbm.at[k])
-            for k in range(w_hbm.shape[1] // TILE)
-        ],
-        sems,
-    )
-    for copy in copies:
-        copy.wait()
-
-
-def project_kernel(heads, index_ref, local_ref, prior_ref, w_hbm, *rest):
-    outs, (mixed_ref, w_ref, sems) = rest[:-3], rest[-3:]
-    copies = fetch([(w_hbm.at[k], w_ref.at[k]) for k in range(w_ref.shape[0])], sems)
+def early_kernel(local_hbm, local_ref, sems):
+    (copy,) = fetch(((local_hbm, local_ref),), sems)
+    copy.wait()
+
+
+def project_kernel(heads, index_ref, local_ref, prior_ref, w_ref, *rest):
+    outs, mixed_ref = rest[:-1], rest[-1]
+    tiles = [slice(k, k + TILE) for k in range(0, w_ref.shape[1], TILE)]
     steps = mixed_ref.shape[0]
     parcels, depth, width = prior_ref.shape
     pieces = len(outs)
@@ -214,10 +205,8 @@
         mixed_ref[pl.ds(pl.multiple_of(ahead * block, block), block), :] = (
             local_ref[rows, :width].astype(F32) + carried
         ).astype(BF16)
-    for k, copy in enumerate(copies):
-        columns = slice(k * TILE, (k + 1) * TILE)
-        copy.wait()
-        product = mm(mixed_ref[...], w_ref[k]).astype(BF16)
+    for columns in tiles:
+        product = mm(mixed_ref[...], w_ref[:, columns]).astype(BF16)
         for d in range(pieces):
             outs[d][:, columns] = product[d * block : (d + 1) * block, :]
 
@@ -242,7 +231,7 @@
     out_ref[...] = mm(select, normed).astype(BF16).reshape(owners, capacity, width)
 
 
-def call(kernel, outs, scratch, flops, moved, limit, *args, far=(), far_out=(), scalars=()):
+def call(kernel, outs, scratch, flops, moved, limit, *args, far=(), scalars=()):
     vmem = pl.BlockSpec(memory_space=pltpu.VMEM)
     hbm = pl.BlockSpec(memory_space=pltpu.HBM)
     smem = pl.BlockSpec(memory_space=pltpu.SMEM)
@@ -250,9 +239,7 @@
         kernel,
         out_shape=outs,
         in_specs=[hbm if k in far else smem if k in scalars else vmem for k in range(len(args))],
-        out_specs=tuple(hbm if k in far_out else vmem for k in range(len(outs)))
-        if isinstance(outs, tuple)
-        else vmem,
+        out_specs=jax.tree.map(lambda _: vmem, outs),
         scratch_shapes=scratch,
         cost_estimate=pl.CostEstimate(flops=flops, bytes_accessed=moved, transcendentals=0),
         compiler_params=pltpu.CompilerParams(vmem_limit_bytes=int(limit * 1024 * 1024)),
@@ -316,18 +303,16 @@
         skip_gain[None, :],
         far=(0, 1, 2, 3),
     )
-    parcel, local, w_late = lax.optimization_barrier((parcel, local, w_out))
-    local, shelf = call(
+    parcel, local = lax.optimization_barrier((parcel, local))
+    local = call(
         early_kernel,
-        (spec(local.shape, BF16), spec((SHELF, width, TILE), BF16)),
-        [pltpu.SemaphoreType.DMA((1 + width_out // TILE,))],
+        spec(local.shape, BF16),
+        [pltpu.SemaphoreType.DMA((1,))],
         0,
-        4 * width * width_out,
-        48,
+        4 * steps * width,
+        16,
         local,
-        w_late,
-        far=(0, 1),
-        far_out=(1,),
+        far=(0,),
     )
     prior = call(
         functools.partial(prefix_kernel, heads),
@@ -343,19 +328,14 @@
     parts = call(
         functools.partial(project_kernel, heads),
         (spec((block, width_out), BF16),) * pieces,
-        [
-            wide,
-            pltpu.VMEM((width_out // TILE, width, TILE), BF16),
-            pltpu.SemaphoreType.DMA((width_out // TILE,)),
-        ],
+        [wide],
         2 * steps * width * (width_out + state_dim),
         2 * steps * (width + width_out) + 2 * width * width_out,
-        40,
+        24,
         index,
         local,
         prior,
-        shelf,
-        far=(3,),
+        w_out,
         scalars=(0,),
     )
     ring = range(pieces)

time: 113 us -> 112 us (level)
  Pallas kernels: 18 us -> 14.3 us
  waiting for transfers between devices: 22.9 us -> 26.3 us
    pallas_call x6, Pallas kernels: 18 us -> 14.3 us  [call(): pl.pallas_call(kernel, out_shape=outs, in_specs=[hbm if k in far else sme...]
    all_to_all x1, waiting for transfers between devices: 7.22 us -> 10.4 us  [shards(): prior = lax.all_to_all(prior, 'tm', split_axis=0, concat_axis=0, tiled=True)]
  transfers between devices with their start and end apart: 5 -> 5, of which waited for: 3 -> 3; matrix products, arithmetic and copies ran while one was open for 0% -> 0% of each run, Pallas kernels for 7% -> 6%
where the time goes in v9:
time: 112 us; the launch traced here: 111 us
  starting transfers between devices  34.9 us (31%)
  blocking collectives  31.8 us (28%)
  waiting for transfers between devices  26.3 us (23%)
  Pallas kernels  14.3 us (13%)
  local copies, waits for them, and re-layouts  3.75 us (3%)
    all_to_all x1, blocking collectives, shards(): lax.all_to_all(outgoing, ('tm', 'farm'), split_axis=0, concat_axis=0, til...  31.8 us
    all_to_all x1, starting transfers between devices, shards(): lax.all_to_all(parcel, 'tm', split_axis=0, concat_axis=0, tiled=True)  17.2 us
    pallas_call x6, Pallas kernels, call(): pl.pallas_call(kernel, out_shape=outs, in_specs=[hbm if k in far else sme...  14.3 us
    ppermute x3, starting transfers between devices, shards(): lax.ppermute(parts[d], 'head', [(k, (k + d) % pieces) for k in ring])  11.1 us
    all_to_all x1, waiting for transfers between devices, shards(): prior = lax.all_to_all(prior, 'tm', split_axis=0, concat_axis=0, tiled=True)  10.4 us
    ppermute x3, waiting for transfers between devices, shards(): lax.ppermute(parts[d], 'head', [(k, (k + d) % pieces) for k in ring])  10.3 us
    all_to_all x1, starting transfers between devices, shards(): prior = lax.all_to_all(prior, 'tm', split_axis=0, concat_axis=0, tiled=True)  6.6 us
    all_to_all x1, waiting for transfers between devices, shards(): lax.all_to_all(parcel, 'tm', split_axis=0, concat_axis=0, tiled=True)  5.55 us
  transfers between devices with their start and end apart: 5, of which 3 were waited for; matrix products, arithmetic and copies ran while one was open for 0% of the time, Pallas kernels for 6%

profile of v9, /device:TPU:1, one launch (start us, length us, event | category | flops | bytes accessed | tf_op | source)
XLA Modules:
  0.0 111.1 jit_solution(12197396426286656091)
XLA Ops:
  0.0 3.3 %shard_map.82 = bf16[64,2,896]{2,1,0:T(2,128)(2,1)} custom-call(bf16[512,768]{1,0:T(8,128)(2,1)} %bitcast.9, bf16[512,128]{1,0:T(8,128)(2,1)} %bitcast.12, f32[12,1,512]{2,1,0:T(1,128)} %bitcast.15), custom_call_target="tpu_custom_call" | custom-call | flops 100663296 | bytes 786432 | tf_op jit(solution)/shard_map/pallas_call | solution.py:238
  3.3 17.2 %all-to-all-start = ((bf16[64,2,896]{2,1,0:T(2,128)(2,1)}), bf16[64,2,896]{2,1,0:T(2,128)(2,1)S(1)}, u32[]{:S(2)}, u32[]{:S(2)}) async-start(bf16[64,2,896]{2,1,0:T(2,128)(2,1)} %shard_map.82), calls=%async_computation | async-start | bytes 458752 | tf_op jit(solution)/shard_map/all_to_all | solution.py:284
  20.5 6.5 %shard_map.83.local_hbm = bf16[544,896]{1,0:T(8,128)(2,1)} custom-call(bf16[512,768]{1,0:T(8,128)(2,1)} %bitcast.10, bf16[512,128]{1,0:T(8,128)(2,1)} %bitcast.13, bf16[512,128]{1,0:T(8,128)(2,1)} %bitcast.14, f32[12,1,512]{2,1,0:T(1,128)} %bitcast.16, f32[1,12]{1,0:T(1,128)} %bitcast.17), custom_call_target="tpu_custom_call" | custom-call | flops 301989888 | bytes 3145728 | tf_op jit(solution)/shard_map/pallas_call | solution.py:238
  27.0 5.5 %all-to-all-done.in_ref = bf16[64,2,896]{2,1,0:T(2,128)(2,1)S(1)} async-done(((bf16[64,2,896]{2,1,0:T(2,128)(2,1)}), bf16[64,2,896]{2,1,0:T(2,128)(2,1)S(1)}, u32[]{:S(2)}, u32[]{:S(2)}) %all-to-all-start) | async-done | bytes 229408 | tf_op jit(solution)/shard_map/all_to_all | solution.py:284
  32.6 1.3 %shard_map.85 = bf16[64,2,768]{2,1,0:T(2,128)(2,1)} custom-call(bf16[64,2,896]{2,1,0:T(2,128)(2,1)S(1)} %all-to-all-done.in_ref), custom_call_target="tpu_custom_call" | custom-call | flops 25165824 | bytes 393216 | tf_op jit(solution)/shard_map/pallas_call | solution.py:238
  33.9 6.6 %all-to-all-start.1 = ((bf16[64,2,768]{2,1,0:T(2,128)(2,1)}), bf16[64,2,768]{2,1,0:T(2,128)(2,1)S(1)}, u32[]{:S(2)}, u32[]{:S(2)}) async-start(bf16[64,2,768]{2,1,0:T(2,128)(2,1)} %shard_map.85), calls=%async_computation.1 | async-start | bytes 393216 | tf_op jit(solution)/shard_map/all_to_all | solution.py:326
  40.5 0.0 copy-start
  40.5 1.2 %copy-done = bf16[544,896]{1,0:T(8,128)(2,1)S(1)} copy-done((bf16[544,896]{1,0:T(8,128)(2,1)S(1)}, bf16[544,896]{1,0:T(8,128)(2,1)}, u32[]{:S(2)}) %copy-start) | copy-done | bytes 974872
  41.7 0.3 shard_map.84.local_ref
  42.0 10.4 %all-to-all-done.1.prior_ref = bf16[64,2,768]{2,1,0:T(2,128)(2,1)S(1)} async-done(((bf16[64,2,768]{2,1,0:T(2,128)(2,1)}), bf16[64,2,768]{2,1,0:T(2,128)(2,1)S(1)}, u32[]{:S(2)}, u32[]{:S(2)}) %all-to-all-start.1) | async-done | bytes 196640 | tf_op jit(solution)/shard_map/all_to_all | solution.py:326
  52.4 0.0 copy-start.2
  52.4 1.7 %copy-done.2 = bf16[768,1536]{1,0:T(8,128)(2,1)S(1)} copy-done((bf16[768,1536]{1,0:T(8,128)(2,1)S(1)}, bf16[768,1536]{1,0:T(8,128)(2,1)}, u32[]{:S(2)}) %copy-start.2) | copy-done | bytes 2359320
  54.1 0.0 copy-start.3
  54.1 0.0 copy-start.1
  54.1 2.1 %shard_map.86 = (bf16[128,1536]{1,0:T(8,128)(2,1)S(1)}, bf16[128,1536]{1,0:T(8,128)(2,1)S(1)}, bf16[128,1536]{1,0:T(8,128)(2,1)S(1)}, bf16[128,1536]{1,0:T(8,128)(2,1)S(1)}) custom-call(s32[1]{0:T(128)} %bitcast.1.index_ref, bf16[544,896]{1,0:T(8,128)(2,1)S(1)} %shard_map.84.local_ref, bf16[64,2,768]{2,1,0:T(2,128)(2,1)S(1)} %all-to-all-done.1.prior_ref, ...), custom_call_target="tpu_custom_call" | custom-call | flops 1308622848 | bytes 4718592 | tf_op jit(solution)/shard_map/pallas_call | solution.py:238
  56.2 4.6 %collective-permute-start = (bf16[128,1536]{1,0:T(8,128)(2,1)S(1)}, bf16[128,1536]{1,0:T(8,128)(2,1)S(1)}, u32[]{:S(2)}, u32[]{:S(2)}) collective-permute-start(bf16[128,1536]{1,0:T(8,128)(2,1)S(1)} %get-tuple-element.14), channel_id=1, source_target_pairs={{0,4},{2,6},{4,0},{6,2},{1,5},{3,7},{5,1},{7,3},{8,12},{10,14},{12... | collective-permute-start | bytes 1179656 | tf_op jit(solution)/shard_map/ppermute | solution.py:343
  60.9 2.2 %collective-permute-start.1 = (bf16[128,1536]{1,0:T(8,128)(2,1)S(1)}, bf16[128,1536]{1,0:T(8,128)(2,1)S(1)}, u32[]{:S(2)}, u32[]{:S(2)}) collective-permute-start(bf16[128,1536]{1,0:T(8,128)(2,1)S(1)} %get-tuple-element.15), channel_id=1, source_target_pairs={{0,2},{2,4},{4,6},{6,0},{1,3},{3,5},{5,7},{7,1},{8,10},{10,12},{12... | collective-permute-start | bytes 1179656 | tf_op jit(solution)/shard_map/ppermute | solution.py:343
  63.1 4.3 %collective-permute-start.2 = (bf16[128,1536]{1,0:T(8,128)(2,1)S(1)}, bf16[128,1536]{1,0:T(8,128)(2,1)S(1)}, u32[]{:S(2)}, u32[]{:S(2)}) collective-permute-start(bf16[128,1536]{1,0:T(8,128)(2,1)S(1)} %get-tuple-element.16), channel_id=1, source_target_pairs={{0,6},{2,0},{4,2},{6,4},{1,7},{3,1},{5,3},{7,5},{8,14},{10,8},{12,... | collective-permute-start | bytes 1179656 | tf_op jit(solution)/shard_map/ppermute | solution.py:343
  67.4 0.0 copy-done.3
  67.4 0.0 collective-permute-done.rest_1_
  67.4 10.3 %collective-permute-done.1.rest_2_ = bf16[128,1536]{1,0:T(8,128)(2,1)S(1)} collective-permute-done((bf16[128,1536]{1,0:T(8,128)(2,1)S(1)}, bf16[128,1536]{1,0:T(8,128)(2,1)S(1)}, u32[]{:S(2)}, u32[]{:S(2)}) %collective-permute-start.1) | collective-permute-done | bytes 393248 | tf_op jit(solution)/shard_map/ppermute | solution.py:343
  77.7 0.0 collective-permute-done.2.rest_3_
  77.7 0.0 copy-done.1
  77.7 0.7 shard_map.87
  78.4 31.8 %all_to_all.15 = bf16[128,2,1536]{2,1,0:T(2,128)(2,1)S(1)} all-to-all(bf16[128,2,1536]{2,1,0:T(2,128)(2,1)S(1)} %shard_map.87), channel_id=1, replica_groups=mesh['tm'=64,'head'=4,'farm'=2] {'tm','farm'}, dimensions={0} | all-to-all | bytes 1572864 | tf_op jit(solution)/shard_map/all_to_all | solution.py:357
  110.2 0.9 copy.10
  (1 shorter events, 0.0 us)
Async XLA Ops:
  3.3 29.2 %all-to-all-start = ((bf16[64,2,896]{2,1,0:T(2,128)(2,1)}), bf16[64,2,896]{2,1,0:T(2,128)(2,1)S(1)}, u32[]{:S(2)}, u32[]{:S(2)}) async-start(bf16[64,2,896]{2,1,0:T(2,128)(2,1)} %shard_map.82), calls=%async_computation | async-start | bytes 458752 | tf_op jit(solution)/shard_map/all_to_all | solution.py:284
  33.9 18.6 %all-to-all-start.1 = ((bf16[64,2,768]{2,1,0:T(2,128)(2,1)}), bf16[64,2,768]{2,1,0:T(2,128)(2,1)S(1)}, u32[]{:S(2)}, u32[]{:S(2)}) async-start(bf16[64,2,768]{2,1,0:T(2,128)(2,1)} %shard_map.85), calls=%async_computation.1 | async-start | bytes 393216 | tf_op jit(solution)/shard_map/all_to_all | solution.py:326
  40.5 1.2 %copy-start = (bf16[544,896]{1,0:T(8,128)(2,1)S(1)}, bf16[544,896]{1,0:T(8,128)(2,1)}, u32[]{:S(2)}) copy-start(bf16[544,896]{1,0:T(8,128)(2,1)} %shard_map.83.local_hbm) | copy-start | bytes 2924548
  52.4 1.7 %copy-start.2 = (bf16[768,1536]{1,0:T(8,128)(2,1)S(1)}, bf16[768,1536]{1,0:T(8,128)(2,1)}, u32[]{:S(2)}) copy-start(bf16[768,1536]{1,0:T(8,128)(2,1)} %w_ref.1) | copy-start | bytes 7077892
  54.1 13.3 %copy-start.3 = (f32[1536]{0:T(1024)S(1)}, f32[1536]{0:T(1024)}, u32[]{:S(2)}) copy-start(f32[1536]{0:T(1024)} %param.14) | copy-start | bytes 18436
  54.1 23.6 %copy-start.1 = (s32[1,128,1]{1,2,0:T(1,128)S(1)}, s32[1,128,1]{1,2,0:T(1,128)}, u32[]{:S(2)}) copy-start(s32[1,128,1]{1,2,0:T(1,128)} %param.15) | copy-start | bytes 1540
  56.2 11.2 %collective-permute-start = (bf16[128,1536]{1,0:T(8,128)(2,1)S(1)}, bf16[128,1536]{1,0:T(8,128)(2,1)S(1)}, u32[]{:S(2)}, u32[]{:S(2)}) collective-permute-start(bf16[128,1536]{1,0:T(8,128)(2,1)S(1)} %get-tuple-element.14), channel_id=1, source_target_pairs={{0,4},{2,6},{4,0},{6,2},{1,5},{3,7},{5,1},{7,3},{8,12},{10,14},{12... | collective-permute-start | bytes 1179656 | tf_op jit(solution)/shard_map/ppermute | solution.py:343
  60.9 16.8 %collective-permute-start.1 = (bf16[128,1536]{1,0:T(8,128)(2,1)S(1)}, bf16[128,1536]{1,0:T(8,128)(2,1)S(1)}, u32[]{:S(2)}, u32[]{:S(2)}) collective-permute-start(bf16[128,1536]{1,0:T(8,128)(2,1)S(1)} %get-tuple-element.15), channel_id=1, source_target_pairs={{0,2},{2,4},{4,6},{6,0},{1,3},{3,5},{5,7},{7,1},{8,10},{10,12},{12... | collective-permute-start | bytes 1179656 | tf_op jit(solution)/shard_map/ppermute | solution.py:343
  63.1 14.6 %collective-permute-start.2 = (bf16[128,1536]{1,0:T(8,128)(2,1)S(1)}, bf16[128,1536]{1,0:T(8,128)(2,1)S(1)}, u32[]{:S(2)}, u32[]{:S(2)}) collective-permute-start(bf16[128,1536]{1,0:T(8,128)(2,1)S(1)} %get-tuple-element.16), channel_id=1, source_target_pairs={{0,6},{2,0},{4,2},{6,4},{1,7},{3,1},{5,3},{7,5},{8,14},{10,8},{12,... | collective-permute-start | bytes 1179656 | tf_op jit(solution)/shard_map/ppermute | solution.py:343

commit v10 on v4

--- a/solution.py
+++ b/solution.py
@@ -65,10 +65,9 @@
     heads, _, steps = decay_ref.shape
     width = x_ref.shape[1]
     blocks = [slice(k * LANES, (k + 1) * LANES) for k in range(steps // LANES)]
-    first, *others, last = fetch(
-        [(decay_hbm, decay_ref)]
-        + [(x_hbm.at[rows, :], x_ref.at[rows, :]) for rows in blocks]
-        + [(b_hbm, b_ref)],
+    first, second, *others = fetch(
+        [(decay_hbm, decay_ref), (b_hbm, b_ref)]
+        + [(x_hbm.at[rows, :], x_ref.at[rows, :]) for rows in blocks],
         sems,
     )
     matrix = head_spread(heads, width, width // heads)
@@ -79,12 +78,13 @@
         values = decay_ref[:, 0, blocks[k]]
         weights[k] = jnp.exp(running(values, lambda s, t: s > t) + later)
         later = later + jnp.sum(values, axis=1, keepdims=True)
+    second.wait()
+    across = b_ref[...].T
     for rows, weight, copy in zip(blocks, weights, others):
         weight = spread(weight, matrix)
         copy.wait()
         wx_ref[rows, :] = (x_ref[rows, :].astype(F32) * weight).astype(BF16)
-    last.wait()
-    state_ref[...] = lax.dot_general(b_ref[...], wx_ref[...], FIRST, preferred_element_type=F32)
+    state_ref[...] = mm(across, wx_ref[...])
     parcels, depth, _ = out_ref.shape
     unit = head_spread(heads, LANES, 1)
     tail = [
@@ -97,17 +97,16 @@
         out_ref[k, :, width:] = tail
 
 
-def prefix_kernel(heads, in_ref, out_ref, log_ref):
+def prefix_kernel(heads, in_ref, out_ref, factor_ref):
     parcels, depth, width = out_ref.shape
     matrix = head_spread(LANES, width, width // heads)
-    logs = in_ref[:, :, width:].reshape(parcels * depth, LANES)
-    log_ref[...] = mm(logs, matrix)
+    pairs = head_spread(parcels, parcels * depth, depth)
+    logs = mm(pairs, in_ref[:, :, width:].reshape(parcels * depth, LANES))
+    factor_ref[...] = sum(mm(part, matrix) for part in split2(jnp.exp(logs)))
     carried = jnp.zeros((depth, width), F32)
     for k in range(parcels):
         out_ref[k] = carried.astype(BF16)
-        both = log_ref[k * depth : (k + 1) * depth, :]
-        factor = jnp.exp(both[0:1, :] + both[1:2, :])
-        carried = factor * carried + in_ref[k, :, :width].astype(F32)
+        carried = factor_ref[k : k + 1, :] * carried + in_ref[k, :, :width].astype(F32)
 
 
 def local_kernel(
@@ -334,7 +333,7 @@
     prior = call(
         functools.partial(prefix_kernel, heads),
         spec((times, depth, width), BF16),
-        [pltpu.VMEM((times * depth, width), F32)],
+        [pltpu.VMEM((times, width), F32)],
         2 * state_dim * width * LANES,
         4 * state_dim * width,
         16,

time: 112 us -> 112 us (level)
  no operation moved by 1% of the time
where the time goes in v10:
time: 112 us; the launch traced here: 111 us
  blocking collectives  55.4 us (49%)
  starting transfers between devices  23.7 us (21%)
  Pallas kernels  14.5 us (13%)
  waiting for transfers between devices  13.9 us (12%)
  local copies, waits for them, and re-layouts  3.75 us (3%)
    all_to_all x1, blocking collectives, shards(): lax.all_to_all(outgoing, ('tm', 'farm'), split_axis=0, concat_axis=0, til...  33.8 us
    all_to_all x1, blocking collectives, shards(): lax.all_to_all(parts, 'head', split_axis=0, concat_axis=0, tiled=True)  21.5 us
    all_to_all x1, starting transfers between devices, shards(): lax.all_to_all(parcel, 'tm', split_axis=0, concat_axis=0, tiled=True)  17.1 us
    pallas_call x6, Pallas kernels, call(): pl.pallas_call(kernel, out_shape=outs, in_specs=[hbm if k in far else vme...  14.5 us
    all_to_all x1, waiting for transfers between devices, shards(): prior = lax.all_to_all(prior, 'tm', split_axis=0, concat_axis=0, tiled=True)  8.34 us
    all_to_all x1, starting transfers between devices, shards(): prior = lax.all_to_all(prior, 'tm', split_axis=0, concat_axis=0, tiled=True)  6.59 us
    all_to_all x1, waiting for transfers between devices, shards(): lax.all_to_all(parcel, 'tm', split_axis=0, concat_axis=0, tiled=True)  5.55 us
    unnamed x9, local copies, waits for them, and re-layouts  3.74 us
  transfers between devices with their start and end apart: 2, of which 2 were waited for; matrix products, arithmetic and copies ran while one was open for 0% of the time, Pallas kernels for 6%

profile of v10, /device:TPU:1, one launch (start us, length us, event | category | flops | bytes accessed | tf_op | source)
XLA Modules:
  0.0 111.4 jit_solution(10353817766705058565)
XLA Ops:
  0.0 0.0 copy-start.3
  0.0 0.0 copy-start.2
  0.0 3.4 %shard_map.82 = bf16[64,2,896]{2,1,0:T(2,128)(2,1)} custom-call(bf16[512,768]{1,0:T(8,128)(2,1)} %bitcast.8, bf16[512,128]{1,0:T(8,128)(2,1)} %bitcast.11, f32[12,1,512]{2,1,0:T(1,128)} %bitcast.14), custom_call_target="tpu_custom_call" | custom-call | flops 100663296 | bytes 786432 | tf_op jit(solution)/shard_map/pallas_call | solution.py:246
  3.4 17.1 %all-to-all-start = ((bf16[64,2,896]{2,1,0:T(2,128)(2,1)}), bf16[64,2,896]{2,1,0:T(2,128)(2,1)S(1)}, u32[]{:S(2)}, u32[]{:S(2)}) async-start(bf16[64,2,896]{2,1,0:T(2,128)(2,1)} %shard_map.82), calls=%async_computation | async-start | bytes 458752 | tf_op jit(solution)/shard_map/all_to_all | solution.py:292
  20.5 6.5 %shard_map.83.local_hbm = bf16[544,896]{1,0:T(8,128)(2,1)} custom-call(bf16[512,768]{1,0:T(8,128)(2,1)} %bitcast.9, bf16[512,128]{1,0:T(8,128)(2,1)} %bitcast.12, bf16[512,128]{1,0:T(8,128)(2,1)} %bitcast.13, f32[12,1,512]{2,1,0:T(1,128)} %bitcast.15, f32[1,12]{1,0:T(1,128)} %bitcast.16), custom_call_target="tpu_custom_call" | custom-call | flops 301989888 | bytes 3145728 | tf_op jit(solution)/shard_map/pallas_call | solution.py:246
  27.1 5.6 %all-to-all-done.in_ref = bf16[64,2,896]{2,1,0:T(2,128)(2,1)S(1)} async-done(((bf16[64,2,896]{2,1,0:T(2,128)(2,1)}), bf16[64,2,896]{2,1,0:T(2,128)(2,1)S(1)}, u32[]{:S(2)}, u32[]{:S(2)}) %all-to-all-start) | async-done | bytes 229408 | tf_op jit(solution)/shard_map/all_to_all | solution.py:292
  32.6 1.3 %shard_map.85 = bf16[64,2,768]{2,1,0:T(2,128)(2,1)} custom-call(bf16[64,2,896]{2,1,0:T(2,128)(2,1)S(1)} %all-to-all-done.in_ref), custom_call_target="tpu_custom_call" | custom-call | flops 25165824 | bytes 393216 | tf_op jit(solution)/shard_map/pallas_call | solution.py:246
  33.9 6.6 %all-to-all-start.1 = ((bf16[64,2,768]{2,1,0:T(2,128)(2,1)}), bf16[64,2,768]{2,1,0:T(2,128)(2,1)S(1)}, u32[]{:S(2)}, u32[]{:S(2)}) async-start(bf16[64,2,768]{2,1,0:T(2,128)(2,1)} %shard_map.85), calls=%async_computation.1 | async-start | bytes 393216 | tf_op jit(solution)/shard_map/all_to_all | solution.py:342
  40.5 0.0 copy-done.3
  40.5 0.0 copy-done.2
  40.6 0.0 copy-start
  40.6 1.2 %copy-done = bf16[544,896]{1,0:T(8,128)(2,1)S(1)} copy-done((bf16[544,896]{1,0:T(8,128)(2,1)S(1)}, bf16[544,896]{1,0:T(8,128)(2,1)}, u32[]{:S(2)}) %copy-start) | copy-done | bytes 974872
  41.8 0.0 copy-start.1
  41.8 1.7 %copy-done.1 = bf16[768,1536]{1,0:T(8,128)(2,1)S(1)} copy-done((bf16[768,1536]{1,0:T(8,128)(2,1)S(1)}, bf16[768,1536]{1,0:T(8,128)(2,1)}, u32[]{:S(2)}) %copy-start.1) | copy-done | bytes 2359320
  43.4 0.6 shard_map.84
  44.1 8.3 %all-to-all-done.1.prior_ref = bf16[64,2,768]{2,1,0:T(2,128)(2,1)S(1)} async-done(((bf16[64,2,768]{2,1,0:T(2,128)(2,1)}), bf16[64,2,768]{2,1,0:T(2,128)(2,1)S(1)}, u32[]{:S(2)}, u32[]{:S(2)}) %all-to-all-start.1) | async-done | bytes 196640 | tf_op jit(solution)/shard_map/all_to_all | solution.py:342
  52.4 2.0 %shard_map.86 = bf16[4,128,1536]{2,1,0:T(8,128)(2,1)S(1)} custom-call(bf16[544,896]{1,0:T(8,128)(2,1)S(1)} %get-tuple-element.16.local_ref, bf16[64,2,768]{2,1,0:T(2,128)(2,1)S(1)} %all-to-all-done.1.prior_ref, bf16[768,1536]{1,0:T(8,128)(2,1)S(1)} %get-tuple-element.18.w_ref), custom_call_target="tpu_custom_call" | custom-call | flops 1308622848 | bytes 4718592 | tf_op jit(solution)/shard_map/pallas_call | solution.py:246
  54.4 21.5 %all_to_all.20.parts_ref = bf16[4,128,1536]{2,1,0:T(8,128)(2,1)S(1)} all-to-all(bf16[4,128,1536]{2,1,0:T(8,128)(2,1)S(1)} %shard_map.86), channel_id=1, replica_groups=mesh['tm'=64,'head'=4,'farm'=2] {'head'}, dimensions={0} | all-to-all | bytes 3145728 | tf_op jit(solution)/shard_map/all_to_all | solution.py:354
  76.0 0.7 shard_map.87
  76.6 33.8 %all_to_all.21 = bf16[128,2,1536]{2,1,0:T(2,128)(2,1)S(1)} all-to-all(bf16[128,2,1536]{2,1,0:T(2,128)(2,1)S(1)} %shard_map.87), channel_id=1, replica_groups=mesh['tm'=64,'head'=4,'farm'=2] {'tm','farm'}, dimensions={0} | all-to-all | bytes 1572864 | tf_op jit(solution)/shard_map/all_to_all | solution.py:366
  110.5 0.9 copy.10
  (1 shorter events, 0.0 us)
Async XLA Ops:
  0.0 40.5 %copy-start.3 = (f32[1536]{0:T(1024)S(1)}, f32[1536]{0:T(1024)}, u32[]{:S(2)}) copy-start(f32[1536]{0:T(1024)} %param.14) | copy-start | bytes 18436
  0.0 40.5 %copy-start.2 = (s32[1,128,1]{1,2,0:T(1,128)S(1)}, s32[1,128,1]{1,2,0:T(1,128)}, u32[]{:S(2)}) copy-start(s32[1,128,1]{1,2,0:T(1,128)} %param.15) | copy-start | bytes 1540
  3.4 29.2 %all-to-all-start = ((bf16[64,2,896]{2,1,0:T(2,128)(2,1)}), bf16[64,2,896]{2,1,0:T(2,128)(2,1)S(1)}, u32[]{:S(2)}, u32[]{:S(2)}) async-start(bf16[64,2,896]{2,1,0:T(2,128)(2,1)} %shard_map.82), calls=%async_computation | async-start | bytes 458752 | tf_op jit(solution)/shard_map/all_to_all | solution.py:292
  33.9 18.5 %all-to-all-start.1 = ((bf16[64,2,768]{2,1,0:T(2,128)(2,1)}), bf16[64,2,768]{2,1,0:T(2,128)(2,1)S(1)}, u32[]{:S(2)}, u32[]{:S(2)}) async-start(bf16[64,2,768]{2,1,0:T(2,128)(2,1)} %shard_map.85), calls=%async_computation.1 | async-start | bytes 393216 | tf_op jit(solution)/shard_map/all_to_all | solution.py:342
  40.6 1.2 %copy-start = (bf16[544,896]{1,0:T(8,128)(2,1)S(1)}, bf16[544,896]{1,0:T(8,128)(2,1)}, u32[]{:S(2)}) copy-start(bf16[544,896]{1,0:T(8,128)(2,1)} %shard_map.83.local_hbm) | copy-start | bytes 2924548
  41.8 1.7 %copy-start.1 = (bf16[768,1536]{1,0:T(8,128)(2,1)S(1)}, bf16[768,1536]{1,0:T(8,128)(2,1)}, u32[]{:S(2)}) copy-start(bf16[768,1536]{1,0:T(8,128)(2,1)} %w_hbm) | copy-start | bytes 7077892
